TPU v7x, 512 devices: a whole 4x8x8 slice. The times are simulated.
512 devices in a mesh: ctx: 16 (over x, z_hi), dp: 8 (over y), tp: 4 (over z_lo, core).
Axes of the slice: x: 4, y: 8, z: 8 (z_hi: 4, z_lo: 2; z = z_hi * 2 + z_lo), core: 2. Of those that a mesh axis runs over, the one named last changes fastest.
Arguments:
- token_ids: int32 [4, 16], replicated, may hold values from 0 to 50279
- decode_prompt: int32 [16], replicated, may hold values from 0 to 15, as said below
- embedding: bfloat16 [50280, 4096], P('dp', ('ctx', 'tp')), may hold values from -6 to 6
- norm_gain: float32 [4096], replicated, may hold values from 0.1 to 1.9
- w_zx: bfloat16 [2, 128, 64, 4096], P(None, ('tp', 'ctx')), may hold values from -0.09375 to 0.09375
- w_bcdt: bfloat16 [4096, 384], P(None, ('ctx', 'tp')), may hold values from -0.09375 to 0.09375
- conv_x_weight: float32 [4, 128, 64], P(None, ('tp', 'ctx')), may hold values from -3 to 3
- conv_x_bias: float32 [128, 64], P(('tp', 'ctx')), may hold values from -3 to 3
- conv_bc_weight: float32 [4, 256], replicated, may hold values from -3 to 3
- conv_bc_bias: float32 [256], replicated, may hold values from -3 to 3
- dt_bias: float32 [128], P(('tp', 'ctx')), may hold values from -4 to -1
- a_log: float32 [128], P(('tp', 'ctx')), may hold values from 0 to 2.7
- d_skip: float32 [128], P(('tp', 'ctx')), may hold values from 0.5 to 1.5
- gate_norm_gain: float32 [128, 64], P(('tp', 'ctx')), may hold values from 0.1 to 1.9
- w_out: bfloat16 [128, 64, 4096], P(('tp', 'ctx')), may hold values from -0.0625 to 0.0625
- state_parts: bfloat16 [16, 16, 128, 64, 128], P('ctx', 'dp', 'tp'), may hold values from -6 to 6
- seg_rate: float32 [16, 16, 128], P('ctx', 'dp', 'tp'), may hold values from 0 to 2
- x_tail: bfloat16 [16, 3, 128, 64], P('dp', None, ('tp', 'ctx')), may hold values from -6 to 6
- bc_tail: bfloat16 [16, 3, 256], P('dp'), may hold values from -6 to 6
Outputs:
- mixer_out: bfloat16 [4, 16, 4096], P(None, 'dp', ('ctx', 'tp'))
- final_state: float32 [16, 128, 64, 128], P('dp', ('tp', 'ctx'))
Inputs may be any that keep to these rules, and one draw needn't show every extreme that they name: decode_prompt is a permutation of the prompts; slot s is decoded by dp group s // 2, and prompt q is held by dp group q // 2; the 2 prompts held by one dp group are decoded by 2 different dp groups.
All inputs are finite; a program needn't handle non-finite values.
Results may differ from a plain program's by a relative error of at most 0.02.
Values may be sent and summed in bfloat16 or wider, within the bound.
No kernel may reach another device: no remote copies, remote signals or barrier semaphores. Data moves between devices by JAX's collectives and lax.ppermute only.
A program may use at most 64 MiB of HBM per device.

v0:
```python
import jax
import jax.numpy as jnp
from jax import lax
from jax.sharding import PartitionSpec as P

HEADS = 128
HEAD_DIM = 64


epsilon = 1e-05


def from_everyone(shard, axis):
    count = lax.axis_size(axis)
    return lax.all_to_all(
        jnp.broadcast_to(shard[None], (count, *shard.shape)), axis, 0, 0, tiled=True
    )


def folded_in_pairs(pieces, combine):
    while len(jax.tree.leaves(pieces)[0]) > 1:
        pieces = jax.vmap(combine)(*(pieces[side::2] for side in (0, 1)))
    return pieces[0]


def prefix(shard, axis, combine, identity):
    count, here = (lax.axis_size(axis), lax.axis_index(axis))
    passed = jnp.arange(count) > here

    def kept(part, zero, own):
        part = jnp.where(
            passed.reshape(-1, *(1 for _ in own.shape)), part, jnp.asarray(zero, own.dtype)
        )
        return part[::-1]

    pieces = from_everyone(shard, axis)
    return folded_in_pairs(kept(pieces, identity, shard), combine)


def split_up(shard, dim, count):
    before, after = (shard.shape[:dim], shard.shape[dim + 1 :])
    return jnp.moveaxis(shard.reshape(*before, count, -1, *after), dim, 0)


def sum_at_owner(shard, axis, dim):
    count = lax.axis_size(axis)
    pieces = lax.all_to_all(split_up(shard, dim, count), axis, 0, 0, tiled=True)
    return jnp.sum(pieces.astype(jnp.float32), axis=0)


def rows_first(arrays, axis, dims):
    turned = [jnp.moveaxis(a, dim, 0) for a, dim in zip(arrays, dims)]
    widths = [t[0].size for t in turned]
    both = jnp.concatenate([t.reshape(-1, w) for t, w in zip(turned, widths)], axis=1)
    filled = lax.all_gather(both, axis, axis=0, tiled=True)
    pieces = jnp.split(filled, [sum(widths[:k]) for k in range(1, len(widths))], axis=1)
    return tuple(
        (
            jnp.moveaxis(b.reshape(-1, *t.shape[1:]), 0, dim)
            for b, t, dim in zip(pieces, turned, dims)
        )
    )


def laid_out(pieces, dim):
    dims = list(pieces.shape[1:])
    dims[dim] *= pieces.shape[0]
    return jnp.moveaxis(pieces, 0, dim).reshape(dims)


def collect(shard, axis, dim):
    pieces = from_everyone(shard, axis)
    return laid_out(pieces, dim)


def over_copies(shard, axis):
    everything = from_everyone(shard, axis)
    return jnp.sum(everything, axis=0)


def sum_at_owner_2(shard, axis, dim):
    pieces = split_up(shard, dim, lax.axis_size(axis))
    arrived = lax.all_to_all(pieces, axis, split_axis=0, concat_axis=0, tiled=True)
    return arrived.sum(axis=0)


def rms_scale(values, gain):
    return values * lax.rsqrt(jnp.mean(values * values, axis=-1, keepdims=True) + epsilon) * gain


def select_rows(picker, values):
    return jnp.tensordot(picker, values, axes=1, precision=lax.Precision.HIGHEST)


def add_rates(earlier, later_one):
    return earlier + later_one


def per_device(
    token_ids,
    decode_prompt,
    embedding,
    norm_gain,
    w_zx,
    w_bcdt,
    conv_x_weight,
    conv_x_bias,
    conv_bc_weight,
    conv_bc_bias,
    dt_bias,
    a_log,
    d_skip,
    gate_norm_gain,
    w_out,
    state_parts,
    seg_rate,
    x_tail,
    bc_tail,
):
    group = lax.axis_index("dp")
    local_count = state_parts.shape[1]
    slot_count = decode_prompt.shape[0]
    head_count = w_zx.shape[1]
    state_width = conv_bc_bias.shape[0] // 2
    after_rates = prefix(seg_rate, "ctx", add_rates, jnp.zeros_like(seg_rate))
    seg_weight = jnp.exp(-after_rates[0])
    scaled = seg_weight[:, :, None, None] * state_parts[0].astype(jnp.float32)
    combined = sum_at_owner(scaled.astype(jnp.bfloat16), "ctx", 1)
    tails_x = x_tail.astype(jnp.float32)
    tails_bc = bc_tail.astype(jnp.float32)
    own_slots = lax.dynamic_slice_in_dim(decode_prompt, group * local_count, local_count)
    prompt_ids = jnp.arange(slot_count, dtype=jnp.int32)
    every_state, every_x, every_bc = tuple(
        (
            part.astype(jnp.float32)
            for part in rows_first(
                (
                    combined.astype(jnp.bfloat16),
                    tails_x.astype(jnp.bfloat16),
                    tails_bc.astype(jnp.bfloat16),
                ),
                "dp",
                (0, 0, 0),
            )
        )
    )
    picker = (own_slots[:, None] == prompt_ids[None, :]).astype(jnp.float32)
    ssm_state = select_rows(picker, every_state)
    x_window = select_rows(picker, every_x)
    bc_window = select_rows(picker, every_bc)
    vocab_rows = embedding.shape[0]
    holder = (decode_prompt[:, None] == prompt_ids[None, :]).astype(jnp.int32)
    slot_tokens = jnp.sum(token_ids[:, None, :] * holder[None], axis=2)
    offset_tokens = slot_tokens - group * vocab_rows
    inside = (offset_tokens >= 0) & (offset_tokens < vocab_rows)
    looked = jnp.take(embedding, jnp.clip(offset_tokens, 0, vocab_rows - 1), axis=0)
    partial_rows = jnp.where(inside[..., None], looked.astype(jnp.float32), 0.0)
    own_rows = sum_at_owner(partial_rows.astype(jnp.bfloat16), "dp", 1)
    embedded = collect(own_rows.astype(jnp.bfloat16), ("ctx", "tp"), 2)
    steps_count = embedded.shape[0]
    flat_rows = embedded.reshape(-1, embedded.shape[2]).astype(jnp.float32)
    normed = rms_scale(flat_rows, norm_gain).astype(jnp.bfloat16)
    projected = jnp.einsum("rd,khed->krhe", normed, w_zx, preferred_element_type=jnp.float32)
    projected = projected.reshape(
        2, steps_count, local_count, projected.shape[2], projected.shape[3]
    )
    columns = collect(jnp.dot(normed, w_bcdt, preferred_element_type=jnp.float32), ("ctx", "tp"), 1)
    columns = columns.reshape(steps_count, local_count, -1)
    head_block = lax.axis_index("tp") * lax.axis_size("ctx") + lax.axis_index("ctx")
    head_start = 2 * state_width + head_block * head_count
    dt_raw = lax.dynamic_slice_in_dim(columns, head_start, head_count, 2)
    decay_rate = -jnp.exp(a_log)
    gated_steps = []
    for moment in range(steps_count):
        x_window = jnp.concatenate([x_window, projected[1, moment][:, None]], axis=1)
        bc_window = jnp.concatenate(
            [bc_window, columns[moment, :, None, : 2 * state_width]], axis=1
        )
        x_conv = jax.nn.silu(jnp.einsum("pkhe,khe->phe", x_window, conv_x_weight) + conv_x_bias)
        bc_conv = jax.nn.silu(jnp.einsum("pkn,kn->pn", bc_window, conv_bc_weight) + conv_bc_bias)
        step_size = jax.nn.softplus(dt_raw[moment] + dt_bias)
        retain = jnp.exp(step_size * decay_rate)
        ssm_state = (
            retain[:, :, None, None] * ssm_state
            + (step_size[:, :, None] * x_conv)[:, :, :, None] * bc_conv[:, None, None, :state_width]
        )
        output = (
            jnp.einsum("phen,pn->phe", ssm_state, bc_conv[:, state_width:])
            + d_skip[None, :, None] * x_conv
        )
        gated_steps.append(output * jax.nn.silu(projected[0, moment]))
        x_window = x_window[:, 1:]
        bc_window = bc_window[:, 1:]
    gated_all = jnp.stack(gated_steps)
    local_squares = jnp.sum(gated_all * gated_all, axis=(2, 3))
    total_squares = over_copies(local_squares, ("ctx", "tp"))
    inverse = lax.rsqrt(total_squares / (HEADS * HEAD_DIM) + epsilon)
    normed_out = (gated_all * inverse[:, :, None, None] * gate_norm_gain).astype(jnp.bfloat16)
    partial_out = jnp.einsum("tphe,hed->tpd", normed_out, w_out, preferred_element_type=jnp.float32)
    mixed = sum_at_owner_2(partial_out, ("ctx", "tp"), 2)
    return (mixed.astype(jnp.bfloat16), ssm_state)


def solution(mesh):
    return jax.shard_map(
        per_device,
        mesh=mesh,
        in_specs=(
            P(),
            P(),
            P("dp", ("ctx", "tp")),
            P(),
            P(None, ("tp", "ctx"), None, None),
            P(None, ("ctx", "tp")),
            P(None, ("tp", "ctx"), None),
            P(("tp", "ctx"), None),
            P(),
            P(),
            P(("tp", "ctx")),
            P(("tp", "ctx")),
            P(("tp", "ctx")),
            P(("tp", "ctx"), None),
            P(("tp", "ctx"), None, None),
            P("ctx", "dp", "tp", None, None),
            P("ctx", "dp", "tp"),
            P("dp", None, ("tp", "ctx"), None),
            P("dp", None, None),
        ),
        out_specs=(P(None, "dp", ("ctx", "tp")), P("dp", ("tp", "ctx"), None, None)),
        check_vma=False,
    )
```

profile of v0, /device:TPU:1, one launch (start us, length us, event | category | flops | bytes accessed | tf_op | source)
XLA Modules:
  0.0 178.2 jit_solution(10364687955391233364)
XLA Ops:
  0.6 1.4 broadcast_in_dim.52
  2.1 13.4 %all-to-all-start.3 = ((f32[16,1,2,32]{3,2,1,0:T(2,128)}), f32[16,1,2,32]{3,2,1,0:T(2,128)S(1)}, u32[]{:S(2)}, u32[]{:S(2)}) async-start(f32[16,1,2,32]{3,2,1,0:T(2,128)} %broadcast_in_dim.52), calls=%async_computation.3 | async-start | bytes 32768 | tf_op jit(solution)/shard_map/all_to_all | solution.py:15
  16.2 0.8 multiply_reduce_fusion
  17.5 2.6 %copy.222 = bf16[6285,64]{1,0:T(8,128)(2,1)} copy(bf16[6285,64]{0,1:T(8,128)(2,1)} %param.21) | data formatting | bytes 1608960 | tf_op args[2]
  20.1 2.2 %gather_fusion = bf16[64,64]{1,0:T(8,128)(2,1)S(1)} fusion(bf16[6285,64]{1,0:T(8,128)(2,1)} %copy.222, s32[1024]{0:T(1024)S(1)} %pad_clamp_fusion), kind=kCustom, calls=%fused_computation | custom fusion | bytes 16640 | tf_op jit(solution)/shard_map/jit(_take)/gather | solution.py:156
  23.2 1.1 all-to-all-done.3
  24.3 6.8 %all-to-all-start = ((bf16[8,2,256]{2,1,0:T(2,128)(2,1)}), bf16[8,2,256]{2,1,0:T(2,128)(2,1)S(1)}, u32[]{:S(2)}, u32[]{:S(2)}) async-start(bf16[8,2,256]{2,1,0:T(2,128)(2,1)} %reshape.439), calls=%async_computation | async-start | bytes 16384 | tf_op jit(solution)/shard_map/all_to_all | solution.py:47
  31.3 6.4 %all-to-all-done = bf16[8,2,256]{2,1,0:T(2,128)(2,1)S(1)} async-done(((bf16[8,2,256]{2,1,0:T(2,128)(2,1)}), bf16[8,2,256]{2,1,0:T(2,128)(2,1)S(1)}, u32[]{:S(2)}, u32[]{:S(2)}) %all-to-all-start) | async-done | bytes 8224 | tf_op jit(solution)/shard_map/all_to_all | solution.py:47
  38.0 0.8 reshape.441
  38.7 11.3 %all-to-all-start.1 = ((bf16[64,2,256]{2,1,0:T(2,128)(2,1)}), bf16[64,2,256]{2,1,0:T(2,128)(2,1)S(1)}, u32[]{:S(2)}, u32[]{:S(2)}) async-start(bf16[64,2,256]{2,1,0:T(2,128)(2,1)} %reshape.441), calls=%async_computation.1 | async-start | bytes 131072 | tf_op jit(solution)/shard_map/all_to_all | solution.py:15
  50.2 9.7 %all-to-all-done.1 = bf16[64,2,256]{2,1,0:T(2,128)(2,1)S(1)} async-done(((bf16[64,2,256]{2,1,0:T(2,128)(2,1)}), bf16[64,2,256]{2,1,0:T(2,128)(2,1)S(1)}, u32[]{:S(2)}, u32[]{:S(2)}) %all-to-all-start.1) | async-done | bytes 65568 | tf_op jit(solution)/shard_map/all_to_all | solution.py:15
  61.6 4.4 %all-to-all-start.2 = ((f32[64,8,6]{2,1,0:T(8,128)}), f32[64,8,6]{2,1,0:T(8,128)S(1)}, u32[]{:S(2)}, u32[]{:S(2)}) async-start(f32[64,8,6]{2,1,0:T(8,128)} %broadcast_in_dim.49), calls=%async_computation.2 | async-start | bytes 524288 | tf_op jit(solution)/shard_map/all_to_all | solution.py:15
  66.1 1.5 fusion.2
  67.6 1.1 copy.227
  68.7 9.4 %all-to-all-done.2 = f32[64,8,6]{2,1,0:T(8,128)S(1)} async-done(((f32[64,8,6]{2,1,0:T(8,128)}), f32[64,8,6]{2,1,0:T(8,128)S(1)}, u32[]{:S(2)}, u32[]{:S(2)}) %all-to-all-start.2) | async-done | bytes 12320 | tf_op jit(solution)/shard_map/all_to_all | solution.py:15
  78.1 4.8 %all-to-all-start.4 = ((bf16[16,2,2,64,128]{4,3,2,1,0:T(8,128)(2,1)}), bf16[16,2,2,64,128]{4,3,2,1,0:T(8,128)(2,1)S(1)}, u32[]{:S(2)}, u32[]{:S(2)}) async-start(bf16[16,2,2,64,128]{4,3,2,1,0:T(8,128)(2,1)} %copy.227), calls=%async_computation.4 | async-start | bytes 2097152 | tf_op jit(solution)/shard_map/all_to_all | solution.py:47
  84.7 1.6 fusion.12
  87.7 1.1 reshape_reshape.4
  93.2 13.3 %all-to-all-done.4 = bf16[16,2,2,64,128]{4,3,2,1,0:T(8,128)(2,1)S(1)} async-done(((bf16[16,2,2,64,128]{4,3,2,1,0:T(8,128)(2,1)}), bf16[16,2,2,64,128]{4,3,2,1,0:T(8,128)(2,1)S(1)}, u32[]{:S(2)}, u32[]{:S(2)}) %all-to-all-start.4) | async-done | bytes 1048608 | tf_op jit(solution)/shard_map/all_to_all | solution.py:47
  106.9 20.3 %all-gather = bf16[8,2,17536]{2,1,0:T(2,128)(2,1)S(1)} all-gather(bf16[1,2,17536]{2,1,0:T(2,128)(2,1)S(1)} %maximum_bitcast_fusion), channel_id=1, replica_groups=mesh['ctx'=16,'dp'=8,'tp'=4] {'dp'}, dimensions={0}, use_global_device_ids=true | all-gather | bytes 631296 | tf_op jit(solution)/shard_map/all_gather | solution.py:55
  130.8 1.7 multiply_add_fusion
  133.5 26.3 %all_to_all.35 = f32[64,4,2]{1,2,0:T(2,128)S(1)} all-to-all(f32[64,4,2]{1,2,0:T(2,128)S(1)} %broadcast_in_dim.54), channel_id=1, replica_groups=mesh['ctx'=16,'dp'=8,'tp'=4] {'ctx','tp'}, dimensions={0} | all-to-all | bytes 4096 | tf_op jit(solution)/shard_map/all_to_all | solution.py:15
  161.7 14.2 %all_to_all.36 = f32[64,1,512]{2,1,0:T(1,128)S(1)} all-to-all(f32[64,1,512]{2,1,0:T(1,128)S(1)} %reshape.443), channel_id=1, replica_groups=mesh['ctx'=16,'dp'=8,'tp'=4] {'ctx','tp'}, dimensions={0} | all-to-all | bytes 262144 | tf_op jit(solution)/shard_map/all_to_all | solution.py:83
  176.4 0.9 reduce.20
  (135 shorter events, 19.6 us)
Async XLA Ops:
  0.6 84.1 %copy-start = (bf16[2,2,64,4096]{3,2,1,0:T(8,128)(2,1)S(1)}, bf16[2,2,64,4096]{3,2,1,0:T(8,128)(2,1)}, u32[]{:S(2)}) copy-start(bf16[2,2,64,4096]{3,2,1,0:T(8,128)(2,1)} %param.23) | copy-start | bytes 6291460
  2.1 22.3 %all-to-all-start.3 = ((f32[16,1,2,32]{3,2,1,0:T(2,128)}), f32[16,1,2,32]{3,2,1,0:T(2,128)S(1)}, u32[]{:S(2)}, u32[]{:S(2)}) async-start(f32[16,1,2,32]{3,2,1,0:T(2,128)} %broadcast_in_dim.52), calls=%async_computation.3 | async-start | bytes 32768 | tf_op jit(solution)/shard_map/all_to_all | solution.py:15
  17.5 43.2 %copy-start.3 = (f32[4096]{0:T(1024)S(1)}, f32[4096]{0:T(1024)}, u32[]{:S(2)}) copy-start(f32[4096]{0:T(1024)} %param.22) | copy-start | bytes 49156
  17.5 43.2 %copy-start.4 = (bf16[4096,6]{0,1:T(8,128)(2,1)S(1)}, bf16[4096,6]{0,1:T(8,128)(2,1)}, u32[]{:S(2)}) copy-start(bf16[4096,6]{0,1:T(8,128)(2,1)} %param.24) | copy-start | bytes 147460
  24.3 13.4 %all-to-all-start = ((bf16[8,2,256]{2,1,0:T(2,128)(2,1)}), bf16[8,2,256]{2,1,0:T(2,128)(2,1)S(1)}, u32[]{:S(2)}, u32[]{:S(2)}) async-start(bf16[8,2,256]{2,1,0:T(2,128)(2,1)} %reshape.439), calls=%async_computation | async-start | bytes 16384 | tf_op jit(solution)/shard_map/all_to_all | solution.py:47
  38.7 21.1 %all-to-all-start.1 = ((bf16[64,2,256]{2,1,0:T(2,128)(2,1)}), bf16[64,2,256]{2,1,0:T(2,128)(2,1)S(1)}, u32[]{:S(2)}, u32[]{:S(2)}) async-start(bf16[64,2,256]{2,1,0:T(2,128)(2,1)} %reshape.441), calls=%async_computation.1 | async-start | bytes 131072 | tf_op jit(solution)/shard_map/all_to_all | solution.py:15
  60.7 8.1 %copy-start.11 = (f32[8]{0:T(128)}, f32[8]{0:T(128)S(1)}, u32[]{:S(2)}) copy-start(f32[8]{0:T(128)S(1)} %rsqrt.19) | copy-start | bytes 100
  61.6 16.5 %all-to-all-start.2 = ((f32[64,8,6]{2,1,0:T(8,128)}), f32[64,8,6]{2,1,0:T(8,128)S(1)}, u32[]{:S(2)}, u32[]{:S(2)}) async-start(f32[64,8,6]{2,1,0:T(8,128)} %broadcast_in_dim.49), calls=%async_computation.2 | async-start | bytes 524288 | tf_op jit(solution)/shard_map/all_to_all | solution.py:15
  67.6 15.4 %copy-start.13 = (bf16[2,3,2,64]{3,2,1,0:T(2,128)(2,1)S(1)}, bf16[2,3,2,64]{3,2,1,0:T(2,128)(2,1)}, u32[]{:S(2)}) copy-start(bf16[2,3,2,64]{3,2,1,0:T(2,128)(2,1)} %param.36) | copy-start | bytes 4612
  67.6 16.0 %copy-start.17 = (s32[16]{0:T(128)S(1)}, s32[16]{0:T(128)}, u32[]{:S(2)}) copy-start(s32[16]{0:T(128)} %param.20) | copy-start | bytes 196
  67.6 16.6 %copy-start.18 = (f32[2]{0:T(128)S(1)}, f32[2]{0:T(128)}, u32[]{:S(2)}) copy-start(f32[2]{0:T(128)} %param.30) | copy-start | bytes 28
  78.1 28.5 %all-to-all-start.4 = ((bf16[16,2,2,64,128]{4,3,2,1,0:T(8,128)(2,1)}), bf16[16,2,2,64,128]{4,3,2,1,0:T(8,128)(2,1)S(1)}, u32[]{:S(2)}, u32[]{:S(2)}) async-start(bf16[16,2,2,64,128]{4,3,2,1,0:T(8,128)(2,1)} %copy.227), calls=%async_computation.4 | async-start | bytes 2097152 | tf_op jit(solution)/shard_map/all_to_all | solution.py:47
  86.3 20.5 %copy-start.10 = (bf16[2,384]{1,0:T(2,128)(2,1)S(1)}, bf16[2,384]{1,0:T(2,128)(2,1)}, u32[]{:S(2)}) copy-start(bf16[2,384]{1,0:T(2,128)(2,1)} %reshape.389) | copy-start | bytes 4612
  86.3 20.5 %copy-start.14 = (bf16[2,3,256]{2,0,1:T(2,128)(2,1)S(1)}, bf16[2,3,256]{2,0,1:T(2,128)(2,1)}, u32[]{:S(2)}) copy-start(bf16[2,3,256]{2,0,1:T(2,128)(2,1)} %param.37) | copy-start | bytes 9220
  93.2 34.4 %copy-start.19 = (s32[2]{0:T(128)S(1)}, s32[2]{0:T(128)}, u32[]{:S(2)}) copy-start(s32[2]{0:T(128)} %dynamic_slice.7) | copy-start | bytes 28
  93.2 34.8 %copy-start.5 = (f32[2,1,2,64]{3,0,2,1:T(2,128)S(1)}, f32[2,1,2,64]{3,0,2,1:T(2,128)}, u32[]{:S(2)}) copy-start(f32[2,1,2,64]{3,0,2,1:T(2,128)} %get-tuple-element.51) | copy-start | bytes 3076
  93.2 34.8 %copy-start.12 = (f32[4,2,64]{2,1,0:T(2,128)S(1)}, f32[4,2,64]{2,1,0:T(2,128)}, u32[]{:S(2)}) copy-start(f32[4,2,64]{2,1,0:T(2,128)} %param.25) | copy-start | bytes 6148
  93.2 34.8 %copy-start.15 = (f32[2,64]{1,0:T(2,128)S(1)}, f32[2,64]{1,0:T(2,128)}, u32[]{:S(2)}) copy-start(f32[2,64]{1,0:T(2,128)} %param.26) | copy-start | bytes 1540
  130.8 2.4 %copy-start.6 = (f32[2,2,64]{2,0,1:T(2,128)S(1)}, f32[2,2,64]{2,0,1:T(2,128)}, u32[]{:S(2)}) copy-start(f32[2,2,64]{2,0,1:T(2,128)} %get-tuple-element.44) | copy-start | bytes 3076
  130.8 2.4 %copy-start.8 = (f32[2,2,64]{2,0,1:T(2,128)S(1)}, f32[2,2,64]{2,0,1:T(2,128)}, u32[]{:S(2)}) copy-start(f32[2,2,64]{2,0,1:T(2,128)} %get-tuple-element.78) | copy-start | bytes 3076
  130.8 2.4 %copy-start.9 = (f32[2,2,64]{2,0,1:T(2,128)S(1)}, f32[2,2,64]{2,0,1:T(2,128)}, u32[]{:S(2)}) copy-start(f32[2,2,64]{2,0,1:T(2,128)} %get-tuple-element.80) | copy-start | bytes 3076
  130.8 2.4 %copy-start.16 = (f32[2]{0:T(128)S(1)}, f32[2]{0:T(128)}, u32[]{:S(2)}) copy-start(f32[2]{0:T(128)} %param.31) | copy-start | bytes 28
  130.8 30.0 %copy-start.1 = (bf16[2,64,4096]{2,1,0:T(8,128)(2,1)S(1)}, bf16[2,64,4096]{2,1,0:T(8,128)(2,1)}, u32[]{:S(2)}) copy-start(bf16[2,64,4096]{2,1,0:T(8,128)(2,1)} %param.33) | copy-start | bytes 3145732
  132.5 45.1 %copy-start.2 = (f32[2,2,64,128]{3,2,1,0:T(8,128)}, f32[2,2,64,128]{3,2,1,0:T(8,128)S(1)}, u32[]{:S(2)}) copy-start(f32[2,2,64,128]{3,2,1,0:T(8,128)S(1)} %copy.256) | copy-start | bytes 393220
  (1 other events, 2.4 us)
where the time goes:
time: 179 us; the launch traced here: 178 us
  blocking collectives  60.8 us (34%)
  starting transfers between devices  40.8 us (23%)
  waiting for transfers between devices  40 us (22%)
  local copies, waits for them, and re-layouts  21.1 us (12%)
  other arithmetic  9.52 us (5%)
  matrix products  4.86 us (3%)
    all_to_all x3, starting transfers between devices, from_everyone(): lax.all_to_all(jnp.broadcast_to(shard[None], (count, *shard.shape)), axis...  29.2 us
    all_to_all x1, blocking collectives, from_everyone(): lax.all_to_all(jnp.broadcast_to(shard[None], (count, *shard.shape)), axis...  26.3 us
    all_gather x1, blocking collectives, rows_first(): filled = lax.all_gather(both, axis, axis=0, tiled=True)  20.3 us
    all_to_all x3, waiting for transfers between devices, from_everyone(): lax.all_to_all(jnp.broadcast_to(shard[None], (count, *shard.shape)), axis...  20.2 us
    all_to_all x2, waiting for transfers between devices, sum_at_owner(): pieces = lax.all_to_all(split_up(shard, dim, count), axis, 0, 0, tiled=True)  19.8 us
    all_to_all x1, blocking collectives, sum_at_owner_2(): lax.all_to_all(pieces, axis, split_axis=0, concat_axis=0, tiled=True)  14.2 us
    all_to_all x2, starting transfers between devices, sum_at_owner(): pieces = lax.all_to_all(split_up(shard, dim, count), axis, 0, 0, tiled=True)  11.6 us
    unnamed x53, local copies, waits for them, and re-layouts  5.79 us
  transfers between devices with their start and end apart: 5, of which 5 were waited for; matrix products, arithmetic and copies ran while one was open for 12% of the time, Pallas kernels for 0%

commit v1 on v0

v1 whole, which is shorter than its diff:
```python
import jax
import jax.numpy as jnp
from jax import lax
from jax.sharding import PartitionSpec as P

HEADS = 128
HEAD_DIM = 64
EPS = 1e-05
BOTH = ("ctx", "tp")
BF = jnp.bfloat16
F32 = jnp.float32


def exchange(pieces, axis):
    return lax.all_to_all(pieces, axis, 0, 0, tiled=True)


def in_three(values):
    first = values.astype(BF)
    rest = values - first.astype(F32)
    second = rest.astype(BF)
    third = (rest - second.astype(F32)).astype(BF)
    return first, second, third


def per_device(
    token_ids,
    decode_prompt,
    embedding,
    norm_gain,
    w_zx,
    w_bcdt,
    conv_x_weight,
    conv_x_bias,
    conv_bc_weight,
    conv_bc_bias,
    dt_bias,
    a_log,
    d_skip,
    gate_norm_gain,
    w_out,
    state_parts,
    seg_rate,
    x_tail,
    bc_tail,
):
    ctx, group, tp = (lax.axis_index(a) for a in ("ctx", "dp", "tp"))
    n_ctx, n_dp, n_tp = (lax.axis_size(a) for a in ("ctx", "dp", "tp"))
    slots = state_parts.shape[1]
    heads = w_zx.shape[1]
    state_width = state_parts.shape[-1]
    steps = token_ids.shape[0]
    vocab_rows, features = embedding.shape
    model = norm_gain.shape[0]
    rows = steps * slots
    channels = heads * HEAD_DIM
    block = features * n_tp

    states = state_parts[0].reshape(slots, n_ctx, heads, HEAD_DIM, state_width)
    states = jnp.swapaxes(states, 0, 1).reshape(n_ctx, -1, state_width)
    own_columns = w_bcdt.shape[1]
    w_pieces = w_bcdt.T.reshape(own_columns, n_ctx, block)
    w_pieces = jnp.swapaxes(w_pieces, 0, 1).reshape(n_ctx, -1, state_width)
    rates = jnp.swapaxes(seg_rate[0].reshape(slots, n_ctx, heads), 0, 1)
    rates = jnp.stack(in_three(rates), axis=1).reshape(n_ctx, -1, 1)
    rates = jnp.broadcast_to(rates, (*rates.shape[:2], state_width))
    state_rows, w_rows, rate_rows = states.shape[1], w_pieces.shape[1], rates.shape[1]
    sent = jnp.concatenate([states, w_pieces, rates], axis=1)
    filler = -sent.shape[1] % 16
    sent = jnp.pad(sent, ((0, 0), (0, filler), (0, 0)))
    got = exchange(sent, "ctx")

    prompts = decode_prompt.shape[0]
    chosen = (decode_prompt[:, None] == jnp.arange(prompts)[None, :]).astype(jnp.int32)
    tokens = jnp.sum(token_ids[:, None, :] * chosen[None], axis=2)
    tokens = jnp.swapaxes(tokens.reshape(steps, n_dp, slots), 0, 1).reshape(-1)
    hot = (tokens[:, None] - group * vocab_rows == jnp.arange(vocab_rows)[None, :]).astype(BF)
    found = jnp.dot(hot, embedding, preferred_element_type=F32).astype(BF)
    found = lax.psum(found, "dp")
    own = lax.dynamic_slice_in_dim(found, group * rows, rows)
    beside = lax.all_gather(own, "tp")

    near = jnp.swapaxes(beside, 0, 1).reshape(rows, block).astype(F32)
    near_gain = lax.dynamic_slice_in_dim(norm_gain, ctx * block, block)
    w_block = got[:, state_rows : state_rows + w_rows].reshape(-1, block)
    partial = lax.dot_general(
        (near * near_gain).astype(BF), w_block, (((1,), (1,)), ((), ())), preferred_element_type=F32
    ).astype(BF)
    piece = jnp.concatenate([own.reshape(-1, 128), partial.reshape(-1, 128)], axis=0)
    own_rows = own.size // 128
    everyone = exchange(jnp.broadcast_to(piece[None], (n_ctx * n_tp, *piece.shape)), BOTH)

    parts = got[:, state_rows + w_rows : state_rows + w_rows + rate_rows, 0].astype(F32)
    parts = parts.reshape(n_ctx, 3, slots, heads)
    rate = parts[:, 0] + parts[:, 1] + parts[:, 2]
    later = jnp.cumsum(rate[::-1], axis=0)[::-1] - rate
    weight = jnp.exp(-later)[..., None, None]
    scaled = weight * got[:, :state_rows].reshape(n_ctx, slots, heads, HEAD_DIM, state_width).astype(F32)
    combined = jnp.sum(scaled.astype(BF).astype(F32), axis=0).astype(BF)
    bundle = jnp.concatenate(
        [
            combined.reshape(slots, -1, 128),
            jnp.swapaxes(x_tail, 1, 1).reshape(slots, -1, 128),
            bc_tail.reshape(slots, -1, 128),
        ],
        axis=1,
    )
    bundle = jnp.pad(bundle, ((0, 0), (0, -bundle.shape[1] % 16), (0, 0)))
    wanted = decode_prompt.reshape(n_dp, slots) - group * slots
    second = jnp.any(wanted == 1, axis=1)
    routed = jnp.where(second[:, None, None], bundle[1][None], bundle[0][None])
    arrived = exchange(routed, "dp")

    taken = everyone[:, :own_rows].reshape(n_ctx * n_tp, rows, features)
    flat = jnp.swapaxes(taken, 0, 1).reshape(rows, model).astype(F32)
    inverse = lax.rsqrt(jnp.mean(flat * flat, axis=-1, keepdims=True) + EPS)
    normed = (flat * inverse * norm_gain).astype(BF)
    projected = jnp.einsum("rd,khed->krhe", normed, w_zx, preferred_element_type=F32)
    projected = projected.reshape(2, steps, slots, heads, HEAD_DIM)
    sums = everyone[:, own_rows:].reshape(n_ctx, n_tp, rows, n_ctx, own_columns).astype(F32)
    sums = jnp.sum(sums, axis=0).transpose(1, 2, 0, 3).reshape(rows, -1)
    columns = (sums * inverse).reshape(steps, slots, -1)

    own_slots = lax.dynamic_slice_in_dim(decode_prompt, group * slots, slots)
    taken = jnp.stack(
        [lax.dynamic_index_in_dim(arrived, own_slots[s] // slots, 0, keepdims=False) for s in range(slots)]
    ).astype(F32)
    at = combined.size // slots // 128
    ssm_state = taken[:, :at].reshape(slots, heads, HEAD_DIM, state_width)
    tail_rows = x_tail.size // slots // 128
    x_window = taken[:, at : at + tail_rows].reshape(slots, 3, heads, HEAD_DIM)
    bc_rows = bc_tail.size // slots // 128
    bc_window = taken[:, at + tail_rows : at + tail_rows + bc_rows].reshape(slots, 3, -1)

    head_start = 2 * state_width + (tp * n_ctx + ctx) * heads
    dt_raw = lax.dynamic_slice_in_dim(columns, head_start, heads, 2)
    decay_rate = -jnp.exp(a_log)
    gated_steps = []
    for moment in range(steps):
        x_window = jnp.concatenate([x_window, projected[1, moment][:, None]], axis=1)
        bc_window = jnp.concatenate([bc_window, columns[moment, :, None, : 2 * state_width]], axis=1)
        x_conv = jax.nn.silu(jnp.einsum("pkhe,khe->phe", x_window, conv_x_weight) + conv_x_bias)
        bc_conv = jax.nn.silu(jnp.einsum("pkn,kn->pn", bc_window, conv_bc_weight) + conv_bc_bias)
        step_size = jax.nn.softplus(dt_raw[moment] + dt_bias)
        retain = jnp.exp(step_size * decay_rate)
        ssm_state = (
            retain[:, :, None, None] * ssm_state
            + (step_size[:, :, None] * x_conv)[:, :, :, None] * bc_conv[:, None, None, :state_width]
        )
        output = (
            jnp.einsum("phen,pn->phe", ssm_state, bc_conv[:, state_width:])
            + d_skip[None, :, None] * x_conv
        )
        gated_steps.append(output * jax.nn.silu(projected[0, moment]))
        x_window = x_window[:, 1:]
        bc_window = bc_window[:, 1:]
    gated = jnp.stack(gated_steps).reshape(rows, channels)
    squares = jnp.sum(gated * gated, axis=1)
    weighted = (gated * gate_norm_gain.reshape(-1)).astype(BF)
    partial_out = jnp.dot(weighted, w_out.reshape(channels, model), preferred_element_type=F32)
    partial_out = jnp.swapaxes(partial_out.reshape(rows, n_ctx * n_tp, -1), 0, 1)
    partial_out = partial_out.reshape(n_ctx * n_tp, -1, 128).astype(BF)
    square_parts = jnp.concatenate(in_three(squares))
    square_parts = jnp.pad(square_parts, (0, 128 * 4 - square_parts.shape[0])).reshape(1, 4, 128)
    outgoing = jnp.concatenate(
        [partial_out, jnp.broadcast_to(square_parts, (n_ctx * n_tp, 4, 128))], axis=1
    )
    incoming = jnp.sum(exchange(outgoing, BOTH).astype(F32), axis=0)
    out_rows = partial_out.shape[1]
    total = jnp.sum(incoming[out_rows, : 3 * rows].reshape(3, rows), axis=0)
    scale = lax.rsqrt(total / (HEADS * HEAD_DIM) + EPS)
    mixed = incoming[:out_rows].reshape(rows, -1) * scale[:, None]
    return (mixed.reshape(steps, slots, -1).astype(BF), ssm_state)


def solution(mesh):
    return jax.shard_map(
        per_device,
        mesh=mesh,
        in_specs=(
            P(),
            P(),
            P("dp", ("ctx", "tp")),
            P(),
            P(None, ("tp", "ctx"), None, None),
            P(None, ("ctx", "tp")),
            P(None, ("tp", "ctx"), None),
            P(("tp", "ctx"), None),
            P(),
            P(),
            P(("tp", "ctx")),
            P(("tp", "ctx")),
            P(("tp", "ctx")),
            P(("tp", "ctx"), None),
            P(("tp", "ctx"), None, None),
            P("ctx", "dp", "tp", None, None),
            P("ctx", "dp", "tp"),
            P("dp", None, ("tp", "ctx"), None),
            P("dp", None, None),
        ),
        out_specs=(P(None, "dp", ("ctx", "tp")), P("dp", ("tp", "ctx"), None, None)),
        check_vma=False,
    )
```

time: 179 us -> 136 us (0.76)
  waiting for transfers between devices: 40 us -> 9.13 us
  starting transfers between devices: 40.8 us -> 27.8 us
  blocking collectives: 60.8 us -> 52.7 us
  between operations: 1.22 us -> 6.49 us
  other arithmetic: 9.52 us -> 14.2 us
    all_to_all x5 -> x3, waiting for transfers between devices: 40 us -> 9.13 us  [exchange(): return lax.all_to_all(pieces, axis, 0, 0, tiled=True)]
    psum x0 -> x1, blocking collectives: none -> 24.6 us  [per_device(): found = lax.psum(found, 'dp')]
    all_to_all x2 -> x1, blocking collectives: 40.5 us -> 16.4 us  [exchange(): return lax.all_to_all(pieces, axis, 0, 0, tiled=True)]
    all_to_all x5 -> x3, starting transfers between devices: 40.8 us -> 27.8 us  [exchange(): return lax.all_to_all(pieces, axis, 0, 0, tiled=True)]
    all_gather x1, blocking collectives: 20.3 us -> 11.7 us  [per_device(): beside = lax.all_gather(own, 'tp')]
    convert_element_type x2 -> x8, local copies, waits for them, and re-layouts: 0.17 us -> 6.33 us  [the longest x1 5.71 us: per_device(): everyone[:, own_rows:].reshape(n_ctx, n_tp, rows, n_ctx, own_columns)]
    unnamed x53 -> x44, local copies, waits for them, and re-layouts: 5.79 us -> 0.81 us
    exp x5 -> x1, local copies, waits for them, and re-layouts: 2.73 us -> 0.1 us  [per_device(): weight = jnp.exp(-later)[..., None, None]]
  transfers between devices with their start and end apart: 5 -> 3, of which waited for: 5 -> 1; matrix products, arithmetic and copies ran while one was open for 12% -> 19% of each run, Pallas kernels for 0% -> 0%
where the time goes in v1:
time: 136 us; the launch traced here: 135 us
  blocking collectives  52.7 us (39%)
  starting transfers between devices  27.8 us (20%)
  local copies, waits for them, and re-layouts  19.7 us (14%)
  other arithmetic  14.2 us (10%)
  waiting for transfers between devices  9.13 us (7%)
  between operations  6.49 us (5%)
  matrix products  5.28 us (4%)
    all_to_all x3, starting transfers between devices, exchange(): return lax.all_to_all(pieces, axis, 0, 0, tiled=True)  27.8 us
    psum x1, blocking collectives, per_device(): found = lax.psum(found, 'dp')  24.6 us
    all_to_all x1, blocking collectives, exchange(): return lax.all_to_all(pieces, axis, 0, 0, tiled=True)  16.4 us
    all_gather x1, blocking collectives, per_device(): beside = lax.all_gather(own, 'tp')  11.7 us
    all_to_all x3, waiting for transfers between devices, exchange(): return lax.all_to_all(pieces, axis, 0, 0, tiled=True)  9.13 us
    convert_element_type x1, local copies, waits for them, and re-layouts, per_device(): everyone[:, own_rows:].reshape(n_ctx, n_tp, rows, n_ctx, own_columns)  5.71 us
  transfers between devices with their start and end apart: 3, of which 1 were waited for; matrix products, arithmetic and copies ran while one was open for 19% of the time, Pallas kernels for 0%

profile of v1, /device:TPU:1, one launch (start us, length us, event | category | flops | bytes accessed | tf_op | source)
XLA Modules:
  0.0 135.3 jit_solution(1942876022011710154)
XLA Ops:
  0.7 0.9 reshape_squeeze.10
  1.8 1.3 copy.239
  3.3 1.1 fusion.5
  4.5 13.4 %all-to-all-start = ((bf16[16,288,128]{2,1,0:T(8,128)(2,1)}), bf16[16,288,128]{2,1,0:T(8,128)(2,1)S(1)}, u32[]{:S(2)}, u32[]{:S(2)}) async-start(bf16[16,288,128]{2,1,0:T(8,128)(2,1)} %fusion.5), calls=%async_computation | async-start | bytes 2359296 | tf_op jit(solution)/shard_map/all_to_all | solution.py:15
  25.8 0.8 dynamic_slice.20
  26.6 1.6 %fusion.7 = bf16[64,64]{1,0:T(8,128)(2,1)S(1)} fusion(bf16[6285,64]{0,1:T(8,128)(2,1)} %param.21, s32[64]{0:T(128)S(1)} %sub.53), kind=kOutput, calls=%fused_computation.11 | convolution fusion | flops 51893056 | bytes 812928 | tf_op jit(solution)/shard_map/dot_general | solution.py:78
  28.2 24.6 %psum.7 = bf16[64,64]{1,0:T(8,128)(2,1)S(1)} all-reduce(bf16[64,64]{1,0:T(8,128)(2,1)S(1)} %fusion.7), channel_id=1, replica_groups=mesh['ctx'=16,'dp'=8,'tp'=4] {'dp'}, use_global_device_ids=true, to_apply=%region_1.2 | all-reduce | flops 4096 | bytes 16384 | tf_op jit(solution)/shard_map/psum | solution.py:79
  52.9 11.7 %all-gather = bf16[32,64]{1,0:T(8,128)(2,1)S(1)} all-gather(bf16[8,64]{1,0:T(8,128)(2,1)S(1)} %constant_dynamic-slice_fusion.6), channel_id=2, replica_groups=mesh['ctx'=16,'dp'=8,'tp'=4] {'tp'}, dimensions={0}, use_global_device_ids=true | all-gather | bytes 5120 | tf_op jit(solution)/shard_map/all_gather | solution.py:81
  64.7 2.3 %copy.273 = bf16[4096,128]{1,0:T(8,128)(2,1)} copy(bf16[4096,128]{0,1:T(8,128)(2,1)} %bitcast.343) | data formatting | bytes 2097152 | tf_op jit(solution)/shard_map/dot_general | solution.py:160
  69.4 0.7 broadcast_in_dim.40
  70.1 10.3 %all-to-all-start.1 = ((bf16[64,10,128]{2,1,0:T(8,128)(2,1)}), bf16[64,10,128]{2,1,0:T(8,128)(2,1)S(1)}, u32[]{:S(2)}, u32[]{:S(2)}) async-start(bf16[64,10,128]{2,1,0:T(8,128)(2,1)} %broadcast_in_dim.40), calls=%async_computation.1 | async-start | bytes 524288 | tf_op jit(solution)/shard_map/all_to_all | solution.py:15
  81.8 1.4 %broadcast_select_fusion = bf16[8,144,128]{2,1,0:T(8,128)(2,1)} fusion(pred[8]{0:T(512)(128)(4,1)} %reduce_or.9, bf16[144,128]{1,0:T(8,128)(2,1)S(1)} %get-tuple-element.31, bf16[144,128]{1,0:T(8,128)(2,1)S(1)} %get-tuple-element.30), kind=kLoop, calls=%fused_computation.15 | loop fusion | flops 147456 | bytes 368648 | tf_op jit(solution)/shard_map/jit(_where)/select_n | solution.py:111
  83.2 9.1 %all-to-all-done.1 = bf16[64,10,128]{2,1,0:T(8,128)(2,1)S(1)} async-done(((bf16[64,10,128]{2,1,0:T(8,128)(2,1)}), bf16[64,10,128]{2,1,0:T(8,128)(2,1)S(1)}, u32[]{:S(2)}, u32[]{:S(2)}) %all-to-all-start.1) | async-done | bytes 163872 | tf_op jit(solution)/shard_map/all_to_all | solution.py:15
  92.4 4.1 %all-to-all-start.2 = ((bf16[8,144,128]{2,1,0:T(8,128)(2,1)}), bf16[8,144,128]{2,1,0:T(8,128)(2,1)}, u32[]{:S(2)}, u32[]{:S(2)}) async-start(bf16[8,144,128]{2,1,0:T(8,128)(2,1)} %broadcast_select_fusion), calls=%async_computation.2 | async-start | bytes 589824 | tf_op jit(solution)/shard_map/all_to_all | solution.py:15
  97.4 5.7 %reshape.454 = f32[16,4,8,16,6]{4,3,2,1,0:T(8,128)} reshape(f32[64,6,128]{2,1,0:T(8,128)S(1)} %slice_convert_fusion) | data formatting | bytes 393216 | tf_op jit(solution)/shard_map/convert_element_type | solution.py:120
  103.1 2.6 %reduce_sum.76 = f32[4,8,16,6]{3,2,1,0:T(8,128)S(1)} reduce(f32[16,4,8,16,6]{4,3,2,1,0:T(8,128)} %reshape.454, f32[]{:T(128)} %constant.87.clone.1), dimensions={0}, to_apply=%region_2.3 | reduce | flops 46080 | bytes 208900 | tf_op jit(solution)/shard_map/reduce_sum | solution.py:121
  107.3 1.7 %fusion.18 = f32[8,2,2,64]{3,0,2,1:T(8,128)S(1)} fusion(bf16[2,2,64,4096]{3,2,1,0:T(8,128)(2,1)S(1)} %copy-done, f32[8,4096]{1,0:T(8,128)S(1)} %reshape.456, f32[4096]{0:T(1024)} %param.22, f32[8]{0:T(128)} %copy-done.16), kind=kOutput, calls=%fused_computation.35 | convolution fusion | flops 16875520 | bytes 2252832 | tf_op jit(solution)/shard_map/rd,khed->krhe/dot_general | solution.py:118
  109.1 1.4 %multiply_exponential_fusion.3 = (f32[2,2]{1,0:T(2,128)S(1)}, f32[2,2]{1,0:T(2,128)S(1)}, f32[2,2]{1,0:T(2,128)S(1)}, f32[2,2]{1,0:T(2,128)S(1)}, f32[2,2]{1,0:T...) fusion(f32[2]{0:T(128)} %exponential_negate_fusion, f32[2]{0:T(128)} %param.29, ...), kind=kLoop, calls=%fused_computation.217 | loop fusion | flops 128 | bytes 224 | tf_op jit(solution)/shard_map/exp | solution.py:145
  111.0 0.8 constant_dynamic-slice_fusion.4
  112.0 0.8 broadcast_multiply_fusion.4
  113.8 0.9 multiply_add_fusion
  114.9 0.7 fusion.87
  116.4 0.9 fusion.6
  117.9 16.4 %all_to_all.20 = bf16[64,8,128]{2,1,0:T(8,128)(2,1)S(1)} all-to-all(bf16[64,8,128]{2,1,0:T(8,128)(2,1)S(1)} %pad_maximum_fusion), channel_id=1, replica_groups=mesh['ctx'=16,'dp'=8,'tp'=4] {'ctx','tp'}, dimensions={0} | all-to-all | bytes 262144 | tf_op jit(solution)/shard_map/all_to_all | solution.py:15
  (163 shorter events, 13.5 us)
Async XLA Ops:
  0.6 106.7 %copy-start = (bf16[2,2,64,4096]{3,2,1,0:T(8,128)(2,1)S(1)}, bf16[2,2,64,4096]{3,2,1,0:T(8,128)(2,1)}, u32[]{:S(2)}) copy-start(bf16[2,2,64,4096]{3,2,1,0:T(8,128)(2,1)} %param.23) | copy-start | bytes 6291460
  0.6 2.5 %copy-start.3 = (bf16[4096,6]{0,1:T(8,128)(2,1)S(1)}, bf16[4096,6]{0,1:T(8,128)(2,1)}, u32[]{:S(2)}) copy-start(bf16[4096,6]{0,1:T(8,128)(2,1)} %param.24) | copy-start | bytes 147460
  3.3 14.6 %copy-start.19 = (s32[16]{0:T(128)S(1)}, s32[16]{0:T(128)}, u32[]{:S(2)}) copy-start(s32[16]{0:T(128)} %param.20) | copy-start | bytes 196
  3.3 20.5 %copy-start.14 = (bf16[2,3,256]{2,0,1:T(2,128)(2,1)S(1)}, bf16[2,3,256]{2,0,1:T(2,128)(2,1)}, u32[]{:S(2)}) copy-start(bf16[2,3,256]{2,0,1:T(2,128)(2,1)} %param.37) | copy-start | bytes 9220
  3.3 21.1 %copy-start.15 = (bf16[2,3,2,64]{3,2,1,0:T(2,128)(2,1)S(1)}, bf16[2,3,2,64]{3,2,1,0:T(2,128)(2,1)}, u32[]{:S(2)}) copy-start(bf16[2,3,2,64]{3,2,1,0:T(2,128)(2,1)} %param.36) | copy-start | bytes 4612
  3.3 21.9 %copy-start.17 = (s32[4,16]{1,0:T(4,128)S(1)}, s32[4,16]{1,0:T(4,128)}, u32[]{:S(2)}) copy-start(s32[4,16]{1,0:T(4,128)} %param.19) | copy-start | bytes 772
  4.5 63.7 %all-to-all-start = ((bf16[16,288,128]{2,1,0:T(8,128)(2,1)}), bf16[16,288,128]{2,1,0:T(8,128)(2,1)S(1)}, u32[]{:S(2)}, u32[]{:S(2)}) async-start(bf16[16,288,128]{2,1,0:T(8,128)(2,1)} %fusion.5), calls=%async_computation | async-start | bytes 2359296 | tf_op jit(solution)/shard_map/all_to_all | solution.py:15
  17.9 49.7 %copy-start.20 = (f32[2]{0:T(128)S(1)}, f32[2]{0:T(128)}, u32[]{:S(2)}) copy-start(f32[2]{0:T(128)} %param.30) | copy-start | bytes 28
  70.1 22.3 %all-to-all-start.1 = ((bf16[64,10,128]{2,1,0:T(8,128)(2,1)}), bf16[64,10,128]{2,1,0:T(8,128)(2,1)S(1)}, u32[]{:S(2)}, u32[]{:S(2)}) async-start(bf16[64,10,128]{2,1,0:T(8,128)(2,1)} %broadcast_in_dim.40), calls=%async_computation.1 | async-start | bytes 524288 | tf_op jit(solution)/shard_map/all_to_all | solution.py:15
  92.4 18.6 %all-to-all-start.2 = ((bf16[8,144,128]{2,1,0:T(8,128)(2,1)}), bf16[8,144,128]{2,1,0:T(8,128)(2,1)}, u32[]{:S(2)}, u32[]{:S(2)}) async-start(bf16[8,144,128]{2,1,0:T(8,128)(2,1)} %broadcast_select_fusion), calls=%async_computation.2 | async-start | bytes 589824 | tf_op jit(solution)/shard_map/all_to_all | solution.py:15
  96.7 0.5 copy-start.16
  106.3 0.6 copy-start.4
  106.9 3.6 %copy-start.8 = (f32[2,1,256]{2,0,1:T(2,128)S(1)}, f32[2,1,256]{2,0,1:T(2,128)}, u32[]{:S(2)}) copy-start(f32[2,1,256]{2,0,1:T(2,128)} %get-tuple-element.49) | copy-start | bytes 6148
  106.9 3.6 %copy-start.7 = (f32[2,1,256]{2,0,1:T(2,128)S(1)}, f32[2,1,256]{2,0,1:T(2,128)}, u32[]{:S(2)}) copy-start(f32[2,1,256]{2,0,1:T(2,128)} %get-tuple-element.48) | copy-start | bytes 6148
  106.9 3.6 %copy-start.6 = (f32[2,1,256]{2,0,1:T(2,128)S(1)}, f32[2,1,256]{2,0,1:T(2,128)}, u32[]{:S(2)}) copy-start(f32[2,1,256]{2,0,1:T(2,128)} %get-tuple-element.47) | copy-start | bytes 6148
  106.9 3.6 %copy-start.5 = (f32[2,1,256]{2,0,1:T(2,128)S(1)}, f32[2,1,256]{2,0,1:T(2,128)}, u32[]{:S(2)}) copy-start(f32[2,1,256]{2,0,1:T(2,128)} %get-tuple-element.46) | copy-start | bytes 6148
  107.1 4.9 %copy-start.12 = (f32[4,2,64]{2,1,0:T(2,128)S(1)}, f32[4,2,64]{2,1,0:T(2,128)}, u32[]{:S(2)}) copy-start(f32[4,2,64]{2,1,0:T(2,128)} %param.25) | copy-start | bytes 6148
  107.1 5.8 %copy-start.13 = (f32[4,256]{1,0:T(4,128)S(1)}, f32[4,256]{1,0:T(4,128)}, u32[]{:S(2)}) copy-start(f32[4,256]{1,0:T(4,128)} %param.27) | copy-start | bytes 12292
  107.1 5.8 %copy-start.18 = (f32[256]{0:T(256)S(1)}, f32[256]{0:T(256)}, u32[]{:S(2)}) copy-start(f32[256]{0:T(256)} %param.28) | copy-start | bytes 3076
  107.3 9.1 %copy-start.1 = (bf16[4096,128]{1,0:T(8,128)(2,1)S(1)}, bf16[4096,128]{1,0:T(8,128)(2,1)}, u32[]{:S(2)}) copy-start(bf16[4096,128]{1,0:T(8,128)(2,1)} %copy.273) | copy-start | bytes 3145732
  110.5 3.3 %copy-start.9 = (f32[2,2]{1,0:T(2,128)}, f32[2,2]{1,0:T(2,128)S(1)}, u32[]{:S(2)}) copy-start(f32[2,2]{1,0:T(2,128)S(1)} %get-tuple-element.14) | copy-start | bytes 52
  110.5 3.3 %copy-start.10 = (f32[2,2]{1,0:T(2,128)}, f32[2,2]{1,0:T(2,128)S(1)}, u32[]{:S(2)}) copy-start(f32[2,2]{1,0:T(2,128)S(1)} %get-tuple-element.40) | copy-start | bytes 52
  110.5 3.3 %copy-start.11 = (f32[2,2]{1,0:T(2,128)}, f32[2,2]{1,0:T(2,128)S(1)}, u32[]{:S(2)}) copy-start(f32[2,2]{1,0:T(2,128)S(1)} %get-tuple-element.42) | copy-start | bytes 52
  114.7 20.6 %copy-start.2 = (f32[2,2,64,128]{3,2,1,0:T(8,128)}, f32[2,2,64,128]{3,2,1,0:T(8,128)S(1)}, u32[]{:S(2)}) copy-start(f32[2,2,64,128]{3,2,1,0:T(8,128)S(1)} %multiply_add_fusion) | copy-start | bytes 393220

commit v2 on v1

v2 whole, which is shorter than its diff:
```python
import functools

import jax
import jax.numpy as jnp
from jax import lax
from jax.experimental import pallas as pl
from jax.experimental.pallas import tpu as pltpu
from jax.sharding import PartitionSpec as P

HEADS = 128
HEAD_DIM = 64
EPS = 1e-05
BOTH = ("ctx", "tp")
BF = jnp.bfloat16
F32 = jnp.float32
LANES = 128
HALF = 64
VMEM_LIMIT = 48 * 1024 * 1024

STATE_ROWS = 256
RATE_ROWS = 16
TOKEN_ROWS = 32
ONE_STATE = 128
TAIL_ROWS = 16
NEAR_ROWS = 64


def exchange(pieces, axis):
    return lax.all_to_all(pieces, axis, 0, 0, tiled=True)


def in_three(values):
    first = values.astype(BF)
    rest = values - first.astype(F32)
    second = rest.astype(BF)
    third = (rest - second.astype(F32)).astype(BF)
    return first, second, third


def silu(v):
    return v / (1.0 + jnp.exp(-v))


def low_half(shape=(8, LANES)):
    return lax.broadcasted_iota(jnp.int32, shape, 1) < HALF


def combine_kernel(chosen_ref, got_ref, tails_ref, out_ref, combined_ref):
    count = got_ref.shape[0]
    groups = out_ref.shape[0]
    rates = []
    for k in range(count):
        parts = got_ref[k, STATE_ROWS : STATE_ROWS + RATE_ROWS, :].astype(F32)
        rates.append(parts[0:4] + parts[4:8] + parts[8:12])
    weights = [None] * count
    later = jnp.zeros_like(rates[0])
    for k in reversed(range(count)):
        weights[k] = jnp.exp(-later)
        later = later + rates[k]
    for part in range(4):
        total = jnp.zeros((HEAD_DIM, LANES), F32)
        for k in range(count):
            own = got_ref[k, part * HEAD_DIM : (part + 1) * HEAD_DIM, :].astype(F32)
            total = total + (own * weights[k][part : part + 1]).astype(BF).astype(F32)
        at = (part % 2) * HEAD_DIM
        combined_ref[part // 2, at : at + HEAD_DIM, :] = total.astype(BF)
    for g in range(groups):
        prompt = chosen_ref[g]
        out_ref[g, 0:ONE_STATE, :] = combined_ref[prompt]
        out_ref[g, ONE_STATE : ONE_STATE + TAIL_ROWS, :] = tails_ref[prompt]
    low = low_half((TOKEN_ROWS, LANES))
    at = STATE_ROWS + RATE_ROWS
    for pair in range(0, count // 2, 2):
        early, late = [], []
        for k in (pair, pair + 1):
            one = got_ref[k, at : at + TOKEN_ROWS, :].astype(F32)
            two = got_ref[count // 2 + k, at : at + TOKEN_ROWS, :].astype(F32)
            early.append(jnp.where(low, one, pltpu.roll(two, HALF, 1)))
            late.append(jnp.where(low, pltpu.roll(one, HALF, 1), two))
        for g in range(groups):
            source = early if g < groups // 2 else late
            r = (g % (groups // 2)) * 8
            both = jnp.concatenate([s[r : r + 8] for s in source], axis=0)
            start = ONE_STATE + TAIL_ROWS + pair * 8
            out_ref[g, start : start + 16, :] = both.astype(BF)


def columns_kernel(place_ref, arrived_ref, gain_ref, weight_ref, out_ref, near_ref):
    groups = arrived_ref.shape[0]
    at = ONE_STATE + TAIL_ROWS
    total = arrived_ref[0, at : at + NEAR_ROWS, :].astype(F32)
    for g in range(1, groups):
        total = total + arrived_ref[g, at : at + NEAR_ROWS, :].astype(F32)
    pieces = []
    for k in range(NEAR_ROWS // 8):
        rows = total[k * 8 : (k + 1) * 8]
        near_ref[k] = rows
        pieces.append((rows * gain_ref[k : k + 1, :]).astype(BF))
    weighted = jnp.concatenate(pieces, axis=1)
    partial = lax.dot_general(
        weighted, weight_ref[...], (((1,), (1,)), ((), ())), preferred_element_type=F32
    )
    own = pltpu.roll(near_ref[place_ref[0]], place_ref[1], 1)
    lane = lax.broadcasted_iota(jnp.int32, (8, LANES), 1)
    first = partial.astype(BF).astype(F32)
    tile = jnp.where(lane < HALF, own, jnp.where(lane < HALF + 24, first, partial - first))
    out_ref[...] = jnp.broadcast_to(tile.astype(BF)[None], out_ref.shape)


def decode_kernel(
    place_ref,
    everyone_ref,
    arrived_ref,
    gain_ref,
    small_ref,
    w_zx_ref,
    w_out_ref,
    out_ref,
    start_ref,
    extra_ref,
    zx_ref,
    wo_ref,
    x_ref,
    b_ref,
    c_ref,
    sems,
):
    load_zx = pltpu.make_async_copy(w_zx_ref, zx_ref, sems.at[0])
    load_zx.start()
    load_out = pltpu.make_async_copy(w_out_ref, wo_ref, sems.at[1])
    load_out.start()
    peers = everyone_ref.shape[0]
    model = peers * HALF
    lane = lax.broadcasted_iota(jnp.int32, (8, LANES), 1)
    row = lax.broadcasted_iota(jnp.int32, (8, LANES), 0)
    low = lane < HALF

    tiles = [everyone_ref[p].astype(F32) for p in range(peers)]
    rows = [
        jnp.where(low, tiles[2 * n], pltpu.roll(tiles[2 * n + 1], HALF, 1)) for n in range(peers // 2)
    ]
    squares = rows[0] * rows[0]
    for r in rows[1:]:
        squares = squares + r * r
    inverse = lax.rsqrt(jnp.sum(squares, axis=1, keepdims=True) * (1.0 / model) + EPS)
    normed = jnp.concatenate(
        [(r * inverse * gain_ref[n : n + 1, :]).astype(BF) for n, r in enumerate(rows)], axis=1
    )

    columns = [jnp.zeros((8, LANES), F32) for _ in range(3)]
    for c in range(16):
        part = tiles[4 * c] + tiles[4 * c + 1] + tiles[4 * c + 2] + tiles[4 * c + 3]
        part = part + pltpu.roll(part, LANES - 24, 1)
        part = jnp.where((lane >= HALF) & (lane < HALF + 24), part, 0.0)
        first, offset = divmod(c * 24, LANES)
        part = pltpu.roll(part, (offset - HALF) % LANES, 1)
        if offset + 24 <= LANES:
            columns[first] = columns[first] + part
        else:
            columns[first] = columns[first] + jnp.where(lane >= offset, part, 0.0)
            columns[first + 1] = columns[first + 1] + jnp.where(lane < offset, part, 0.0)
    columns = [v * inverse for v in columns]

    for slot in range(2):
        tail = arrived_ref[place_ref[slot], ONE_STATE : ONE_STATE + TAIL_ROWS, :].astype(F32)
        for k in range(3):
            at = 2 * k + slot
            x_ref[at : at + 1, :] = tail[k : k + 1]
            b_ref[at : at + 1, :] = tail[3 + 2 * k : 4 + 2 * k]
            c_ref[at : at + 1, :] = tail[4 + 2 * k : 5 + 2 * k]
    b_ref[6:14, :] = columns[0]
    c_ref[6:14, :] = columns[1]

    def convolved(ref, weight_at, bias_at):
        total = ref[0:8, :] * small_ref[weight_at : weight_at + 1, :]
        for k in range(1, 4):
            total = total + ref[2 * k : 2 * k + 8, :] * small_ref[weight_at + k : weight_at + k + 1, :]
        return silu(total + small_ref[bias_at : bias_at + 1, :])

    b_conv = convolved(b_ref, 4, 13)
    c_conv = convolved(c_ref, 8, 14)

    raw = pltpu.roll(columns[2], place_ref[2], 1)
    raw = jnp.where(low, raw[:, 0:1], raw[:, 1:2]) + small_ref[15:16, :]
    step = jnp.maximum(raw, 0.0) + jnp.log1p(jnp.exp(-jnp.abs(raw)))
    log_retain = -step * jnp.exp(small_ref[16:17, :])

    def earlier(v, lag):
        return jnp.where(row >= 2 * lag, pltpu.roll(v, 2 * lag, 0), 0.0)

    log_total = log_retain
    for lag in range(1, 4):
        log_total = log_total + earlier(log_retain, lag)

    c_parts = jnp.concatenate([p.astype(F32) for p in in_three(c_conv)], axis=0).astype(BF)
    from_start = []
    for slot in range(2):
        state = arrived_ref[place_ref[slot], 0:ONE_STATE, :]
        start_ref[slot] = state
        product = lax.dot_general(
            c_parts, state, (((1,), (1,)), ((), ())), preferred_element_type=F32
        )
        from_start.append(product[0:8] + product[8:16] + product[16:24])
    y = jnp.exp(log_total) * jnp.where(row % 2 == 0, from_start[0], from_start[1])

    load_zx.wait()
    projected = lax.dot_general(
        normed, zx_ref[...], (((1,), (1,)), ((), ())), preferred_element_type=F32
    )
    gate = projected[:, 0:LANES]
    x_ref[6:14, :] = projected[:, LANES : 2 * LANES]
    x_conv = convolved(x_ref, 0, 12)
    drive = step * x_conv
    y = y + small_ref[17:18, :] * x_conv
    for lag in range(4):
        match = jnp.sum(c_conv * earlier(b_conv, lag), axis=1, keepdims=True)
        if lag == 0:
            y = y + drive * match
        else:
            decay = jnp.exp(log_total - earlier(log_total, lag))
            y = y + decay * earlier(drive, lag) * match
    gated = y * silu(gate)
    total = jnp.sum(gated * gated, axis=1, keepdims=True)
    parts = [p.astype(F32) for p in in_three(total)]
    aside = jnp.where(
        lane == HALF,
        parts[0],
        jnp.where(lane == HALF + 1, parts[1], jnp.where(lane == HALF + 2, parts[2], 0.0)),
    )
    weighted = (gated * small_ref[18:19, :]).astype(BF)

    last = jnp.where(row % 2 == 0, log_total[6:7], log_total[7:8])
    extra_ref[0:8, :] = jnp.exp(last - log_total) * drive
    extra_ref[8:16, :] = b_conv
    extra_ref[16:24, :] = jnp.exp(last)

    load_out.wait()
    for n in range(peers // 8):
        wide = jnp.dot(
            weighted, wo_ref[:, n * 512 : (n + 1) * 512], preferred_element_type=F32
        )
        for m in range(4):
            piece = wide[:, m * LANES : (m + 1) * LANES]
            out_ref[8 * n + 2 * m] = jnp.where(low, piece, aside).astype(BF)
            out_ref[8 * n + 2 * m + 1] = jnp.where(low, pltpu.roll(piece, HALF, 1), aside).astype(BF)


def finish_kernel(incoming_ref, out_ref):
    total = incoming_ref[0].astype(F32)
    for p in range(1, incoming_ref.shape[0]):
        total = total + incoming_ref[p].astype(F32)
    squares = total[:, HALF : HALF + 1] + total[:, HALF + 1 : HALF + 2] + total[:, HALF + 2 : HALF + 3]
    scale = lax.rsqrt(squares * (1.0 / (HEADS * HEAD_DIM)) + EPS)
    out_ref[...] = (total[:, 0:HALF] * scale).astype(BF)


VM = pl.BlockSpec(memory_space=pltpu.VMEM)
SM = pl.BlockSpec(memory_space=pltpu.SMEM)
HB = pl.BlockSpec(memory_space=pl.ANY)
PARAMS = pltpu.CompilerParams(vmem_limit_bytes=VMEM_LIMIT)


def per_device(
    token_ids,
    decode_prompt,
    embedding,
    norm_gain,
    w_zx,
    w_bcdt,
    conv_x_weight,
    conv_x_bias,
    conv_bc_weight,
    conv_bc_bias,
    dt_bias,
    a_log,
    d_skip,
    gate_norm_gain,
    w_out,
    state_parts,
    seg_rate,
    x_tail,
    bc_tail,
):
    ctx, group, tp = (lax.axis_index(a) for a in ("ctx", "dp", "tp"))
    n_ctx, n_dp, n_tp = (lax.axis_size(a) for a in ("ctx", "dp", "tp"))
    peers = n_ctx * n_tp
    slots = state_parts.shape[1]
    heads = w_zx.shape[1]
    width = state_parts.shape[-1]
    steps = token_ids.shape[0]
    vocab_rows, features = embedding.shape
    model = norm_gain.shape[0]
    rows = steps * slots
    channels = heads * HEAD_DIM

    prompts = decode_prompt.shape[0]
    chosen = (decode_prompt[:, None] == jnp.arange(prompts)[None, :]).astype(jnp.int32)
    tokens = jnp.sum(token_ids[:, None, :] * chosen[None], axis=2)
    tokens = jnp.swapaxes(tokens.reshape(steps, n_dp, slots), 0, 1).reshape(-1)
    hot = (tokens[:, None] - group * vocab_rows == jnp.arange(vocab_rows)[None, :]).astype(BF)
    found = jnp.dot(hot, embedding, preferred_element_type=F32).astype(BF)
    found = jnp.concatenate([found[:TOKEN_ROWS], found[TOKEN_ROWS:]], axis=1)

    states = state_parts[0].reshape(slots, n_ctx, heads, HEAD_DIM, width)
    states = jnp.swapaxes(states, 0, 1).reshape(n_ctx, STATE_ROWS, width)
    rates = jnp.swapaxes(seg_rate[0].reshape(slots, n_ctx, heads), 0, 1)
    rates = jnp.stack(in_three(rates), axis=1).reshape(n_ctx, -1)
    rates = jnp.pad(rates, ((0, 0), (0, RATE_ROWS - rates.shape[1])))
    rates = jnp.broadcast_to(rates[..., None], (n_ctx, RATE_ROWS, width))
    sent = jnp.concatenate(
        [states, rates, jnp.broadcast_to(found[None], (n_ctx, *found.shape))], axis=1
    )
    got = exchange(sent, "ctx")

    w_near = lax.all_gather(w_bcdt.T, "tp")
    own_columns = n_tp * w_bcdt.shape[1]
    w_near = w_near.reshape(own_columns, 2, n_ctx // 2, n_tp, features)
    w_near = lax.dynamic_index_in_dim(w_near, tp, 3, keepdims=False)
    w_near = jnp.swapaxes(w_near, 1, 2).reshape(own_columns, -1)
    w_near = jnp.concatenate([w_near, w_near], axis=0)
    w_near = jnp.pad(w_near, ((HALF, LANES - HALF - 2 * own_columns), (0, 0)))
    near_gain = norm_gain.reshape(2, n_ctx // 2, n_tp, features)
    near_gain = lax.dynamic_index_in_dim(near_gain, tp, 2, keepdims=False)
    near_gain = jnp.swapaxes(near_gain, 0, 1).reshape(n_ctx // 2, -1)
    tails = jnp.concatenate([x_tail.reshape(slots, 3, LANES), bc_tail.reshape(slots, 6, LANES)], axis=1)
    tails = jnp.pad(tails, ((0, 0), (0, TAIL_ROWS - tails.shape[1]), (0, 0)))
    wanted = decode_prompt.reshape(n_dp, slots) - group * slots
    prompt_for = jnp.any(wanted == 1, axis=1).astype(jnp.int32)
    own_slots = lax.dynamic_slice_in_dim(decode_prompt, group * slots, slots)
    spread = functools.partial(jnp.repeat, repeats=HEAD_DIM, total_repeat_length=channels)
    small = jnp.concatenate(
        [
            conv_x_weight.reshape(4, channels),
            conv_bc_weight[:, :width],
            conv_bc_weight[:, width:],
            conv_x_bias.reshape(1, channels),
            conv_bc_bias.reshape(2, width),
            spread(dt_bias)[None],
            spread(a_log)[None],
            spread(d_skip)[None],
            gate_norm_gain.reshape(1, channels),
        ],
        axis=0,
    )
    small = jnp.pad(small, ((0, -small.shape[0] % 8), (0, 0)))

    routed = pl.pallas_call(
        combine_kernel,
        out_shape=jax.ShapeDtypeStruct((n_dp, ONE_STATE + TAIL_ROWS + NEAR_ROWS, width), BF),
        in_specs=[SM, VM, VM],
        out_specs=VM,
        scratch_shapes=[pltpu.VMEM((slots, ONE_STATE, width), BF)],
        compiler_params=PARAMS,
        name="combine",
    )(prompt_for, got, tails)
    arrived = exchange(routed, "dp")

    place = jnp.stack([ctx % (n_ctx // 2), (ctx // (n_ctx // 2)) * HALF]).astype(jnp.int32)
    piece = pl.pallas_call(
        columns_kernel,
        out_shape=jax.ShapeDtypeStruct((peers, rows, LANES), BF),
        in_specs=[SM, VM, VM, VM],
        out_specs=VM,
        scratch_shapes=[pltpu.VMEM((NEAR_ROWS // 8, 8, LANES), F32)],
        compiler_params=PARAMS,
        name="columns",
    )(place, arrived, near_gain, w_near)
    everyone = exchange(piece, BOTH)

    head_at = (tp * n_ctx + ctx) * heads
    place = jnp.concatenate(
        [own_slots // slots, ((LANES - head_at) % LANES)[None]]
    ).astype(jnp.int32)
    outgoing, start, extra = pl.pallas_call(
        decode_kernel,
        out_shape=(
            jax.ShapeDtypeStruct((peers, rows, LANES), BF),
            jax.ShapeDtypeStruct((slots, ONE_STATE, width), BF),
            jax.ShapeDtypeStruct((24, LANES), F32),
        ),
        in_specs=[SM, VM, VM, VM, VM, HB, HB],
        out_specs=(VM, VM, VM),
        scratch_shapes=[
            pltpu.VMEM((2 * channels, model), BF),
            pltpu.VMEM((channels, model), BF),
            pltpu.VMEM((16, LANES), F32),
            pltpu.VMEM((16, LANES), F32),
            pltpu.VMEM((16, LANES), F32),
            pltpu.SemaphoreType.DMA((2,)),
        ],
        compiler_params=PARAMS,
        name="decode",
    )(
        place,
        everyone,
        arrived,
        norm_gain.reshape(model // LANES, LANES),
        small,
        w_zx.reshape(2 * channels, model),
        w_out.reshape(channels, model),
    )
    incoming = exchange(outgoing, BOTH)

    push = extra[0:8].reshape(steps, slots, channels)
    b_conv = extra[8:16].reshape(steps, slots, width)
    kept = extra[16:18]
    final = kept[:, :, None] * start.astype(F32) + jnp.einsum(
        "tpc,tpn->pcn", push, b_conv, precision=lax.Precision.HIGHEST
    )

    mixed = pl.pallas_call(
        finish_kernel,
        out_shape=jax.ShapeDtypeStruct((rows, features), BF),
        in_specs=[VM],
        out_specs=VM,
        compiler_params=PARAMS,
        name="finish",
    )(incoming)
    return (
        mixed.reshape(steps, slots, features),
        final.reshape(slots, heads, HEAD_DIM, width),
    )


def solution(mesh):
    return jax.shard_map(
        per_device,
        mesh=mesh,
        in_specs=(
            P(),
            P(),
            P("dp", ("ctx", "tp")),
            P(),
            P(None, ("tp", "ctx"), None, None),
            P(None, ("ctx", "tp")),
            P(None, ("tp", "ctx"), None),
            P(("tp", "ctx"), None),
            P(),
            P(),
            P(("tp", "ctx")),
            P(("tp", "ctx")),
            P(("tp", "ctx")),
            P(("tp", "ctx"), None),
            P(("tp", "ctx"), None, None),
            P("ctx", "dp", "tp", None, None),
            P("ctx", "dp", "tp"),
            P("dp", None, ("tp", "ctx"), None),
            P("dp", None, None),
        ),
        out_specs=(P(None, "dp", ("ctx", "tp")), P("dp", ("tp", "ctx"), None, None)),
        check_vma=False,
    )
```

time: 136 us -> 124 us (0.912)
  blocking collectives: 52.7 us -> 30.5 us
  starting transfers between devices: 27.8 us -> 42.4 us
  waiting for transfers between devices: 9.13 us -> 19.9 us
  other arithmetic: 14.2 us -> 8.27 us
  between operations: 6.49 us -> 1.05 us
  local copies, waits for them, and re-layouts: 19.7 us -> 14.5 us
  Pallas kernels: 0 us -> 5.04 us
  matrix products: 5.28 us -> 1.48 us
    psum x1 -> x0, blocking collectives: 24.6 us -> none  [per_device(): found = lax.psum(found, 'dp')]
    all_gather x1, blocking collectives: 11.7 us -> 30.5 us  [per_device(): w_near = lax.all_gather(w_bcdt.T, 'tp')]
    all_to_all x1 -> x0, blocking collectives: 16.4 us -> none  [exchange(): return lax.all_to_all(pieces, axis, 0, 0, tiled=True)]
    all_to_all x3 -> x4, starting transfers between devices: 27.8 us -> 42.4 us  [exchange(): return lax.all_to_all(pieces, axis, 0, 0, tiled=True)]
    all_to_all x3 -> x4, waiting for transfers between devices: 9.13 us -> 19.9 us  [exchange(): return lax.all_to_all(pieces, axis, 0, 0, tiled=True)]
    convert_element_type x8 -> x0, local copies, waits for them, and re-layouts: 6.33 us -> none  [the longest x1 5.71 us: per_device(): everyone[:, own_rows:].reshape(n_ctx, n_tp, rows, n_ctx, own_columns)]
    unnamed x44 -> x48, local copies, waits for them, and re-layouts: 0.81 us -> 6.22 us
    pallas_call x0 -> x4, Pallas kernels: none -> 5.04 us  [the longest x1 2.59 us: per_device(): pl.pallas_call(decode_kernel, out_shape=(jax.ShapeDtypeStruct((peers, row...]
  transfers between devices with their start and end apart: 3 -> 4, of which waited for: 1 -> 3; matrix products, arithmetic and copies ran while one was open for 19% -> 11% of each run, Pallas kernels for 0% -> 0%
where the time goes in v2:
time: 124 us; the launch traced here: 123 us
  starting transfers between devices  42.4 us (34%)
  blocking collectives  30.5 us (25%)
  waiting for transfers between devices  19.9 us (16%)
  local copies, waits for them, and re-layouts  14.5 us (12%)
  other arithmetic  8.27 us (7%)
  Pallas kernels  5.04 us (4%)
  matrix products  1.48 us (1%)
    all_to_all x4, starting transfers between devices, exchange(): return lax.all_to_all(pieces, axis, 0, 0, tiled=True)  42.4 us
    all_gather x1, blocking collectives, per_device(): w_near = lax.all_gather(w_bcdt.T, 'tp')  30.5 us
    all_to_all x4, waiting for transfers between devices, exchange(): return lax.all_to_all(pieces, axis, 0, 0, tiled=True)  19.9 us
    unnamed x48, local copies, waits for them, and re-layouts  6.22 us
    broadcast_in_dim x1, other arithmetic, per_device(): spread(d_skip)[None]  3.84 us
    pallas_call x1, Pallas kernels, per_device(): pl.pallas_call(decode_kernel, out_shape=(jax.ShapeDtypeStruct((peers, row...  2.59 us
  transfers between devices with their start and end apart: 4, of which 3 were waited for; matrix products, arithmetic and copies ran while one was open for 11% of the time, Pallas kernels for 0%

profile of v2, /device:TPU:1, one launch (start us, length us, event | category | flops | bytes accessed | tf_op | source)
XLA Modules:
  0.0 123.2 jit_solution(11868133446952215805)
XLA Ops:
  0.7 0.9 reshape_squeeze.7
  1.7 0.7 fusion.10
  2.4 0.8 multiply_reduce_fusion
  4.5 1.2 pad_maximum_fusion
  5.6 13.6 %all-to-all-start = ((bf16[16,304,128]{2,1,0:T(8,128)(2,1)}), bf16[16,304,128]{2,1,0:T(8,128)(2,1)S(1)}, u32[]{:S(2)}, u32[]{:S(2)}) async-start(bf16[16,304,128]{2,1,0:T(8,128)(2,1)} %pad_maximum_fusion), calls=%async_computation | async-start | bytes 2490368 | tf_op jit(solution)/shard_map/all_to_all | solution.py:29
  19.6 30.5 %all-gather.1 = bf16[4,6,4096]{2,1,0:T(8,128)(2,1)S(1)} all-gather(bf16[1,6,4096]{2,1,0:T(8,128)(2,1)S(1)} %bitcast.76), channel_id=2, replica_groups=mesh['ctx'=16,'dp'=8,'tp'=4] {'tp'}, dimensions={0}, use_global_device_ids=true | all-gather | bytes 245760 | tf_op jit(solution)/shard_map/all_gather | solution.py:315
  51.3 0.9 combine.1
  52.2 0.7 copy-done.2
  53.0 7.0 %all-to-all-start.1 = ((bf16[8,208,128]{2,1,0:T(8,128)(2,1)}), bf16[8,208,128]{2,1,0:T(8,128)(2,1)S(1)}, u32[]{:S(2)}, u32[]{:S(2)}) async-start(bf16[8,208,128]{2,1,0:T(8,128)(2,1)} %copy-done.2), calls=%async_computation.1 | async-start | bytes 851968 | tf_op jit(solution)/shard_map/all_to_all | solution.py:29
  61.8 0.7 fusion.6.weight_ref
  62.5 8.5 %all-to-all-done.1.arrived_ref = bf16[8,208,128]{2,1,0:T(8,128)(2,1)S(1)} async-done(((bf16[8,208,128]{2,1,0:T(8,128)(2,1)}), bf16[8,208,128]{2,1,0:T(8,128)(2,1)S(1)}, u32[]{:S(2)}, u32[]{:S(2)}) %all-to-all-start.1) | async-done | bytes 426016 | tf_op jit(solution)/shard_map/all_to_all | solution.py:29
  71.0 0.9 copy-done.4
  72.0 0.7 columns.1
  73.4 15.1 %all-to-all-start.2 = ((bf16[64,8,128]{2,1,0:T(8,128)(2,1)}), bf16[64,8,128]{2,1,0:T(8,128)(2,1)S(1)}, u32[]{:S(2)}, u32[]{:S(2)}) async-start(bf16[64,8,128]{2,1,0:T(8,128)(2,1)} %copy-done.5), calls=%async_computation.2 | async-start | bytes 262144 | tf_op jit(solution)/shard_map/all_to_all | solution.py:29
  88.5 3.8 %select_bitcast_fusion = (f32[1,128]{1,0:T(1,128)S(1)}, f32[1,128]{1,0:T(1,128)S(1)}, f32[1,128]{1,0:T(1,128)S(1)}) fusion(pred[128]{0:T(512)(128)(4,1)S(1)} %copy-done.22, f32[]{:T(128)} %bitcast.26, f32[]{:T(128)} %bitcast.25, f32[]{:T(128)} %bitcast.23, f32[]{:T(128)} %bitcast.22, f32[]{:T(128)} %bitcast.20, f32[]{:T(128)} %bitcast.19), kind=kLoop, calls=%fused_computation.38 | loop fusion | flops 384 | bytes 1688 | tf_op jit(solution)/shard_map/broadcast_in_dim | solution.py:340
  92.5 0.8 reshape.169
  93.2 0.8 reshape.171
  95.3 3.5 %all-to-all-done.2.everyone_ref = bf16[64,8,128]{2,1,0:T(8,128)(2,1)S(1)} async-done(((bf16[64,8,128]{2,1,0:T(8,128)(2,1)}), bf16[64,8,128]{2,1,0:T(8,128)(2,1)S(1)}, u32[]{:S(2)}, u32[]{:S(2)}) %all-to-all-start.2) | async-done | bytes 131104 | tf_op jit(solution)/shard_map/all_to_all | solution.py:29
  98.8 1.2 copy-done.3
  101.4 2.6 %decode.1 = (bf16[64,8,128]{2,1,0:T(8,128)(2,1)S(1)}, bf16[2,128,128]{2,1,0:T(8,128)(2,1)S(1)}, f32[24,128]{1,0:T(8,128)S(1)}) custom-call(s32[3]{0:T(128)S(1)} %copy-done.10, bf16[64,8,128]{2,1,0:T(8,128)(2,1)S(1)} %all-to-all-done.2.everyone_ref, bf16[8,208,128]{2,1,0:T(8,128)(2,1)S(1)} %all-to-all-done.1.arrived_ref, f32[32,128]{1,0:T(8,128)S(1)} %bitcast.71, ...), custom_call_target="tpu_custom_call" | custom-call | tf_op jit(solution)/shard_map/decode/pallas_call | solution.py:374
  105.2 6.8 %all-to-all-start.3 = ((bf16[64,8,128]{2,1,0:T(8,128)(2,1)}), bf16[64,8,128]{2,1,0:T(8,128)(2,1)S(1)}, u32[]{:S(2)}, u32[]{:S(2)}) async-start(bf16[64,8,128]{2,1,0:T(8,128)(2,1)} %copy-done.6), calls=%async_computation.3 | async-start | bytes 262144 | tf_op jit(solution)/shard_map/all_to_all | solution.py:29
  113.4 1.1 convolution_add_fusion
  114.5 7.9 %all-to-all-done.3.incoming_ref = bf16[64,8,128]{2,1,0:T(8,128)(2,1)S(1)} async-done(((bf16[64,8,128]{2,1,0:T(8,128)(2,1)}), bf16[64,8,128]{2,1,0:T(8,128)(2,1)S(1)}, u32[]{:S(2)}, u32[]{:S(2)}) %all-to-all-start.3) | async-done | bytes 131104 | tf_op jit(solution)/shard_map/all_to_all | solution.py:29
  122.4 0.8 finish.1
  (90 shorter events, 10.6 us)
Async XLA Ops:
  0.6 2.9 %copy-start = (bf16[6285,64]{0,1:T(8,128)(2,1)S(1)}, bf16[6285,64]{0,1:T(8,128)(2,1)}, u32[]{:S(2)}) copy-start(bf16[6285,64]{0,1:T(8,128)(2,1)} %param.29) | copy-start | bytes 2413444
  0.6 3.5 %copy-start.11 = (bf16[1,2,32,64,128]{4,3,2,1,0:T(8,128)(2,1)S(1)}, bf16[1,2,32,64,128]{4,3,2,1,0:T(8,128)(2,1)}, u32[]{:S(2)}) copy-start(bf16[1,2,32,64,128]{4,3,2,1,0:T(8,128)(2,1)} %param.42) | copy-start | bytes 3145732
  5.6 13.6 %copy-start.21 = (s32[16]{0:T(128)S(1)}, s32[16]{0:T(128)}, u32[]{:S(2)}) copy-start(s32[16]{0:T(128)} %param.28) | copy-start | bytes 196
  5.6 13.9 %copy-start.15 = (bf16[2,3,256]{2,0,1:T(2,128)(2,1)S(1)}, bf16[2,3,256]{2,0,1:T(2,128)(2,1)}, u32[]{:S(2)}) copy-start(bf16[2,3,256]{2,0,1:T(2,128)(2,1)} %param.45) | copy-start | bytes 9220
  5.6 13.9 %copy-start.16 = (bf16[2,3,2,64]{3,2,1,0:T(2,128)(2,1)S(1)}, bf16[2,3,2,64]{3,2,1,0:T(2,128)(2,1)}, u32[]{:S(2)}) copy-start(bf16[2,3,2,64]{3,2,1,0:T(2,128)(2,1)} %param.44) | copy-start | bytes 4612
  5.6 14.0 %copy-start.12 = (bf16[4096,6]{0,1:T(8,128)(2,1)S(1)}, bf16[4096,6]{0,1:T(8,128)(2,1)}, u32[]{:S(2)}) copy-start(bf16[4096,6]{0,1:T(8,128)(2,1)} %param.32) | copy-start | bytes 147460
  5.6 45.6 %all-to-all-start = ((bf16[16,304,128]{2,1,0:T(8,128)(2,1)}), bf16[16,304,128]{2,1,0:T(8,128)(2,1)S(1)}, u32[]{:S(2)}, u32[]{:S(2)}) async-start(bf16[16,304,128]{2,1,0:T(8,128)(2,1)} %pad_maximum_fusion), calls=%async_computation | async-start | bytes 2490368 | tf_op jit(solution)/shard_map/all_to_all | solution.py:29
  19.2 31.8 %copy-start.7 = (f32[4096]{0:T(1024)S(1)}, f32[4096]{0:T(1024)}, u32[]{:S(2)}) copy-start(f32[4096]{0:T(1024)} %param.30) | copy-start | bytes 49156
  50.7 9.3 %copy-start.17 = (f32[2]{0:T(128)S(1)}, f32[2]{0:T(128)}, u32[]{:S(2)}) copy-start(f32[2]{0:T(128)} %param.37) | copy-start | bytes 28
  50.7 9.9 %copy-start.18 = (f32[2]{0:T(128)S(1)}, f32[2]{0:T(128)}, u32[]{:S(2)}) copy-start(f32[2]{0:T(128)} %param.38) | copy-start | bytes 28
  50.7 10.5 %copy-start.19 = (f32[2]{0:T(128)S(1)}, f32[2]{0:T(128)}, u32[]{:S(2)}) copy-start(f32[2]{0:T(128)} %param.39) | copy-start | bytes 28
  50.8 11.8 %copy-start.14 = (f32[4,256]{1,0:T(4,128)S(1)}, f32[4,256]{1,0:T(4,128)}, u32[]{:S(2)}) copy-start(f32[4,256]{1,0:T(4,128)} %param.35) | copy-start | bytes 12292
  51.2 37.3 %copy-start.22 = (pred[128]{0:T(512)(128)(4,1)S(1)}, pred[128]{0:T(512)(128)(4,1)}, u32[]{:S(2)}) copy-start(pred[128]{0:T(512)(128)(4,1)} %constant.225) | copy-start | bytes 388
  51.2 41.1 %copy-start.13 = (f32[4,2,64]{2,1,0:T(2,128)S(1)}, f32[4,2,64]{2,1,0:T(2,128)}, u32[]{:S(2)}) copy-start(f32[4,2,64]{2,1,0:T(2,128)} %param.33) | copy-start | bytes 6148
  51.3 42.7 %copy-start.20 = (f32[256]{0:T(256)S(1)}, f32[256]{0:T(256)}, u32[]{:S(2)}) copy-start(f32[256]{0:T(256)} %param.36) | copy-start | bytes 3076
  52.2 0.8 copy-start.2
  53.0 45.9 %copy-start.1 = (bf16[2,2,64,4096]{3,2,1,0:T(8,128)(2,1)S(1)}, bf16[2,2,64,4096]{3,2,1,0:T(8,128)(2,1)}, u32[]{:S(2)}) copy-start(bf16[2,2,64,4096]{3,2,1,0:T(8,128)(2,1)} %param.31) | copy-start | bytes 6291460
  53.0 18.1 %all-to-all-start.1 = ((bf16[8,208,128]{2,1,0:T(8,128)(2,1)}), bf16[8,208,128]{2,1,0:T(8,128)(2,1)S(1)}, u32[]{:S(2)}, u32[]{:S(2)}) async-start(bf16[8,208,128]{2,1,0:T(8,128)(2,1)} %copy-done.2), calls=%async_computation.1 | async-start | bytes 851968 | tf_op jit(solution)/shard_map/all_to_all | solution.py:29
  71.0 1.0 copy-start.4
  72.7 0.7 copy-start.5
  73.4 25.5 %all-to-all-start.2 = ((bf16[64,8,128]{2,1,0:T(8,128)(2,1)}), bf16[64,8,128]{2,1,0:T(8,128)(2,1)S(1)}, u32[]{:S(2)}, u32[]{:S(2)}) async-start(bf16[64,8,128]{2,1,0:T(8,128)(2,1)} %copy-done.5), calls=%async_computation.2 | async-start | bytes 262144 | tf_op jit(solution)/shard_map/all_to_all | solution.py:29
  98.8 1.2 copy-start.3
  100.1 0.7 copy-start.8
  105.2 17.1 %all-to-all-start.3 = ((bf16[64,8,128]{2,1,0:T(8,128)(2,1)}), bf16[64,8,128]{2,1,0:T(8,128)(2,1)S(1)}, u32[]{:S(2)}, u32[]{:S(2)}) async-start(bf16[64,8,128]{2,1,0:T(8,128)(2,1)} %copy-done.6), calls=%async_computation.3 | async-start | bytes 262144 | tf_op jit(solution)/shard_map/all_to_all | solution.py:29
  (3 other events, 1.8 us)

commit v3 on v2

v3 whole, which is shorter than its diff:
```python
import jax
import jax.numpy as jnp
from jax import lax
from jax.experimental import pallas as pl
from jax.experimental.pallas import tpu as pltpu
from jax.sharding import PartitionSpec as P

HEADS = 128
HEAD_DIM = 64
EPS = 1e-05
BOTH = ("ctx", "tp")
BF = jnp.bfloat16
F32 = jnp.float32
LANES = 128
HALF = 64
VMEM_LIMIT = 24 * 1024 * 1024

STATE_ROWS = 256
SIDE_ROWS = 16
ROWS_AT = 12
ONE_STATE = 128


def exchange(pieces, axis):
    return lax.all_to_all(pieces, axis, 0, 0, tiled=True)


def in_three(values):
    first = values.astype(BF)
    rest = values - first.astype(F32)
    second = rest.astype(BF)
    third = (rest - second.astype(F32)).astype(BF)
    return first, second, third


def silu(v):
    return v / (1.0 + jnp.exp(-v))


def low_half(shape=(8, LANES)):
    return lax.broadcasted_iota(jnp.int32, shape, 1) < HALF


def lookup_kernel(
    tokens_hbm, prompt_hbm, table_hbm, x_tail_hbm, bc_tail_hbm, out_ref,
    tokens_ref, prompt_ref, table_ref, x_tail_ref, bc_tail_ref, token_ref, block_ref, sems,
):
    pairs = [
        (tokens_hbm, tokens_ref),
        (prompt_hbm, prompt_ref),
        (table_hbm, table_ref),
        (x_tail_hbm, x_tail_ref),
        (bc_tail_hbm, bc_tail_ref),
    ]
    loads = [pltpu.make_async_copy(a, b, sems.at[n]) for n, (a, b) in enumerate(pairs)]
    for load in loads:
        load.start()
    group = lax.axis_index("dp")
    groups = out_ref.shape[0]
    slots = prompt_ref.shape[0] // groups
    steps = tokens_ref.shape[0]
    rows = steps * slots
    features, vocab_rows = table_ref.shape
    first = group * vocab_rows
    loads[0].wait()
    loads[1].wait()
    for g in range(groups):
        for step in range(steps):
            for slot in range(slots):
                token = tokens_ref[step, prompt_ref[g * slots + slot]] - first
                at = g * rows + step * slots + slot
                token_ref[at : at + 1, :] = jnp.full((1, LANES), token, jnp.int32)
    loads[2].wait()
    tokens = token_ref[:, 0:1]
    found = jnp.zeros((groups * rows, LANES), F32)
    whole = vocab_rows // LANES * LANES
    bounds = [*range(0, whole, 1024), whole, vocab_rows]
    for low_at, high_at in zip(bounds[:-1], bounds[1:]):
        ids = lax.broadcasted_iota(jnp.int32, (groups * rows, high_at - low_at), 1) + low_at
        hot = jnp.where(tokens == ids, 1.0, 0.0).astype(BF)
        table = table_ref[:, low_at:high_at]
        found = found + lax.dot_general(
            hot,
            jnp.concatenate([table, table], axis=0),
            (((1,), (1,)), ((), ())),
            preferred_element_type=F32,
        )
    low = low_half((4, LANES))
    loads[3].wait()
    loads[4].wait()
    for p in range(slots):
        block_ref[groups + p] = jnp.zeros((SIDE_ROWS, LANES), F32)
        for k in range(3):
            pair = x_tail_ref[p, k].astype(F32)
            block_ref[groups + p, k : k + 1, :] = jnp.concatenate([pair[0:1], pair[1:2]], axis=1)
            both = bc_tail_ref[k, p : p + 1, :].astype(F32)
            block_ref[groups + p, 3 + 2 * k : 4 + 2 * k, :] = both[:, 0:LANES]
            block_ref[groups + p, 4 + 2 * k : 5 + 2 * k, :] = both[:, LANES : 2 * LANES]
    for g in range(groups):
        wanted = group * slots + 1
        second = (prompt_ref[g * slots] == wanted) | (prompt_ref[g * slots + 1] == wanted)
        block_ref[g] = block_ref[jnp.where(second, groups + 1, groups)]
        block_ref[g, ROWS_AT : ROWS_AT + 4, :] = jnp.where(
            low, found[g * rows : g * rows + 4], found[g * rows + 4 : g * rows + 8]
        )
        out_ref[g] = block_ref[g].astype(BF)


def pack_kernel(near_ref, rates_ref, states_ref, out_ref, side_ref, sems):
    moves = []
    for p in range(states_ref.shape[0]):
        moves.append(
            pltpu.make_async_copy(
                states_ref.at[p], out_ref.at[:, p * ONE_STATE : (p + 1) * ONE_STATE, :], sems.at[p]
            )
        )
        moves[-1].start()
    total = near_ref[0].astype(F32)
    for g in range(1, near_ref.shape[0]):
        total = total + near_ref[g].astype(F32)
    row = lax.broadcasted_iota(jnp.int32, (SIDE_ROWS, LANES), 0)
    total = jnp.where(row >= ROWS_AT, total, 0.0)
    for c in range(out_ref.shape[0]):
        side_ref[c] = (rates_ref[c].astype(F32) + total).astype(BF)
    side = pltpu.make_async_copy(
        side_ref, out_ref.at[:, STATE_ROWS : STATE_ROWS + SIDE_ROWS, :], sems.at[2]
    )
    side.start()
    for move in moves:
        move.wait()
    side.wait()


def combine_kernel(chosen_ref, got_ref, out_ref, combined_ref, sems):
    count = got_ref.shape[0]
    groups = out_ref.shape[0]
    rates = []
    for k in range(count):
        parts = got_ref[k, STATE_ROWS : STATE_ROWS + SIDE_ROWS, :].astype(F32)
        rates.append(parts[0:4] + parts[4:8] + parts[8:12])
    weights = [None] * count
    later = jnp.zeros_like(rates[0])
    for k in reversed(range(count)):
        weights[k] = jnp.exp(-later)
        later = later + rates[k]
    for part in range(4):
        total = jnp.zeros((HEAD_DIM, LANES), F32)
        for k in range(count):
            own = got_ref[k, part * HEAD_DIM : (part + 1) * HEAD_DIM, :].astype(F32)
            total = total + (own * weights[k][part : part + 1]).astype(BF).astype(F32)
        at = (part % 2) * HEAD_DIM
        combined_ref[part // 2, at : at + HEAD_DIM, :] = total.astype(BF)
    moves = [
        pltpu.make_async_copy(combined_ref.at[chosen_ref[g]], out_ref.at[g], sems.at[g])
        for g in range(groups)
    ]
    for move in moves:
        move.start()
    for move in moves:
        move.wait()


def columns_kernel(place_ref, got_ref, gain_ref, weight_ref, out_ref, near_ref, tile_ref, sem):
    count = got_ref.shape[0]
    low = low_half()
    for c in range(count):
        side = got_ref[c, STATE_ROWS : STATE_ROWS + SIDE_ROWS, :].astype(F32)
        four = side[ROWS_AT : ROWS_AT + 4]
        near_ref[c, 0:4, :] = four
        near_ref[c, 4:8, :] = pltpu.roll(four, HALF, 1)
    pieces = []
    for k in range(count // 2):
        rows = jnp.where(low, near_ref[k], pltpu.roll(near_ref[count // 2 + k], HALF, 1))
        pieces.append((rows * gain_ref[k : k + 1, :]).astype(BF))
    weighted = jnp.concatenate(pieces, axis=1)
    partial = lax.dot_general(
        weighted, weight_ref[...], (((1,), (1,)), ((), ())), preferred_element_type=F32
    )
    own = near_ref[place_ref[0]]
    lane = lax.broadcasted_iota(jnp.int32, (8, LANES), 1)
    first = partial.astype(BF).astype(F32)
    tile = jnp.where(lane < HALF, own, jnp.where(lane < HALF + 24, first, partial - first))
    tile_ref[...] = jnp.broadcast_to(tile.astype(BF)[None], tile_ref.shape)
    move = pltpu.make_async_copy(tile_ref, out_ref, sem)
    move.start()
    move.wait()


def project_kernel(
    place_ref,
    everyone_ref,
    near_ref,
    gain_ref,
    small_ref,
    w_zx_ref,
    ready_ref,
    c_parts_ref,
    extra_ref,
    x_ref,
    b_ref,
    c_ref,
):
    peers = everyone_ref.shape[0]
    model = peers * HALF
    lane = lax.broadcasted_iota(jnp.int32, (8, LANES), 1)
    row = lax.broadcasted_iota(jnp.int32, (8, LANES), 0)
    low = lane < HALF

    tiles = [everyone_ref[p].astype(F32) for p in range(peers)]
    rows = [
        jnp.where(low, tiles[2 * n], pltpu.roll(tiles[2 * n + 1], HALF, 1)) for n in range(peers // 2)
    ]
    squares = rows[0] * rows[0]
    for r in rows[1:]:
        squares = squares + r * r
    inverse = lax.rsqrt(jnp.sum(squares, axis=1, keepdims=True) * (1.0 / model) + EPS)
    normed = jnp.concatenate(
        [(r * inverse * gain_ref[n : n + 1, :]).astype(BF) for n, r in enumerate(rows)], axis=1
    )

    columns = [jnp.zeros((8, LANES), F32) for _ in range(3)]
    for c in range(16):
        part = tiles[4 * c] + tiles[4 * c + 1] + tiles[4 * c + 2] + tiles[4 * c + 3]
        part = part + pltpu.roll(part, LANES - 24, 1)
        part = jnp.where((lane >= HALF) & (lane < HALF + 24), part, 0.0)
        first, offset = divmod(c * 24, LANES)
        part = pltpu.roll(part, (offset - HALF) % LANES, 1)
        if offset + 24 <= LANES:
            columns[first] = columns[first] + part
        else:
            columns[first] = columns[first] + jnp.where(lane >= offset, part, 0.0)
            columns[first + 1] = columns[first + 1] + jnp.where(lane < offset, part, 0.0)
    columns = [v * inverse for v in columns]

    for slot in range(2):
        tail = near_ref[place_ref[slot]].astype(F32)
        for k in range(3):
            at = 2 * k + slot
            x_ref[at : at + 1, :] = tail[k : k + 1]
            b_ref[at : at + 1, :] = tail[3 + 2 * k : 4 + 2 * k]
            c_ref[at : at + 1, :] = tail[4 + 2 * k : 5 + 2 * k]
    b_ref[6:14, :] = columns[0]
    c_ref[6:14, :] = columns[1]

    def convolved(ref, weight_at, bias_at):
        total = ref[0:8, :] * small_ref[weight_at : weight_at + 1, :]
        for k in range(1, 4):
            total = total + ref[2 * k : 2 * k + 8, :] * small_ref[weight_at + k : weight_at + k + 1, :]
        return silu(total + small_ref[bias_at : bias_at + 1, :])

    b_conv = convolved(b_ref, 4, 13)
    c_conv = convolved(c_ref, 8, 14)

    raw = pltpu.roll(columns[2], place_ref[2], 1)
    raw = jnp.where(low, raw[:, 0:1], raw[:, 1:2]) + small_ref[15:16, :]
    step = jnp.maximum(raw, 0.0) + jnp.log1p(jnp.exp(-jnp.abs(raw)))
    log_retain = -step * jnp.exp(small_ref[16:17, :])

    def earlier(v, lag):
        return jnp.where(row >= 2 * lag, pltpu.roll(v, 2 * lag, 0), 0.0)

    log_total = log_retain
    for lag in range(1, 4):
        log_total = log_total + earlier(log_retain, lag)

    parts = [p.astype(F32) for p in in_three(c_conv)]
    c_parts_ref[...] = jnp.concatenate([*parts, jnp.zeros_like(c_conv)], axis=0).astype(BF)

    projected = lax.dot_general(
        normed, w_zx_ref[...], (((1,), (1,)), ((), ())), preferred_element_type=F32
    )
    x_ref[6:14, :] = projected[:, LANES : 2 * LANES]
    x_conv = convolved(x_ref, 0, 12)
    drive = step * x_conv
    y = small_ref[17:18, :] * x_conv
    for lag in range(4):
        match = jnp.sum(c_conv * earlier(b_conv, lag), axis=1, keepdims=True)
        if lag == 0:
            y = y + drive * match
        else:
            decay = jnp.exp(log_total - earlier(log_total, lag))
            y = y + decay * earlier(drive, lag) * match
    ready_ref[0:8, :] = jnp.exp(log_total)
    ready_ref[8:16, :] = y
    ready_ref[16:24, :] = silu(projected[:, 0:LANES])
    ready_ref[24:32, :] = jnp.broadcast_to(small_ref[18:19, :], (8, LANES))

    last = jnp.where(row % 2 == 0, log_total[6:7], log_total[7:8])
    extra_ref[0:8, :] = jnp.exp(last - log_total) * drive
    extra_ref[8:16, :] = b_conv
    extra_ref[16:24, :] = jnp.exp(last)


def decode_kernel(
    place_ref, arrived_ref, ready_ref, c_parts_ref, w_out_hbm, out_ref, w_out_ref, tile_ref, load_sems, sems
):
    loads = []
    for n in range(out_ref.shape[0] // 16):
        part = pl.ds(n * 1024, 1024)
        loads.append(
            pltpu.make_async_copy(w_out_hbm.at[:, part], w_out_ref.at[:, part], load_sems.at[n])
        )
        loads[-1].start()
    lane = lax.broadcasted_iota(jnp.int32, (8, LANES), 1)
    row = lax.broadcasted_iota(jnp.int32, (8, LANES), 0)
    low = lane < HALF
    from_start = []
    for slot in range(2):
        product = lax.dot_general(
            c_parts_ref[...],
            arrived_ref[place_ref[slot]],
            (((1,), (1,)), ((), ())),
            preferred_element_type=F32,
        )
        from_start.append(product[0:8] + product[8:16] + product[16:24])
    y = ready_ref[0:8, :] * jnp.where(row % 2 == 0, from_start[0], from_start[1]) + ready_ref[8:16, :]
    gated = y * ready_ref[16:24, :]
    weighted = (gated * ready_ref[24:32, :]).astype(BF)
    total = jnp.sum(gated * gated, axis=1, keepdims=True)
    parts = [p.astype(F32) for p in in_three(total)]
    aside = jnp.where(
        lane == HALF,
        parts[0],
        jnp.where(lane == HALF + 1, parts[1], jnp.where(lane == HALF + 2, parts[2], 0.0)),
    )
    moves = []
    for n in range(out_ref.shape[0] // 16):
        loads[n].wait()
        wide = jnp.dot(
            weighted, w_out_ref[:, n * 1024 : (n + 1) * 1024], preferred_element_type=F32
        )
        for m in range(8):
            piece = wide[:, m * LANES : (m + 1) * LANES]
            tile_ref[16 * n + 2 * m] = jnp.where(low, piece, aside).astype(BF)
            tile_ref[16 * n + 2 * m + 1] = jnp.where(low, pltpu.roll(piece, HALF, 1), aside).astype(BF)
        part = pl.ds(16 * n, 16)
        moves.append(pltpu.make_async_copy(tile_ref.at[part], out_ref.at[part], sems.at[n]))
        moves[-1].start()
    for move in moves:
        move.wait()


def finish_kernel(incoming_ref, out_ref):
    total = incoming_ref[0].astype(F32)
    for p in range(1, incoming_ref.shape[0]):
        total = total + incoming_ref[p].astype(F32)
    squares = total[:, HALF : HALF + 1] + total[:, HALF + 1 : HALF + 2] + total[:, HALF + 2 : HALF + 3]
    scale = lax.rsqrt(squares * (1.0 / (HEADS * HEAD_DIM)) + EPS)
    out_ref[...] = (total[:, 0:HALF] * scale).astype(BF)


VM = pl.BlockSpec(memory_space=pltpu.VMEM)
SM = pl.BlockSpec(memory_space=pltpu.SMEM)
HB = pl.BlockSpec(memory_space=pltpu.HBM)


def in_hbm(array):
    return pltpu.with_memory_space_constraint(array, pltpu.HBM)


PARAMS = pltpu.CompilerParams(vmem_limit_bytes=VMEM_LIMIT)


def per_device(
    token_ids,
    decode_prompt,
    embedding,
    norm_gain,
    w_zx,
    w_bcdt,
    conv_x_weight,
    conv_x_bias,
    conv_bc_weight,
    conv_bc_bias,
    dt_bias,
    a_log,
    d_skip,
    gate_norm_gain,
    w_out,
    state_parts,
    seg_rate,
    x_tail,
    bc_tail,
):
    ctx, group, tp = (lax.axis_index(a) for a in ("ctx", "dp", "tp"))
    n_ctx, n_dp, n_tp = (lax.axis_size(a) for a in ("ctx", "dp", "tp"))
    peers = n_ctx * n_tp
    slots = state_parts.shape[1]
    heads = w_zx.shape[1]
    width = state_parts.shape[-1]
    steps = token_ids.shape[0]
    vocab_rows, features = embedding.shape
    model = norm_gain.shape[0]
    rows = steps * slots
    channels = heads * HEAD_DIM

    near = pl.pallas_call(
        lookup_kernel,
        out_shape=jax.ShapeDtypeStruct((n_dp, SIDE_ROWS, LANES), BF),
        in_specs=[HB] * 5,
        out_specs=VM,
        scratch_shapes=[
            pltpu.SMEM(token_ids.shape, jnp.int32),
            pltpu.SMEM(decode_prompt.shape, jnp.int32),
            pltpu.VMEM((features, vocab_rows), BF),
            pltpu.VMEM(x_tail.shape, BF),
            pltpu.VMEM((bc_tail.shape[1], slots, bc_tail.shape[2]), BF),
            pltpu.VMEM((n_dp * rows, LANES), jnp.int32),
            pltpu.VMEM((n_dp + slots, SIDE_ROWS, LANES), F32),
            pltpu.SemaphoreType.DMA((5,)),
        ],
        compiler_params=PARAMS,
        name="lookup",
    )(
        in_hbm(token_ids),
        in_hbm(decode_prompt),
        in_hbm(embedding.T),
        in_hbm(x_tail),
        in_hbm(jnp.swapaxes(bc_tail, 0, 1)),
    )
    near = exchange(near, "dp")

    rates = jnp.swapaxes(seg_rate[0].reshape(slots, n_ctx, heads), 0, 1)
    rates = jnp.stack(in_three(rates), axis=1).reshape(n_ctx, -1)
    rates = jnp.pad(rates, ((0, 0), (0, SIDE_ROWS - rates.shape[1])))
    rates = jnp.broadcast_to(rates[..., None], (n_ctx, SIDE_ROWS, width))
    sent = pl.pallas_call(
        pack_kernel,
        out_shape=jax.ShapeDtypeStruct((n_ctx, STATE_ROWS + SIDE_ROWS, width), BF),
        in_specs=[VM, VM, HB],
        out_specs=HB,
        scratch_shapes=[
            pltpu.VMEM((n_ctx, SIDE_ROWS, width), BF),
            pltpu.SemaphoreType.DMA((3,)),
        ],
        compiler_params=PARAMS,
        name="pack",
    )(near, rates, state_parts.reshape(slots, n_ctx, ONE_STATE, width))
    got = exchange(sent, "ctx")

    w_near = lax.all_gather(w_bcdt.T, "tp")
    own_columns = n_tp * w_bcdt.shape[1]
    w_near = w_near.reshape(own_columns, 2, n_ctx // 2, n_tp, features)
    w_near = lax.dynamic_index_in_dim(w_near, tp, 3, keepdims=False)
    w_near = jnp.swapaxes(w_near, 1, 2).reshape(own_columns, -1)
    w_near = jnp.concatenate([w_near, w_near], axis=0)
    w_near = jnp.pad(w_near, ((HALF, LANES - HALF - 2 * own_columns), (0, 0)))
    near_gain = norm_gain.reshape(2, n_ctx // 2, n_tp, features)
    near_gain = lax.dynamic_index_in_dim(near_gain, tp, 2, keepdims=False)
    near_gain = jnp.swapaxes(near_gain, 0, 1).reshape(n_ctx // 2, -1)
    wanted = decode_prompt.reshape(n_dp, slots) - group * slots
    prompt_for = jnp.any(wanted == 1, axis=1).astype(jnp.int32)
    own_slots = lax.dynamic_slice_in_dim(decode_prompt, group * slots, slots)

    def spread(values):
        return jnp.broadcast_to(values[:, None], (heads, HEAD_DIM)).reshape(1, channels)

    small = jnp.concatenate(
        [
            conv_x_weight.reshape(4, channels),
            conv_bc_weight[:, :width],
            conv_bc_weight[:, width:],
            conv_x_bias.reshape(1, channels),
            conv_bc_bias.reshape(2, width),
            spread(dt_bias),
            spread(a_log),
            spread(d_skip),
            gate_norm_gain.reshape(1, channels),
        ],
        axis=0,
    )
    small = jnp.pad(small, ((0, -small.shape[0] % 8), (0, 0)))

    piece = pl.pallas_call(
        columns_kernel,
        out_shape=jax.ShapeDtypeStruct((peers, rows, LANES), BF),
        in_specs=[SM, VM, VM, VM],
        out_specs=HB,
        scratch_shapes=[
            pltpu.VMEM((n_ctx, 8, LANES), F32),
            pltpu.VMEM((peers, rows, LANES), BF),
            pltpu.SemaphoreType.DMA(()),
        ],
        compiler_params=PARAMS,
        name="columns",
    )(ctx.astype(jnp.int32)[None], got, near_gain, w_near)
    piece, got = lax.optimization_barrier((piece, got))
    everyone = exchange(piece, BOTH)

    routed = pl.pallas_call(
        combine_kernel,
        out_shape=jax.ShapeDtypeStruct((n_dp, ONE_STATE, width), BF),
        in_specs=[SM, VM],
        out_specs=HB,
        scratch_shapes=[
            pltpu.VMEM((slots, ONE_STATE, width), BF),
            pltpu.SemaphoreType.DMA((n_dp,)),
        ],
        compiler_params=PARAMS,
        name="combine",
    )(prompt_for, got)
    arrived = exchange(routed, "dp")

    head_at = (tp * n_ctx + ctx) * heads
    place = jnp.concatenate(
        [own_slots // slots, ((LANES - head_at) % LANES)[None]]
    ).astype(jnp.int32)
    ready, c_parts, extra = pl.pallas_call(
        project_kernel,
        out_shape=(
            jax.ShapeDtypeStruct((32, LANES), F32),
            jax.ShapeDtypeStruct((32, LANES), BF),
            jax.ShapeDtypeStruct((24, LANES), F32),
        ),
        in_specs=[SM, VM, VM, VM, VM, VM],
        out_specs=(VM, VM, VM),
        scratch_shapes=[pltpu.VMEM((16, LANES), F32) for _ in range(3)],
        compiler_params=PARAMS,
        name="project",
    )(
        place,
        everyone,
        near,
        norm_gain.reshape(model // LANES, LANES),
        small,
        w_zx.reshape(2 * channels, model),
    )
    outgoing = pl.pallas_call(
        decode_kernel,
        out_shape=jax.ShapeDtypeStruct((peers, rows, LANES), BF),
        in_specs=[SM, VM, VM, VM, HB],
        out_specs=HB,
        scratch_shapes=[
            pltpu.VMEM((channels, model), BF),
            pltpu.VMEM((peers, rows, LANES), BF),
            pltpu.SemaphoreType.DMA((peers // 16,)),
            pltpu.SemaphoreType.DMA((peers // 16,)),
        ],
        compiler_params=PARAMS,
        name="decode",
    )(place, arrived, ready, c_parts, in_hbm(w_out.reshape(channels, model)))
    incoming = exchange(outgoing, BOTH)

    start = jnp.stack(
        [lax.dynamic_index_in_dim(arrived, place[s], 0, keepdims=False) for s in range(slots)]
    )
    push = extra[0:8].reshape(steps, slots, channels)
    b_conv = extra[8:16].reshape(steps, slots, width)
    kept = extra[16:18]
    final = kept[:, :, None] * start.astype(F32) + jnp.einsum(
        "tpc,tpn->pcn", push, b_conv, precision=lax.Precision.HIGHEST
    )

    mixed = pl.pallas_call(
        finish_kernel,
        out_shape=jax.ShapeDtypeStruct((rows, features), BF),
        in_specs=[VM],
        out_specs=VM,
        compiler_params=PARAMS,
        name="finish",
    )(incoming)
    return (
        mixed.reshape(steps, slots, features),
        final.reshape(slots, heads, HEAD_DIM, width),
    )


def solution(mesh):
    return jax.shard_map(
        per_device,
        mesh=mesh,
        in_specs=(
            P(),
            P(),
            P("dp", ("ctx", "tp")),
            P(),
            P(None, ("tp", "ctx"), None, None),
            P(None, ("ctx", "tp")),
            P(None, ("tp", "ctx"), None),
            P(("tp", "ctx"), None),
            P(),
            P(),
            P(("tp", "ctx")),
            P(("tp", "ctx")),
            P(("tp", "ctx")),
            P(("tp", "ctx"), None),
            P(("tp", "ctx"), None, None),
            P("ctx", "dp", "tp", None, None),
            P("ctx", "dp", "tp"),
            P("dp", None, ("tp", "ctx"), None),
            P("dp", None, None),
        ),
        out_specs=(P(None, "dp", ("ctx", "tp")), P("dp", ("tp", "ctx"), None, None)),
        check_vma=False,
    )
```

time: 124 us -> 119 us (0.960)
  local copies, waits for them, and re-layouts: 14.5 us -> 3.64 us
  waiting for transfers between devices: 19.9 us -> 29.4 us
  other arithmetic: 8.27 us -> 0.34 us
  Pallas kernels: 5.04 us -> 11.6 us
  between operations: 1.05 us -> 4.64 us
  starting transfers between devices: 42.4 us -> 39.5 us
  blocking collectives: 30.5 us -> 28 us
    all_to_all x4 -> x5, waiting for transfers between devices: 19.9 us -> 29.4 us  [exchange(): return lax.all_to_all(pieces, axis, 0, 0, tiled=True)]
    unnamed x48 -> x27, local copies, waits for them, and re-layouts: 6.22 us -> 0.1 us
    pallas_call x1 -> x4, Pallas kernels: 2.59 us -> 8.21 us  [the longest x1 3.07 us: per_device(): pl.pallas_call(decode_kernel, out_shape=jax.ShapeDtypeStruct((peers, rows...]
    broadcast_in_dim x1 -> x0, other arithmetic: 3.84 us -> none  [per_device(): spread(d_skip)[None]]
    all_to_all x4 -> x5, starting transfers between devices: 42.4 us -> 39.5 us  [exchange(): return lax.all_to_all(pieces, axis, 0, 0, tiled=True)]
    all_gather x1, blocking collectives: 30.5 us -> 28 us  [per_device(): w_near = lax.all_gather(w_bcdt.T, 'tp')]
    gather x3 -> x0, local copies, waits for them, and re-layouts: 1.8 us -> none  [the longest x1 0.62 us: per_device(): spread(dt_bias)[None]]
    concatenate x3 -> x0, other arithmetic: 1.24 us -> none  [the longest x1 1.15 us: per_device(): jnp.concatenate([states, rates, jnp.broadcast_to(found[None], (n_ctx, *fo...]
  transfers between devices with their start and end apart: 4 -> 5, of which waited for: 3 -> 4; matrix products, arithmetic and copies ran while one was open for 11% -> 4% of each run, Pallas kernels for 0% -> 3%
where the time goes in v3:
time: 119 us; the launch traced here: 118 us
  starting transfers between devices  39.5 us (33%)
  waiting for transfers between devices  29.4 us (25%)
  blocking collectives  28 us (24%)
  Pallas kernels  11.6 us (10%)
  between operations  4.64 us (4%)
  local copies, waits for them, and re-layouts  3.64 us (3%)
    all_to_all x5, starting transfers between devices, exchange(): return lax.all_to_all(pieces, axis, 0, 0, tiled=True)  39.5 us
    all_to_all x5, waiting for transfers between devices, exchange(): return lax.all_to_all(pieces, axis, 0, 0, tiled=True)  29.4 us
    all_gather x1, blocking collectives, per_device(): w_near = lax.all_gather(w_bcdt.T, 'tp')  28 us
    pallas_call x1, Pallas kernels, per_device(): pl.pallas_call(decode_kernel, out_shape=jax.ShapeDtypeStruct((peers, rows...  3.07 us
    pallas_call x1, Pallas kernels, per_device(): pl.pallas_call(lookup_kernel, out_shape=jax.ShapeDtypeStruct((n_dp, SIDE_...  2.73 us
  transfers between devices with their start and end apart: 5, of which 4 were waited for; matrix products, arithmetic and copies ran while one was open for 4% of the time, Pallas kernels for 3%

profile of v3, /device:TPU:1, one launch (start us, length us, event | category | flops | bytes accessed | tf_op | source)
XLA Modules:
  0.0 118.2 jit_solution(2077746369445179059)
XLA Ops:
  0.6 2.7 %lookup.1 = bf16[8,16,128]{2,1,0:T(8,128)(2,1)} custom-call(s32[4,16]{1,0:T(4,128)} %tokens_hbm.1, s32[16]{0:T(128)} %prompt_hbm.1, bf16[64,6285]{1,0:T(8,128)(2,1)} %bitcast.57, bf16[2,3,2,64]{3,2,1,0:T(2,128)(2,1)} %x_tail_hbm.1, bf16[3,2,256]{2,1,0:T(2,128)(2,1)} %bitcast.64), custom_call_target="tpu_custom_call" | custom-call | tf_op jit(solution)/shard_map/lookup/pallas_call | solution.py:397
  3.4 7.7 %all-to-all-start = ((bf16[8,16,128]{2,1,0:T(8,128)(2,1)}), bf16[8,16,128]{2,1,0:T(8,128)(2,1)S(1)}, u32[]{:S(2)}, u32[]{:S(2)}) async-start(bf16[8,16,128]{2,1,0:T(8,128)(2,1)} %lookup.1), calls=%async_computation | async-start | bytes 65536 | tf_op jit(solution)/shard_map/all_to_all | solution.py:25
  11.0 0.8 reshape_squeeze.3
  12.0 6.0 %all-to-all-done.near_ref = bf16[8,16,128]{2,1,0:T(8,128)(2,1)S(1)} async-done(((bf16[8,16,128]{2,1,0:T(8,128)(2,1)}), bf16[8,16,128]{2,1,0:T(8,128)(2,1)S(1)}, u32[]{:S(2)}, u32[]{:S(2)}) %all-to-all-start) | async-done | bytes 32800 | tf_op jit(solution)/shard_map/all_to_all | solution.py:25
  18.1 1.1 pack.1
  19.2 12.6 %all-to-all-start.1 = ((bf16[16,272,128]{2,1,0:T(8,128)(2,1)}), bf16[16,272,128]{2,1,0:T(8,128)(2,1)S(1)}, u32[]{:S(2)}, u32[]{:S(2)}) async-start(bf16[16,272,128]{2,1,0:T(8,128)(2,1)} %pack.1), calls=%async_computation.1 | async-start | bytes 2228224 | tf_op jit(solution)/shard_map/all_to_all | solution.py:25
  32.1 28.0 %all-gather.1 = bf16[4,6,4096]{2,1,0:T(8,128)(2,1)S(1)} all-gather(bf16[1,6,4096]{2,1,0:T(8,128)(2,1)S(1)} %bitcast.60), channel_id=2, replica_groups=mesh['ctx'=16,'dp'=8,'tp'=4] {'tp'}, dimensions={0}, use_global_device_ids=true | all-gather | bytes 245760 | tf_op jit(solution)/shard_map/all_gather | solution.py:441
  60.0 0.4 reshape.78
  60.4 0.2 constant_dynamic-slice_fusion.2
  60.8 0.1 reshape.79
  61.1 1.0 columns.1
  62.1 10.0 %all-to-all-start.3 = ((bf16[64,8,128]{2,1,0:T(8,128)(2,1)}), bf16[64,8,128]{2,1,0:T(8,128)(2,1)S(1)}, u32[]{:S(2)}, u32[]{:S(2)}) async-start(bf16[64,8,128]{2,1,0:T(8,128)(2,1)} %columns.1), calls=%async_computation.3 | async-start | bytes 262144 | tf_op jit(solution)/shard_map/all_to_all | solution.py:25
  72.1 0.6 fusion.12
  75.3 0.1 reduce_or.9
  76.1 1.6 %combine.1 = bf16[8,128,128]{2,1,0:T(8,128)(2,1)} custom-call(s32[8]{0:T(128)S(1)} %convert_element_type.27.chosen_ref, bf16[16,272,128]{2,1,0:T(8,128)(2,1)S(1)} %all-to-all-done.1.got_ref), custom_call_target="tpu_custom_call" | custom-call | tf_op jit(solution)/shard_map/combine/pallas_call | solution.py:490
  77.8 4.7 %all-to-all-done.3.everyone_ref = bf16[64,8,128]{2,1,0:T(8,128)(2,1)S(1)} async-done(((bf16[64,8,128]{2,1,0:T(8,128)(2,1)}), bf16[64,8,128]{2,1,0:T(8,128)(2,1)S(1)}, u32[]{:S(2)}, u32[]{:S(2)}) %all-to-all-start.3) | async-done | bytes 131104 | tf_op jit(solution)/shard_map/all_to_all | solution.py:25
  82.5 3.4 %all-to-all-start.2 = ((bf16[8,128,128]{2,1,0:T(8,128)(2,1)}), bf16[8,128,128]{2,1,0:T(8,128)(2,1)S(1)}, u32[]{:S(2)}, u32[]{:S(2)}) async-start(bf16[8,128,128]{2,1,0:T(8,128)(2,1)} %combine.1), calls=%async_computation.2 | async-start | bytes 524288 | tf_op jit(solution)/shard_map/all_to_all | solution.py:25
  87.3 1.3 %project.1 = (f32[32,128]{1,0:T(8,128)S(1)}, bf16[32,128]{1,0:T(8,128)(2,1)S(1)}, f32[24,128]{1,0:T(8,128)S(1)}) custom-call(s32[3]{0:T(128)S(1)} %pad_add_fusion.place_ref, bf16[64,8,128]{2,1,0:T(8,128)(2,1)S(1)} %all-to-all-done.3.everyone_ref, bf16[8,16,128]{2,1,0:T(8,128)(2,1)S(1)} %all-to-all-done.near_ref, f32[32,128]{1,0:T(8,128)S(1)} %bitcast.55, ...), custom_call_target="tpu_custom_call" | custom-call | tf_op jit(solution)/shard_map/project/pallas_call | solution.py:508
  88.7 9.5 %all-to-all-done.2.arrived_ref = bf16[8,128,128]{2,1,0:T(8,128)(2,1)S(1)} async-done(((bf16[8,128,128]{2,1,0:T(8,128)(2,1)}), bf16[8,128,128]{2,1,0:T(8,128)(2,1)S(1)}, u32[]{:S(2)}, u32[]{:S(2)}) %all-to-all-start.2) | async-done | bytes 262176 | tf_op jit(solution)/shard_map/all_to_all | solution.py:25
  98.2 3.1 %decode.1 = bf16[64,8,128]{2,1,0:T(8,128)(2,1)} custom-call(s32[3]{0:T(128)S(1)} %pad_add_fusion.place_ref, bf16[8,128,128]{2,1,0:T(8,128)(2,1)S(1)} %all-to-all-done.2.arrived_ref, f32[32,128]{1,0:T(8,128)S(1)} %get-tuple-element.9.ready_ref, bf16[32,128]{1,0:T(8,128)(2,1)S(1)} %get-tuple-element.10.c_parts_ref, bf16[128,4096]{1,0:T(8,128)(2,1)} %bitcast.56), custom_call_target="tpu_custom_call" | custom-call | tf_op jit(solution)/shard_map/decode/pallas_call | solution.py:528
  101.2 5.8 %all-to-all-start.4 = ((bf16[64,8,128]{2,1,0:T(8,128)(2,1)}), bf16[64,8,128]{2,1,0:T(8,128)(2,1)S(1)}, u32[]{:S(2)}, u32[]{:S(2)}) async-start(bf16[64,8,128]{2,1,0:T(8,128)(2,1)} %decode.1), calls=%async_computation.4 | async-start | bytes 262144 | tf_op jit(solution)/shard_map/all_to_all | solution.py:25
  107.1 1.1 convolution_add_fusion
  108.1 9.3 %all-to-all-done.4.incoming_ref = bf16[64,8,128]{2,1,0:T(8,128)(2,1)S(1)} async-done(((bf16[64,8,128]{2,1,0:T(8,128)(2,1)}), bf16[64,8,128]{2,1,0:T(8,128)(2,1)S(1)}, u32[]{:S(2)}, u32[]{:S(2)}) %all-to-all-start.4) | async-done | bytes 131104 | tf_op jit(solution)/shard_map/all_to_all | solution.py:25
  117.4 0.8 finish.1
  (62 shorter events, 1.8 us)
Async XLA Ops:
  0.6 17.5 %copy-start.1 = (bf16[1,2,32,64,128]{4,3,2,1,0:T(8,128)(2,1)S(1)}, bf16[1,2,32,64,128]{4,3,2,1,0:T(8,128)(2,1)}, u32[]{:S(2)}) copy-start(bf16[1,2,32,64,128]{4,3,2,1,0:T(8,128)(2,1)} %param.34) | copy-start | bytes 3145732
  3.4 14.6 %all-to-all-start = ((bf16[8,16,128]{2,1,0:T(8,128)(2,1)}), bf16[8,16,128]{2,1,0:T(8,128)(2,1)S(1)}, u32[]{:S(2)}, u32[]{:S(2)}) async-start(bf16[8,16,128]{2,1,0:T(8,128)(2,1)} %lookup.1), calls=%async_computation | async-start | bytes 65536 | tf_op jit(solution)/shard_map/all_to_all | solution.py:25
  19.2 12.7 %copy-start.2 = (f32[4096]{0:T(1024)S(1)}, f32[4096]{0:T(1024)}, u32[]{:S(2)}) copy-start(f32[4096]{0:T(1024)} %param.22) | copy-start | bytes 49156
  19.2 12.9 %copy-start.3 = (bf16[4096,6]{0,1:T(8,128)(2,1)S(1)}, bf16[4096,6]{0,1:T(8,128)(2,1)}, u32[]{:S(2)}) copy-start(bf16[4096,6]{0,1:T(8,128)(2,1)} %param.24) | copy-start | bytes 147460
  19.2 41.9 %all-to-all-start.1 = ((bf16[16,272,128]{2,1,0:T(8,128)(2,1)}), bf16[16,272,128]{2,1,0:T(8,128)(2,1)S(1)}, u32[]{:S(2)}, u32[]{:S(2)}) async-start(bf16[16,272,128]{2,1,0:T(8,128)(2,1)} %pack.1), calls=%async_computation.1 | async-start | bytes 2228224 | tf_op jit(solution)/shard_map/all_to_all | solution.py:25
  31.9 29.1 %copy-start.7 = (s32[16]{0:T(128)S(1)}, s32[16]{0:T(128)}, u32[]{:S(2)}) copy-start(s32[16]{0:T(128)} %prompt_hbm.1) | copy-start | bytes 196
  60.8 14.6 %copy-start.4 = (f32[4,2,64]{2,1,0:T(2,128)S(1)}, f32[4,2,64]{2,1,0:T(2,128)}, u32[]{:S(2)}) copy-start(f32[4,2,64]{2,1,0:T(2,128)} %param.25) | copy-start | bytes 6148
  60.8 14.7 %copy-start.8 = (f32[2,64]{1,0:T(2,128)S(1)}, f32[2,64]{1,0:T(2,128)}, u32[]{:S(2)}) copy-start(f32[2,64]{1,0:T(2,128)} %param.26) | copy-start | bytes 1540
  60.8 14.8 %copy-start.10 = (f32[2]{0:T(128)S(1)}, f32[2]{0:T(128)}, u32[]{:S(2)}) copy-start(f32[2]{0:T(128)} %param.29) | copy-start | bytes 28
  60.8 14.9 %copy-start.11 = (f32[2]{0:T(128)S(1)}, f32[2]{0:T(128)}, u32[]{:S(2)}) copy-start(f32[2]{0:T(128)} %param.30) | copy-start | bytes 28
  60.9 15.0 %copy-start.12 = (f32[2]{0:T(128)S(1)}, f32[2]{0:T(128)}, u32[]{:S(2)}) copy-start(f32[2]{0:T(128)} %param.31) | copy-start | bytes 28
  61.0 15.1 %copy-start.9 = (f32[2,64]{1,0:T(2,128)S(1)}, f32[2,64]{1,0:T(2,128)}, u32[]{:S(2)}) copy-start(f32[2,64]{1,0:T(2,128)} %param.32) | copy-start | bytes 1540
  62.1 23.8 %copy-start.5 = (f32[4,256]{1,0:T(4,128)S(1)}, f32[4,256]{1,0:T(4,128)}, u32[]{:S(2)}) copy-start(f32[4,256]{1,0:T(4,128)} %param.27) | copy-start | bytes 12292
  62.1 23.8 %copy-start.6 = (f32[256]{0:T(256)S(1)}, f32[256]{0:T(256)}, u32[]{:S(2)}) copy-start(f32[256]{0:T(256)} %param.28) | copy-start | bytes 3076
  62.1 25.2 %copy-start = (bf16[2,2,64,4096]{3,2,1,0:T(8,128)(2,1)S(1)}, bf16[2,2,64,4096]{3,2,1,0:T(8,128)(2,1)}, u32[]{:S(2)}) copy-start(bf16[2,2,64,4096]{3,2,1,0:T(8,128)(2,1)} %param.23) | copy-start | bytes 6291460
  62.1 20.4 %all-to-all-start.3 = ((bf16[64,8,128]{2,1,0:T(8,128)(2,1)}), bf16[64,8,128]{2,1,0:T(8,128)(2,1)S(1)}, u32[]{:S(2)}, u32[]{:S(2)}) async-start(bf16[64,8,128]{2,1,0:T(8,128)(2,1)} %columns.1), calls=%async_computation.3 | async-start | bytes 262144 | tf_op jit(solution)/shard_map/all_to_all | solution.py:25
  82.5 15.7 %all-to-all-start.2 = ((bf16[8,128,128]{2,1,0:T(8,128)(2,1)}), bf16[8,128,128]{2,1,0:T(8,128)(2,1)S(1)}, u32[]{:S(2)}, u32[]{:S(2)}) async-start(bf16[8,128,128]{2,1,0:T(8,128)(2,1)} %combine.1), calls=%async_computation.2 | async-start | bytes 524288 | tf_op jit(solution)/shard_map/all_to_all | solution.py:25
  101.2 16.1 %all-to-all-start.4 = ((bf16[64,8,128]{2,1,0:T(8,128)(2,1)}), bf16[64,8,128]{2,1,0:T(8,128)(2,1)S(1)}, u32[]{:S(2)}, u32[]{:S(2)}) async-start(bf16[64,8,128]{2,1,0:T(8,128)(2,1)} %decode.1), calls=%async_computation.4 | async-start | bytes 262144 | tf_op jit(solution)/shard_map/all_to_all | solution.py:25

commit v4 on v3

--- a/solution.py
+++ b/solution.py
@@ -106,7 +106,7 @@
         out_ref[g] = block_ref[g].astype(BF)
 
 
-def pack_kernel(near_ref, rates_ref, states_ref, out_ref, side_ref, sems):
+def pack_kernel(states_ref, out_ref, sems):
     moves = []
     for p in range(states_ref.shape[0]):
         moves.append(
@@ -115,6 +115,11 @@
             )
         )
         moves[-1].start()
+    for move in moves:
+        move.wait()
+
+
+def side_kernel(near_ref, rates_ref, packed_ref, out_ref, side_ref, sem):
     total = near_ref[0].astype(F32)
     for g in range(1, near_ref.shape[0]):
         total = total + near_ref[g].astype(F32)
@@ -123,11 +128,9 @@
     for c in range(out_ref.shape[0]):
         side_ref[c] = (rates_ref[c].astype(F32) + total).astype(BF)
     side = pltpu.make_async_copy(
-        side_ref, out_ref.at[:, STATE_ROWS : STATE_ROWS + SIDE_ROWS, :], sems.at[2]
+        side_ref, out_ref.at[:, STATE_ROWS : STATE_ROWS + SIDE_ROWS, :], sem
     )
     side.start()
-    for move in moves:
-        move.wait()
     side.wait()
 
 
@@ -292,15 +295,10 @@
 
 
 def decode_kernel(
-    place_ref, arrived_ref, ready_ref, c_parts_ref, w_out_hbm, out_ref, w_out_ref, tile_ref, load_sems, sems
+    place_ref, arrived_ref, ready_ref, c_parts_ref, w_out_hbm, out_ref, w_out_ref, tile_ref, load_sem, sems
 ):
-    loads = []
-    for n in range(out_ref.shape[0] // 16):
-        part = pl.ds(n * 1024, 1024)
-        loads.append(
-            pltpu.make_async_copy(w_out_hbm.at[:, part], w_out_ref.at[:, part], load_sems.at[n])
-        )
-        loads[-1].start()
+    load = pltpu.make_async_copy(w_out_hbm, w_out_ref, load_sem)
+    load.start()
     lane = lax.broadcasted_iota(jnp.int32, (8, LANES), 1)
     row = lax.broadcasted_iota(jnp.int32, (8, LANES), 0)
     low = lane < HALF
@@ -324,8 +322,8 @@
         jnp.where(lane == HALF + 1, parts[1], jnp.where(lane == HALF + 2, parts[2], 0.0)),
     )
     moves = []
+    load.wait()
     for n in range(out_ref.shape[0] // 16):
-        loads[n].wait()
         wide = jnp.dot(
             weighted, w_out_ref[:, n * 1024 : (n + 1) * 1024], preferred_element_type=F32
         )
@@ -420,25 +418,37 @@
     )
     near = exchange(near, "dp")
 
+    w_near = lax.all_gather(w_bcdt.T, "tp")
+
     rates = jnp.swapaxes(seg_rate[0].reshape(slots, n_ctx, heads), 0, 1)
     rates = jnp.stack(in_three(rates), axis=1).reshape(n_ctx, -1)
     rates = jnp.pad(rates, ((0, 0), (0, SIDE_ROWS - rates.shape[1])))
     rates = jnp.broadcast_to(rates[..., None], (n_ctx, SIDE_ROWS, width))
+    packed = pl.pallas_call(
+        pack_kernel,
+        out_shape=pltpu.HBM((n_ctx, STATE_ROWS + SIDE_ROWS, width), BF),
+        in_specs=[HB],
+        out_specs=HB,
+        scratch_shapes=[pltpu.SemaphoreType.DMA((slots,))],
+        compiler_params=PARAMS,
+        name="pack",
+    )(in_hbm(state_parts.reshape(slots, n_ctx, ONE_STATE, width)))
+    w_near, packed, rates = lax.optimization_barrier((w_near, packed, rates))
     sent = pl.pallas_call(
-        pack_kernel,
-        out_shape=jax.ShapeDtypeStruct((n_ctx, STATE_ROWS + SIDE_ROWS, width), BF),
+        side_kernel,
+        out_shape=pltpu.HBM((n_ctx, STATE_ROWS + SIDE_ROWS, width), BF),
         in_specs=[VM, VM, HB],
         out_specs=HB,
         scratch_shapes=[
             pltpu.VMEM((n_ctx, SIDE_ROWS, width), BF),
-            pltpu.SemaphoreType.DMA((3,)),
+            pltpu.SemaphoreType.DMA(()),
         ],
-        compiler_params=PARAMS,
-        name="pack",
-    )(near, rates, state_parts.reshape(slots, n_ctx, ONE_STATE, width))
+        input_output_aliases={2: 0},
+        compiler_params=PARAMS,
+        name="side",
+    )(near, rates, in_hbm(packed))
     got = exchange(sent, "ctx")
 
-    w_near = lax.all_gather(w_bcdt.T, "tp")
     own_columns = n_tp * w_bcdt.shape[1]
     w_near = w_near.reshape(own_columns, 2, n_ctx // 2, n_tp, features)
     w_near = lax.dynamic_index_in_dim(w_near, tp, 3, keepdims=False)
@@ -533,7 +543,7 @@
         scratch_shapes=[
             pltpu.VMEM((channels, model), BF),
             pltpu.VMEM((peers, rows, LANES), BF),
-            pltpu.SemaphoreType.DMA((peers // 16,)),
+            pltpu.SemaphoreType.DMA(()),
             pltpu.SemaphoreType.DMA((peers // 16,)),
         ],
         compiler_params=PARAMS,

time: 119 us -> 154 us (1.29)
  Pallas kernels: 11.6 us -> 43.7 us
  blocking collectives: 28 us -> 8.21 us
  waiting for transfers between devices: 29.4 us -> 45.8 us
  starting transfers between devices: 39.5 us -> 45.9 us
    pallas_call x1 -> x2, Pallas kernels: 1.05 us -> 33.6 us  [the longest x1 32.9 us: per_device(): pl.pallas_call(pack_kernel, out_shape=pltpu.HBM((n_ctx, STATE_ROWS + SIDE...]
    all_gather x1, blocking collectives: 28 us -> 8.21 us  [per_device(): w_near = lax.all_gather(w_bcdt.T, 'tp')]
    all_to_all x5, waiting for transfers between devices: 29.4 us -> 45.8 us  [exchange(): return lax.all_to_all(pieces, axis, 0, 0, tiled=True)]
    all_to_all x5, starting transfers between devices: 39.5 us -> 45.9 us  [exchange(): return lax.all_to_all(pieces, axis, 0, 0, tiled=True)]
  transfers between devices with their start and end apart: 5 -> 5, of which waited for: 4 -> 4; matrix products, arithmetic and copies ran while one was open for 4% -> 3% of each run, Pallas kernels for 3% -> 23%
where the time goes in v4:
time: 154 us; the launch traced here: 153 us
  starting transfers between devices  45.9 us (30%)
  waiting for transfers between devices  45.8 us (30%)
  Pallas kernels  43.7 us (28%)
  blocking collectives  8.21 us (5%)
  between operations  4.8 us (3%)
  local copies, waits for them, and re-layouts  3.61 us (2%)
    all_to_all x5, starting transfers between devices, exchange(): return lax.all_to_all(pieces, axis, 0, 0, tiled=True)  45.9 us
    all_to_all x5, waiting for transfers between devices, exchange(): return lax.all_to_all(pieces, axis, 0, 0, tiled=True)  45.8 us
    pallas_call x1, Pallas kernels, per_device(): pl.pallas_call(pack_kernel, out_shape=pltpu.HBM((n_ctx, STATE_ROWS + SIDE...  32.9 us
    all_gather x1, blocking collectives, per_device(): w_near = lax.all_gather(w_bcdt.T, 'tp')  8.21 us
  transfers between devices with their start and end apart: 5, of which 4 were waited for; matrix products, arithmetic and copies ran while one was open for 3% of the time, Pallas kernels for 23%

profile of v4, /device:TPU:1, one launch (start us, length us, event | category | flops | bytes accessed | tf_op | source)
XLA Modules:
  0.0 153.5 jit_solution(7647439205477803438)
XLA Ops:
  0.6 2.6 %lookup.1 = bf16[8,16,128]{2,1,0:T(8,128)(2,1)} custom-call(s32[4,16]{1,0:T(4,128)} %tokens_hbm.1, s32[16]{0:T(128)} %prompt_hbm.1, bf16[64,6285]{1,0:T(8,128)(2,1)} %bitcast.57, bf16[2,3,2,64]{3,2,1,0:T(2,128)(2,1)} %x_tail_hbm.1, bf16[3,2,256]{2,1,0:T(2,128)(2,1)} %bitcast.64), custom_call_target="tpu_custom_call" | custom-call | tf_op jit(solution)/shard_map/lookup/pallas_call | solution.py:395
  3.3 7.7 %all-to-all-start = ((bf16[8,16,128]{2,1,0:T(8,128)(2,1)}), bf16[8,16,128]{2,1,0:T(8,128)(2,1)S(1)}, u32[]{:S(2)}, u32[]{:S(2)}) async-start(bf16[8,16,128]{2,1,0:T(8,128)(2,1)} %lookup.1), calls=%async_computation | async-start | bytes 65536 | tf_op jit(solution)/shard_map/all_to_all | solution.py:25
  10.9 0.8 reshape_squeeze.3
  11.9 32.9 %pack.1.packed_ref = bf16[16,272,128]{2,1,0:T(8,128)(2,1)} custom-call(bf16[2,16,128,128]{3,2,1,0:T(8,128)(2,1)} %bitcast.55), custom_call_target="tpu_custom_call" | custom-call | tf_op jit(solution)/shard_map/pack/pallas_call | solution.py:427
  44.8 8.2 %all-gather.1 = bf16[4,6,4096]{2,1,0:T(8,128)(2,1)S(1)} all-gather(bf16[1,6,4096]{2,1,0:T(8,128)(2,1)S(1)} %bitcast.60), channel_id=2, replica_groups=mesh['ctx'=16,'dp'=8,'tp'=4] {'tp'}, dimensions={0}, use_global_device_ids=true | all-gather | bytes 245760 | tf_op jit(solution)/shard_map/all_gather | solution.py:421
  53.2 0.7 side.1
  53.9 11.0 %all-to-all-start.1 = ((bf16[16,272,128]{2,1,0:T(8,128)(2,1)}), bf16[16,272,128]{2,1,0:T(8,128)(2,1)S(1)}, u32[]{:S(2)}, u32[]{:S(2)}) async-start(bf16[16,272,128]{2,1,0:T(8,128)(2,1)} %side.1), calls=%async_computation.1 | async-start | bytes 2228224 | tf_op jit(solution)/shard_map/all_to_all | solution.py:25
  64.9 0.4 reshape.78
  65.3 0.2 constant_dynamic-slice_fusion.2
  65.6 0.1 reshape.79
  66.1 23.8 %all-to-all-done.1.got_ref = bf16[16,272,128]{2,1,0:T(8,128)(2,1)S(1)} async-done(((bf16[16,272,128]{2,1,0:T(8,128)(2,1)}), bf16[16,272,128]{2,1,0:T(8,128)(2,1)S(1)}, u32[]{:S(2)}, u32[]{:S(2)}) %all-to-all-start.1) | async-done | bytes 1114144 | tf_op jit(solution)/shard_map/all_to_all | solution.py:25
  89.9 1.0 columns.1
  91.0 11.8 %all-to-all-start.3 = ((bf16[64,8,128]{2,1,0:T(8,128)(2,1)}), bf16[64,8,128]{2,1,0:T(8,128)(2,1)S(1)}, u32[]{:S(2)}, u32[]{:S(2)}) async-start(bf16[64,8,128]{2,1,0:T(8,128)(2,1)} %columns.1), calls=%async_computation.3 | async-start | bytes 262144 | tf_op jit(solution)/shard_map/all_to_all | solution.py:25
  102.8 0.6 fusion.12
  108.2 1.6 %combine.1 = bf16[8,128,128]{2,1,0:T(8,128)(2,1)} custom-call(s32[8]{0:T(128)S(1)} %convert_element_type.27.chosen_ref, bf16[16,272,128]{2,1,0:T(8,128)(2,1)S(1)} %all-to-all-done.1.got_ref), custom_call_target="tpu_custom_call" | custom-call | tf_op jit(solution)/shard_map/combine/pallas_call | solution.py:500
  109.8 3.3 %all-to-all-done.3.everyone_ref = bf16[64,8,128]{2,1,0:T(8,128)(2,1)S(1)} async-done(((bf16[64,8,128]{2,1,0:T(8,128)(2,1)}), bf16[64,8,128]{2,1,0:T(8,128)(2,1)S(1)}, u32[]{:S(2)}, u32[]{:S(2)}) %all-to-all-start.3) | async-done | bytes 131104 | tf_op jit(solution)/shard_map/all_to_all | solution.py:25
  113.1 6.9 %all-to-all-start.2 = ((bf16[8,128,128]{2,1,0:T(8,128)(2,1)}), bf16[8,128,128]{2,1,0:T(8,128)(2,1)S(1)}, u32[]{:S(2)}, u32[]{:S(2)}) async-start(bf16[8,128,128]{2,1,0:T(8,128)(2,1)} %combine.1), calls=%async_computation.2 | async-start | bytes 524288 | tf_op jit(solution)/shard_map/all_to_all | solution.py:25
  120.2 1.3 project.1
  121.6 9.4 %all-to-all-done.2.arrived_ref = bf16[8,128,128]{2,1,0:T(8,128)(2,1)S(1)} async-done(((bf16[8,128,128]{2,1,0:T(8,128)(2,1)}), bf16[8,128,128]{2,1,0:T(8,128)(2,1)S(1)}, u32[]{:S(2)}, u32[]{:S(2)}) %all-to-all-start.2) | async-done | bytes 262176 | tf_op jit(solution)/shard_map/all_to_all | solution.py:25
  131.0 2.7 %decode.1 = bf16[64,8,128]{2,1,0:T(8,128)(2,1)} custom-call(s32[3]{0:T(128)S(1)} %pad_add_fusion.place_ref, bf16[8,128,128]{2,1,0:T(8,128)(2,1)S(1)} %all-to-all-done.2.arrived_ref, f32[32,128]{1,0:T(8,128)S(1)} %get-tuple-element.15.ready_ref, bf16[32,128]{1,0:T(8,128)(2,1)S(1)} %get-tuple-element.16.c_parts_ref, bf16[128,4096]{1,0:T(8,128)(2,1)} %bitcast.56), custom_call_target="tpu_custom_call" | custom-call | tf_op jit(solution)/shard_map/decode/pallas_call | solution.py:538
  133.8 8.5 %all-to-all-start.4 = ((bf16[64,8,128]{2,1,0:T(8,128)(2,1)}), bf16[64,8,128]{2,1,0:T(8,128)(2,1)S(1)}, u32[]{:S(2)}, u32[]{:S(2)}) async-start(bf16[64,8,128]{2,1,0:T(8,128)(2,1)} %decode.1), calls=%async_computation.4 | async-start | bytes 262144 | tf_op jit(solution)/shard_map/all_to_all | solution.py:25
  142.3 1.1 convolution_add_fusion
  143.4 9.3 %all-to-all-done.4.incoming_ref = bf16[64,8,128]{2,1,0:T(8,128)(2,1)S(1)} async-done(((bf16[64,8,128]{2,1,0:T(8,128)(2,1)}), bf16[64,8,128]{2,1,0:T(8,128)(2,1)S(1)}, u32[]{:S(2)}, u32[]{:S(2)}) %all-to-all-start.4) | async-done | bytes 131104 | tf_op jit(solution)/shard_map/all_to_all | solution.py:25
  152.7 0.8 finish.1
  (61 shorter events, 1.9 us)
Async XLA Ops:
  3.3 49.9 %all-to-all-start = ((bf16[8,16,128]{2,1,0:T(8,128)(2,1)}), bf16[8,16,128]{2,1,0:T(8,128)(2,1)S(1)}, u32[]{:S(2)}, u32[]{:S(2)}) async-start(bf16[8,16,128]{2,1,0:T(8,128)(2,1)} %lookup.1), calls=%async_computation | async-start | bytes 65536 | tf_op jit(solution)/shard_map/all_to_all | solution.py:25
  11.7 33.2 %copy-start.2 = (bf16[4096,6]{0,1:T(8,128)(2,1)S(1)}, bf16[4096,6]{0,1:T(8,128)(2,1)}, u32[]{:S(2)}) copy-start(bf16[4096,6]{0,1:T(8,128)(2,1)} %param.24) | copy-start | bytes 147460
  53.9 36.1 %all-to-all-start.1 = ((bf16[16,272,128]{2,1,0:T(8,128)(2,1)}), bf16[16,272,128]{2,1,0:T(8,128)(2,1)S(1)}, u32[]{:S(2)}, u32[]{:S(2)}) async-start(bf16[16,272,128]{2,1,0:T(8,128)(2,1)} %side.1), calls=%async_computation.1 | async-start | bytes 2228224 | tf_op jit(solution)/shard_map/all_to_all | solution.py:25
  64.9 0.9 copy-start.1
  64.9 1.1 copy-start.6
  65.8 40.3 %copy-start.3 = (f32[4,2,64]{2,1,0:T(2,128)S(1)}, f32[4,2,64]{2,1,0:T(2,128)}, u32[]{:S(2)}) copy-start(f32[4,2,64]{2,1,0:T(2,128)} %param.25) | copy-start | bytes 6148
  65.9 40.4 %copy-start.9 = (f32[2]{0:T(128)S(1)}, f32[2]{0:T(128)}, u32[]{:S(2)}) copy-start(f32[2]{0:T(128)} %param.29) | copy-start | bytes 28
  65.9 40.5 %copy-start.10 = (f32[2]{0:T(128)S(1)}, f32[2]{0:T(128)}, u32[]{:S(2)}) copy-start(f32[2]{0:T(128)} %param.30) | copy-start | bytes 28
  65.9 40.7 %copy-start.11 = (f32[2]{0:T(128)S(1)}, f32[2]{0:T(128)}, u32[]{:S(2)}) copy-start(f32[2]{0:T(128)} %param.31) | copy-start | bytes 28
  65.9 40.8 %copy-start.7 = (f32[2,64]{1,0:T(2,128)S(1)}, f32[2,64]{1,0:T(2,128)}, u32[]{:S(2)}) copy-start(f32[2,64]{1,0:T(2,128)} %param.26) | copy-start | bytes 1540
  65.9 40.9 %copy-start.8 = (f32[2,64]{1,0:T(2,128)S(1)}, f32[2,64]{1,0:T(2,128)}, u32[]{:S(2)}) copy-start(f32[2,64]{1,0:T(2,128)} %param.32) | copy-start | bytes 1540
  90.9 29.1 %copy-start.4 = (f32[4,256]{1,0:T(4,128)S(1)}, f32[4,256]{1,0:T(4,128)}, u32[]{:S(2)}) copy-start(f32[4,256]{1,0:T(4,128)} %param.27) | copy-start | bytes 12292
  90.9 29.1 %copy-start.5 = (f32[256]{0:T(256)S(1)}, f32[256]{0:T(256)}, u32[]{:S(2)}) copy-start(f32[256]{0:T(256)} %param.28) | copy-start | bytes 3076
  91.0 29.3 %copy-start = (bf16[2,2,64,4096]{3,2,1,0:T(8,128)(2,1)S(1)}, bf16[2,2,64,4096]{3,2,1,0:T(8,128)(2,1)}, u32[]{:S(2)}) copy-start(bf16[2,2,64,4096]{3,2,1,0:T(8,128)(2,1)} %param.23) | copy-start | bytes 6291460
  91.0 22.2 %all-to-all-start.3 = ((bf16[64,8,128]{2,1,0:T(8,128)(2,1)}), bf16[64,8,128]{2,1,0:T(8,128)(2,1)S(1)}, u32[]{:S(2)}, u32[]{:S(2)}) async-start(bf16[64,8,128]{2,1,0:T(8,128)(2,1)} %columns.1), calls=%async_computation.3 | async-start | bytes 262144 | tf_op jit(solution)/shard_map/all_to_all | solution.py:25
  113.1 17.9 %all-to-all-start.2 = ((bf16[8,128,128]{2,1,0:T(8,128)(2,1)}), bf16[8,128,128]{2,1,0:T(8,128)(2,1)S(1)}, u32[]{:S(2)}, u32[]{:S(2)}) async-start(bf16[8,128,128]{2,1,0:T(8,128)(2,1)} %combine.1), calls=%async_computation.2 | async-start | bytes 524288 | tf_op jit(solution)/shard_map/all_to_all | solution.py:25
  133.8 18.9 %all-to-all-start.4 = ((bf16[64,8,128]{2,1,0:T(8,128)(2,1)}), bf16[64,8,128]{2,1,0:T(8,128)(2,1)S(1)}, u32[]{:S(2)}, u32[]{:S(2)}) async-start(bf16[64,8,128]{2,1,0:T(8,128)(2,1)} %decode.1), calls=%async_computation.4 | async-start | bytes 262144 | tf_op jit(solution)/shard_map/all_to_all | solution.py:25

commit v5 on v2

--- a/solution.py
+++ b/solution.py
@@ -1,5 +1,3 @@
-import functools
-
 import jax
 import jax.numpy as jnp
 from jax import lax
@@ -15,11 +13,12 @@
 F32 = jnp.float32
 LANES = 128
 HALF = 64
-VMEM_LIMIT = 48 * 1024 * 1024
+VMEM_LIMIT = 24 * 1024 * 1024
 
 STATE_ROWS = 256
 RATE_ROWS = 16
 TOKEN_ROWS = 32
+SIDE_ROWS = RATE_ROWS + TOKEN_ROWS
 ONE_STATE = 128
 TAIL_ROWS = 16
 NEAR_ROWS = 64
@@ -45,9 +44,92 @@
     return lax.broadcasted_iota(jnp.int32, shape, 1) < HALF
 
 
-def combine_kernel(chosen_ref, got_ref, tails_ref, out_ref, combined_ref):
+def send_kernel(
+    tokens_hbm, prompt_hbm, rate_hbm, table_hbm, states_hbm, out_ref,
+    tokens_ref, prompt_ref, rate_ref, table_ref, states_ref, token_ref, rows_ref, block_ref, side_ref, sems,
+):
+    pairs = [
+        (tokens_hbm, tokens_ref),
+        (prompt_hbm, prompt_ref),
+        (rate_hbm, rate_ref),
+        (table_hbm, table_ref),
+        (states_hbm, states_ref),
+    ]
+    loads = [pltpu.make_async_copy(a, b, sems.at[n]) for n, (a, b) in enumerate(pairs)]
+    for load in loads:
+        load.start()
+    group = lax.axis_index("dp")
+    count = out_ref.shape[0]
+    slots = states_ref.shape[0]
+    heads = rate_ref.shape[1] // count
+    steps = tokens_ref.shape[0]
+    rows = steps * slots
+    groups = prompt_ref.shape[0] // slots
+    vocab_rows = table_ref.shape[1]
+    first = group * vocab_rows
+    loads[0].wait()
+    loads[1].wait()
+    for g in range(groups):
+        for step in range(steps):
+            for slot in range(slots):
+                token = tokens_ref[step, prompt_ref[g * slots + slot]] - first
+                at = g * rows + step * slots + slot
+                token_ref[at : at + 1, :] = jnp.full((1, LANES), token, jnp.int32)
+    loads[2].wait()
+    for c in range(count):
+        for p in range(slots):
+            for h in range(heads):
+                at = (c * slots + p) * heads + h
+                rows_ref[at : at + 1, :] = jnp.full((1, LANES), rate_ref[p, c * heads + h], F32)
+    each = slots * heads
+    parts = [p.astype(F32) for p in in_three(rows_ref[...])]
+    for c in range(count):
+        for n, part in enumerate(parts):
+            block_ref[c, n * each : (n + 1) * each, :] = part[c * each : (c + 1) * each]
+        block_ref[c, 3 * each : RATE_ROWS, :] = jnp.zeros((RATE_ROWS - 3 * each, LANES), F32)
+        side_ref[c, 0:RATE_ROWS, :] = block_ref[c].astype(BF)
+    loads[4].wait()
+    stores = []
+    for p in range(slots):
+        stores.append(
+            pltpu.make_async_copy(
+                states_ref.at[p], out_ref.at[:, p * ONE_STATE : (p + 1) * ONE_STATE, :], sems.at[5 + p]
+            )
+        )
+        stores[-1].start()
+    loads[3].wait()
+    tokens = token_ref[:, 0:1]
+    found = jnp.zeros((groups * rows, LANES), F32)
+    whole = vocab_rows // LANES * LANES
+    bounds = [*range(0, whole, 1024), whole, vocab_rows]
+    for low_at, high_at in zip(bounds[:-1], bounds[1:]):
+        ids = lax.broadcasted_iota(jnp.int32, (groups * rows, high_at - low_at), 1) + low_at
+        hot = jnp.where(tokens == ids, 1.0, 0.0).astype(BF)
+        table = table_ref[:, low_at:high_at]
+        found = found + lax.dot_general(
+            hot,
+            jnp.concatenate([table, table], axis=0),
+            (((1,), (1,)), ((), ())),
+            preferred_element_type=F32,
+        )
+    low = low_half((TOKEN_ROWS, LANES))
+    tile = jnp.where(low, found[0:TOKEN_ROWS], found[TOKEN_ROWS : 2 * TOKEN_ROWS]).astype(BF)
+    for c in range(count):
+        side_ref[c, RATE_ROWS:SIDE_ROWS, :] = tile
+    stores.append(
+        pltpu.make_async_copy(
+            side_ref, out_ref.at[:, STATE_ROWS : STATE_ROWS + SIDE_ROWS, :], sems.at[5 + slots]
+        )
+    )
+    stores[-1].start()
+    for store in stores:
+        store.wait()
+
+
+def combine_kernel(chosen_ref, got_ref, tails_ref, out_ref, bundle_ref, near_ref, sems):
     count = got_ref.shape[0]
     groups = out_ref.shape[0]
+    own_rows = ONE_STATE + TAIL_ROWS
     rates = []
     for k in range(count):
         parts = got_ref[k, STATE_ROWS : STATE_ROWS + RATE_ROWS, :].astype(F32)
@@ -63,11 +145,17 @@
             own = got_ref[k, part * HEAD_DIM : (part + 1) * HEAD_DIM, :].astype(F32)
             total = total + (own * weights[k][part : part + 1]).astype(BF).astype(F32)
         at = (part % 2) * HEAD_DIM
-        combined_ref[part // 2, at : at + HEAD_DIM, :] = total.astype(BF)
-    for g in range(groups):
-        prompt = chosen_ref[g]
-        out_ref[g, 0:ONE_STATE, :] = combined_ref[prompt]
-        out_ref[g, ONE_STATE : ONE_STATE + TAIL_ROWS, :] = tails_ref[prompt]
+        bundle_ref[part // 2, at : at + HEAD_DIM, :] = total.astype(BF)
+    for p in range(bundle_ref.shape[0]):
+        bundle_ref[p, ONE_STATE:own_rows, :] = tails_ref[p]
+    moves = [
+        pltpu.make_async_copy(
+            bundle_ref.at[chosen_ref[g]], out_ref.at[g, 0:own_rows, :], sems.at[g]
+        )
+        for g in range(groups)
+    ]
+    for move in moves:
+        move.start()
     low = low_half((TOKEN_ROWS, LANES))
     at = STATE_ROWS + RATE_ROWS
     for pair in range(0, count // 2, 2):
@@ -81,11 +169,18 @@
             source = early if g < groups // 2 else late
             r = (g % (groups // 2)) * 8
             both = jnp.concatenate([s[r : r + 8] for s in source], axis=0)
-            start = ONE_STATE + TAIL_ROWS + pair * 8
-            out_ref[g, start : start + 16, :] = both.astype(BF)
-
-
-def columns_kernel(place_ref, arrived_ref, gain_ref, weight_ref, out_ref, near_ref):
+            near_ref[g, pair * 8 : pair * 8 + 16, :] = both.astype(BF)
+    moves.append(
+        pltpu.make_async_copy(
+            near_ref, out_ref.at[:, own_rows : own_rows + NEAR_ROWS, :], sems.at[groups]
+        )
+    )
+    moves[-1].start()
+    for move in moves:
+        move.wait()
+
+
+def columns_kernel(place_ref, arrived_ref, gain_ref, weight_ref, out_ref, near_ref, tile_ref, sem):
     groups = arrived_ref.shape[0]
     at = ONE_STATE + TAIL_ROWS
     total = arrived_ref[0, at : at + NEAR_ROWS, :].astype(F32)
@@ -104,30 +199,17 @@
     lane = lax.broadcasted_iota(jnp.int32, (8, LANES), 1)
     first = partial.astype(BF).astype(F32)
     tile = jnp.where(lane < HALF, own, jnp.where(lane < HALF + 24, first, partial - first))
-    out_ref[...] = jnp.broadcast_to(tile.astype(BF)[None], out_ref.shape)
+    tile_ref[...] = jnp.broadcast_to(tile.astype(BF)[None], tile_ref.shape)
+    move = pltpu.make_async_copy(tile_ref, out_ref, sem)
+    move.start()
+    move.wait()
 
 
 def decode_kernel(
-    place_ref,
-    everyone_ref,
-    arrived_ref,
-    gain_ref,
-    small_ref,
-    w_zx_ref,
-    w_out_ref,
-    out_ref,
-    start_ref,
-    extra_ref,
-    zx_ref,
-    wo_ref,
-    x_ref,
-    b_ref,
-    c_ref,
-    sems,
+    place_ref, everyone_ref, arrived_ref, gain_ref, small_ref, zx_ref, w_out_hbm, out_ref, extra_ref,
+    wo_ref, x_ref, b_ref, c_ref, tile_ref, load_sem, sems,
 ):
-    load_zx = pltpu.make_async_copy(w_zx_ref, zx_ref, sems.at[0])
-    load_zx.start()
-    load_out = pltpu.make_async_copy(w_out_ref, wo_ref, sems.at[1])
+    load_out = pltpu.make_async_copy(w_out_hbm, wo_ref, load_sem)
     load_out.start()
     peers = everyone_ref.shape[0]
     model = peers * HALF
@@ -196,14 +278,12 @@
     from_start = []
     for slot in range(2):
         state = arrived_ref[place_ref[slot], 0:ONE_STATE, :]
-        start_ref[slot] = state
         product = lax.dot_general(
             c_parts, state, (((1,), (1,)), ((), ())), preferred_element_type=F32
         )
         from_start.append(product[0:8] + product[8:16] + product[16:24])
     y = jnp.exp(log_total) * jnp.where(row % 2 == 0, from_start[0], from_start[1])
 
-    load_zx.wait()
     projected = lax.dot_general(
         normed, zx_ref[...], (((1,), (1,)), ((), ())), preferred_element_type=F32
     )
@@ -235,14 +315,20 @@
     extra_ref[16:24, :] = jnp.exp(last)
 
     load_out.wait()
-    for n in range(peers // 8):
+    moves = []
+    for n in range(peers // 16):
         wide = jnp.dot(
-            weighted, wo_ref[:, n * 512 : (n + 1) * 512], preferred_element_type=F32
-        )
-        for m in range(4):
+            weighted, wo_ref[:, n * 1024 : (n + 1) * 1024], preferred_element_type=F32
+        )
+        for m in range(8):
             piece = wide[:, m * LANES : (m + 1) * LANES]
-            out_ref[8 * n + 2 * m] = jnp.where(low, piece, aside).astype(BF)
-            out_ref[8 * n + 2 * m + 1] = jnp.where(low, pltpu.roll(piece, HALF, 1), aside).astype(BF)
+            tile_ref[16 * n + 2 * m] = jnp.where(low, piece, aside).astype(BF)
+            tile_ref[16 * n + 2 * m + 1] = jnp.where(low, pltpu.roll(piece, HALF, 1), aside).astype(BF)
+        part = pl.ds(16 * n, 16)
+        moves.append(pltpu.make_async_copy(tile_ref.at[part], out_ref.at[part], sems.at[n]))
+        moves[-1].start()
+    for move in moves:
+        move.wait()
 
 
 def finish_kernel(incoming_ref, out_ref):
@@ -256,7 +342,13 @@
 
 VM = pl.BlockSpec(memory_space=pltpu.VMEM)
 SM = pl.BlockSpec(memory_space=pltpu.SMEM)
-HB = pl.BlockSpec(memory_space=pl.ANY)
+HB = pl.BlockSpec(memory_space=pltpu.HBM)
+
+
+def in_hbm(array):
+    return pltpu.with_memory_space_constraint(array, pltpu.HBM)
+
+
 PARAMS = pltpu.CompilerParams(vmem_limit_bytes=VMEM_LIMIT)
 
 
@@ -293,22 +385,31 @@
     rows = steps * slots
     channels = heads * HEAD_DIM
 
-    prompts = decode_prompt.shape[0]
-    chosen = (decode_prompt[:, None] == jnp.arange(prompts)[None, :]).astype(jnp.int32)
-    tokens = jnp.sum(token_ids[:, None, :] * chosen[None], axis=2)
-    tokens = jnp.swapaxes(tokens.reshape(steps, n_dp, slots), 0, 1).reshape(-1)
-    hot = (tokens[:, None] - group * vocab_rows == jnp.arange(vocab_rows)[None, :]).astype(BF)
-    found = jnp.dot(hot, embedding, preferred_element_type=F32).astype(BF)
-    found = jnp.concatenate([found[:TOKEN_ROWS], found[TOKEN_ROWS:]], axis=1)
-
-    states = state_parts[0].reshape(slots, n_ctx, heads, HEAD_DIM, width)
-    states = jnp.swapaxes(states, 0, 1).reshape(n_ctx, STATE_ROWS, width)
-    rates = jnp.swapaxes(seg_rate[0].reshape(slots, n_ctx, heads), 0, 1)
-    rates = jnp.stack(in_three(rates), axis=1).reshape(n_ctx, -1)
-    rates = jnp.pad(rates, ((0, 0), (0, RATE_ROWS - rates.shape[1])))
-    rates = jnp.broadcast_to(rates[..., None], (n_ctx, RATE_ROWS, width))
-    sent = jnp.concatenate(
-        [states, rates, jnp.broadcast_to(found[None], (n_ctx, *found.shape))], axis=1
+    sent = pl.pallas_call(
+        send_kernel,
+        out_shape=jax.ShapeDtypeStruct((n_ctx, STATE_ROWS + SIDE_ROWS, width), BF),
+        in_specs=[HB] * 5,
+        out_specs=HB,
+        scratch_shapes=[
+            pltpu.SMEM(token_ids.shape, jnp.int32),
+            pltpu.SMEM(decode_prompt.shape, jnp.int32),
+            pltpu.SMEM(seg_rate.shape[1:], F32),
+            pltpu.VMEM((features, vocab_rows), BF),
+            pltpu.VMEM((slots, n_ctx, ONE_STATE, width), BF),
+            pltpu.VMEM((n_dp * rows, LANES), jnp.int32),
+            pltpu.VMEM((n_ctx * slots * heads, LANES), F32),
+            pltpu.VMEM((n_ctx, RATE_ROWS, LANES), F32),
+            pltpu.VMEM((n_ctx, SIDE_ROWS, LANES), BF),
+            pltpu.SemaphoreType.DMA((6 + slots,)),
+        ],
+        compiler_params=PARAMS,
+        name="send",
+    )(
+        in_hbm(token_ids),
+        in_hbm(decode_prompt),
+        in_hbm(seg_rate[0]),
+        in_hbm(embedding.T),
+        in_hbm(state_parts.reshape(slots, n_ctx, ONE_STATE, width)),
     )
     got = exchange(sent, "ctx")
 
@@ -327,7 +428,10 @@
     wanted = decode_prompt.reshape(n_dp, slots) - group * slots
     prompt_for = jnp.any(wanted == 1, axis=1).astype(jnp.int32)
     own_slots = lax.dynamic_slice_in_dim(decode_prompt, group * slots, slots)
-    spread = functools.partial(jnp.repeat, repeats=HEAD_DIM, total_repeat_length=channels)
+
+    def spread(values):
+        return jnp.broadcast_to(values[:, None], (heads, HEAD_DIM)).reshape(1, channels)
+
     small = jnp.concatenate(
         [
             conv_x_weight.reshape(4, channels),
@@ -335,21 +439,26 @@
             conv_bc_weight[:, width:],
             conv_x_bias.reshape(1, channels),
             conv_bc_bias.reshape(2, width),
-            spread(dt_bias)[None],
-            spread(a_log)[None],
-            spread(d_skip)[None],
+            spread(dt_bias),
+            spread(a_log),
+            spread(d_skip),
             gate_norm_gain.reshape(1, channels),
         ],
         axis=0,
     )
     small = jnp.pad(small, ((0, -small.shape[0] % 8), (0, 0)))
 
+    got, w_near, near_gain = lax.optimization_barrier((got, w_near, near_gain))
     routed = pl.pallas_call(
         combine_kernel,
         out_shape=jax.ShapeDtypeStruct((n_dp, ONE_STATE + TAIL_ROWS + NEAR_ROWS, width), BF),
         in_specs=[SM, VM, VM],
-        out_specs=VM,
-        scratch_shapes=[pltpu.VMEM((slots, ONE_STATE, width), BF)],
+        out_specs=HB,
+        scratch_shapes=[
+            pltpu.VMEM((slots, ONE_STATE + TAIL_ROWS, width), BF),
+            pltpu.VMEM((n_dp, NEAR_ROWS, width), BF),
+            pltpu.SemaphoreType.DMA((n_dp + 1,)),
+        ],
         compiler_params=PARAMS,
         name="combine",
     )(prompt_for, got, tails)
@@ -360,8 +469,12 @@
         columns_kernel,
         out_shape=jax.ShapeDtypeStruct((peers, rows, LANES), BF),
         in_specs=[SM, VM, VM, VM],
-        out_specs=VM,
-        scratch_shapes=[pltpu.VMEM((NEAR_ROWS // 8, 8, LANES), F32)],
+        out_specs=HB,
+        scratch_shapes=[
+            pltpu.VMEM((NEAR_ROWS // 8, 8, LANES), F32),
+            pltpu.VMEM((peers, rows, LANES), BF),
+            pltpu.SemaphoreType.DMA(()),
+        ],
         compiler_params=PARAMS,
         name="columns",
     )(place, arrived, near_gain, w_near)
@@ -371,22 +484,22 @@
     place = jnp.concatenate(
         [own_slots // slots, ((LANES - head_at) % LANES)[None]]
     ).astype(jnp.int32)
-    outgoing, start, extra = pl.pallas_call(
+    outgoing, extra = pl.pallas_call(
         decode_kernel,
         out_shape=(
             jax.ShapeDtypeStruct((peers, rows, LANES), BF),
-            jax.ShapeDtypeStruct((slots, ONE_STATE, width), BF),
             jax.ShapeDtypeStruct((24, LANES), F32),
         ),
-        in_specs=[SM, VM, VM, VM, VM, HB, HB],
-        out_specs=(VM, VM, VM),
+        in_specs=[SM, VM, VM, VM, VM, VM, HB],
+        out_specs=(HB, VM),
         scratch_shapes=[
-            pltpu.VMEM((2 * channels, model), BF),
             pltpu.VMEM((channels, model), BF),
             pltpu.VMEM((16, LANES), F32),
             pltpu.VMEM((16, LANES), F32),
             pltpu.VMEM((16, LANES), F32),
-            pltpu.SemaphoreType.DMA((2,)),
+            pltpu.VMEM((peers, rows, LANES), BF),
+            pltpu.SemaphoreType.DMA(()),
+            pltpu.SemaphoreType.DMA((peers // 16,)),
         ],
         compiler_params=PARAMS,
         name="decode",
@@ -397,10 +510,16 @@
         norm_gain.reshape(model // LANES, LANES),
         small,
         w_zx.reshape(2 * channels, model),
-        w_out.reshape(channels, model),
+        in_hbm(w_out.reshape(channels, model)),
     )
     incoming = exchange(outgoing, BOTH)
 
+    start = jnp.stack(
+        [
+            lax.dynamic_index_in_dim(arrived[:, :ONE_STATE], place[s], 0, keepdims=False)
+            for s in range(slots)
+        ]
+    )
     push = extra[0:8].reshape(steps, slots, channels)
     b_conv = extra[8:16].reshape(steps, slots, width)
     kept = extra[16:18]

time: 124 us -> 117 us (0.944)
  local copies, waits for them, and re-layouts: 14.5 us -> 2.76 us
  other arithmetic: 8.27 us -> 0.4 us
  Pallas kernels: 5.04 us -> 10.9 us
  waiting for transfers between devices: 19.9 us -> 25.1 us
  between operations: 1.05 us -> 4.91 us
  starting transfers between devices: 42.4 us -> 41.1 us
    unnamed x48 -> x30, local copies, waits for them, and re-layouts: 6.22 us -> 0.11 us
    all_to_all x4, waiting for transfers between devices: 19.9 us -> 25.1 us  [exchange(): return lax.all_to_all(pieces, axis, 0, 0, tiled=True)]
    broadcast_in_dim x1 -> x0, other arithmetic: 3.84 us -> none  [per_device(): spread(d_skip)[None]]
    pallas_call x0 -> x1, Pallas kernels: none -> 3.03 us  [per_device(): pl.pallas_call(send_kernel, out_shape=jax.ShapeDtypeStruct((n_ctx, STATE_...]
    gather x3 -> x0, local copies, waits for them, and re-layouts: 1.8 us -> none  [the longest x1 0.62 us: per_device(): spread(dt_bias)[None]]
    pallas_call x1, Pallas kernels: 2.59 us -> 3.92 us  [per_device(): pl.pallas_call(decode_kernel, out_shape=(jax.ShapeDtypeStruct((peers, row...]
    all_to_all x4, starting transfers between devices: 42.4 us -> 41.1 us  [exchange(): return lax.all_to_all(pieces, axis, 0, 0, tiled=True)]
  transfers between devices with their start and end apart: 4 -> 4, of which waited for: 3 -> 3; matrix products, arithmetic and copies ran while one was open for 11% -> 4% of each run, Pallas kernels for 0% -> 0%
where the time goes in v5:
time: 117 us
  starting transfers between devices  41.1 us (35%)
  blocking collectives  30.6 us (26%)
  waiting for transfers between devices  25.1 us (21%)
  Pallas kernels  10.9 us (9%)
  between operations  4.91 us (4%)
  local copies, waits for them, and re-layouts  2.76 us (2%)
    all_to_all x4, starting transfers between devices, exchange(): return lax.all_to_all(pieces, axis, 0, 0, tiled=True)  41.1 us
    all_gather x1, blocking collectives, per_device(): w_near = lax.all_gather(w_bcdt.T, 'tp')  30.6 us
    all_to_all x4, waiting for transfers between devices, exchange(): return lax.all_to_all(pieces, axis, 0, 0, tiled=True)  25.1 us
    pallas_call x1, Pallas kernels, per_device(): pl.pallas_call(decode_kernel, out_shape=(jax.ShapeDtypeStruct((peers, row...  3.92 us
    pallas_call x1, Pallas kernels, per_device(): pl.pallas_call(send_kernel, out_shape=jax.ShapeDtypeStruct((n_ctx, STATE_...  3.03 us
  transfers between devices with their start and end apart: 4, of which 3 were waited for; matrix products, arithmetic and copies ran while one was open for 4% of the time, Pallas kernels for 0%

profile of v5, /device:TPU:1, one launch (start us, length us, event | category | flops | bytes accessed | tf_op | source)
XLA Modules:
  0.0 116.8 jit_solution(4238545342493299681)
XLA Ops:
  0.6 3.0 %send.1 = bf16[16,304,128]{2,1,0:T(8,128)(2,1)} custom-call(s32[4,16]{1,0:T(4,128)} %tokens_hbm.1, s32[16]{0:T(128)} %prompt_hbm.1, f32[2,32]{1,0:T(2,128)} %bitcast.39, bf16[64,6285]{1,0:T(8,128)(2,1)} %bitcast.31, bf16[2,16,128,128]{3,2,1,0:T(8,128)(2,1)} %bitcast.30), custom_call_target="tpu_custom_call" | custom-call | tf_op jit(solution)/shard_map/send/pallas_call | solution.py:388
  3.7 13.6 %all-to-all-start = ((bf16[16,304,128]{2,1,0:T(8,128)(2,1)}), bf16[16,304,128]{2,1,0:T(8,128)(2,1)S(1)}, u32[]{:S(2)}, u32[]{:S(2)}) async-start(bf16[16,304,128]{2,1,0:T(8,128)(2,1)} %send.1), calls=%async_computation | async-start | bytes 2490368 | tf_op jit(solution)/shard_map/all_to_all | solution.py:28
  17.3 0.1 eq.10
  17.4 0.1 reduce_or.9
  17.6 30.6 %all-gather.1 = bf16[4,6,4096]{2,1,0:T(8,128)(2,1)S(1)} all-gather(bf16[1,6,4096]{2,1,0:T(8,128)(2,1)S(1)} %bitcast.34), channel_id=2, replica_groups=mesh['ctx'=16,'dp'=8,'tp'=4] {'tp'}, dimensions={0}, use_global_device_ids=true | all-gather | bytes 245760 | tf_op jit(solution)/shard_map/all_gather | solution.py:416
  48.2 0.4 reshape.77
  48.6 0.2 constant_dynamic-slice_fusion.3
  48.9 0.1 reshape.78
  49.3 0.1 reshape.102
  49.5 1.8 %combine.1 = bf16[8,208,128]{2,1,0:T(8,128)(2,1)} custom-call(s32[8]{0:T(128)S(1)} %convert_element_type.12.chosen_ref, bf16[16,304,128]{2,1,0:T(8,128)(2,1)S(1)} %all-to-all-done.got_ref, bf16[2,16,128]{2,1,0:T(8,128)(2,1)S(1)} %fusion.6.tails_ref), custom_call_target="tpu_custom_call" | custom-call | tf_op jit(solution)/shard_map/combine/pallas_call | solution.py:452
  51.3 7.0 %all-to-all-start.1 = ((bf16[8,208,128]{2,1,0:T(8,128)(2,1)}), bf16[8,208,128]{2,1,0:T(8,128)(2,1)S(1)}, u32[]{:S(2)}, u32[]{:S(2)}) async-start(bf16[8,208,128]{2,1,0:T(8,128)(2,1)} %combine.1), calls=%async_computation.1 | async-start | bytes 851968 | tf_op jit(solution)/shard_map/all_to_all | solution.py:28
  58.4 11.0 %all-to-all-done.1.arrived_ref = bf16[8,208,128]{2,1,0:T(8,128)(2,1)S(1)} async-done(((bf16[8,208,128]{2,1,0:T(8,128)(2,1)}), bf16[8,208,128]{2,1,0:T(8,128)(2,1)S(1)}, u32[]{:S(2)}, u32[]{:S(2)}) %all-to-all-start.1) | async-done | bytes 426016 | tf_op jit(solution)/shard_map/all_to_all | solution.py:28
  69.4 1.4 %columns.1 = bf16[64,8,128]{2,1,0:T(8,128)(2,1)} custom-call(s32[2]{0:T(128)S(1)} %pad_add_fusion.1.place_ref, bf16[8,208,128]{2,1,0:T(8,128)(2,1)S(1)} %all-to-all-done.1.arrived_ref, f32[8,128]{1,0:T(8,128)S(1)} %reshape.80.gain_ref, bf16[128,1024]{1,0:T(8,128)(2,1)S(1)} %fusion.3.weight_ref), custom_call_target="tpu_custom_call" | custom-call | tf_op jit(solution)/shard_map/columns/pallas_call | solution.py:468
  70.8 15.0 %all-to-all-start.2 = ((bf16[64,8,128]{2,1,0:T(8,128)(2,1)}), bf16[64,8,128]{2,1,0:T(8,128)(2,1)S(1)}, u32[]{:S(2)}, u32[]{:S(2)}) async-start(bf16[64,8,128]{2,1,0:T(8,128)(2,1)} %columns.1), calls=%async_computation.2 | async-start | bytes 262144 | tf_op jit(solution)/shard_map/all_to_all | solution.py:28
  85.8 0.7 fusion.11
  89.4 0.1 reshape.87
  89.5 0.1 reshape.88
  89.7 0.1 reshape.89
  91.4 4.8 %all-to-all-done.2.everyone_ref = bf16[64,8,128]{2,1,0:T(8,128)(2,1)S(1)} async-done(((bf16[64,8,128]{2,1,0:T(8,128)(2,1)}), bf16[64,8,128]{2,1,0:T(8,128)(2,1)S(1)}, u32[]{:S(2)}, u32[]{:S(2)}) %all-to-all-start.2) | async-done | bytes 131104 | tf_op jit(solution)/shard_map/all_to_all | solution.py:28
  96.2 3.9 %decode.1 = (bf16[64,8,128]{2,1,0:T(8,128)(2,1)}, f32[24,128]{1,0:T(8,128)S(1)}) custom-call(s32[3]{0:T(128)S(1)} %pad_add_fusion.place_ref, bf16[64,8,128]{2,1,0:T(8,128)(2,1)S(1)} %all-to-all-done.2.everyone_ref, bf16[8,208,128]{2,1,0:T(8,128)(2,1)S(1)} %all-to-all-done.1.arrived_ref, f32[32,128]{1,0:T(8,128)S(1)} %bitcast.28, ...), custom_call_target="tpu_custom_call" | custom-call | tf_op jit(solution)/shard_map/decode/pallas_call | solution.py:487
  100.1 5.5 %all-to-all-start.3 = ((bf16[64,8,128]{2,1,0:T(8,128)(2,1)}), bf16[64,8,128]{2,1,0:T(8,128)(2,1)S(1)}, u32[]{:S(2)}, u32[]{:S(2)}) async-start(bf16[64,8,128]{2,1,0:T(8,128)(2,1)} %get-tuple-element.10), calls=%async_computation.3 | async-start | bytes 262144 | tf_op jit(solution)/shard_map/all_to_all | solution.py:28
  105.7 1.1 convolution_add_fusion
  106.8 9.3 %all-to-all-done.3.incoming_ref = bf16[64,8,128]{2,1,0:T(8,128)(2,1)S(1)} async-done(((bf16[64,8,128]{2,1,0:T(8,128)(2,1)}), bf16[64,8,128]{2,1,0:T(8,128)(2,1)S(1)}, u32[]{:S(2)}, u32[]{:S(2)}) %all-to-all-start.3) | async-done | bytes 131104 | tf_op jit(solution)/shard_map/all_to_all | solution.py:28
  116.0 0.8 finish.1
  (57 shorter events, 1.2 us)
Async XLA Ops:
  3.7 13.6 %copy-start.8 = (s32[16]{0:T(128)S(1)}, s32[16]{0:T(128)}, u32[]{:S(2)}) copy-start(s32[16]{0:T(128)} %prompt_hbm.1) | copy-start | bytes 196
  3.7 13.9 %copy-start.2 = (bf16[4096,6]{0,1:T(8,128)(2,1)S(1)}, bf16[4096,6]{0,1:T(8,128)(2,1)}, u32[]{:S(2)}) copy-start(bf16[4096,6]{0,1:T(8,128)(2,1)} %param.24) | copy-start | bytes 147460
  3.7 45.7 %all-to-all-start = ((bf16[16,304,128]{2,1,0:T(8,128)(2,1)}), bf16[16,304,128]{2,1,0:T(8,128)(2,1)S(1)}, u32[]{:S(2)}, u32[]{:S(2)}) async-start(bf16[16,304,128]{2,1,0:T(8,128)(2,1)} %send.1), calls=%async_computation | async-start | bytes 2490368 | tf_op jit(solution)/shard_map/all_to_all | solution.py:28
  17.3 31.8 %copy-start.1 = (f32[4096]{0:T(1024)S(1)}, f32[4096]{0:T(1024)}, u32[]{:S(2)}) copy-start(f32[4096]{0:T(1024)} %param.22) | copy-start | bytes 49156
  17.3 32.0 %copy-start.5 = (bf16[2,3,256]{2,0,1:T(2,128)(2,1)S(1)}, bf16[2,3,256]{2,0,1:T(2,128)(2,1)}, u32[]{:S(2)}) copy-start(bf16[2,3,256]{2,0,1:T(2,128)(2,1)} %param.37) | copy-start | bytes 9220
  17.3 32.0 %copy-start.6 = (bf16[2,3,2,64]{3,2,1,0:T(2,128)(2,1)S(1)}, bf16[2,3,2,64]{3,2,1,0:T(2,128)(2,1)}, u32[]{:S(2)}) copy-start(bf16[2,3,2,64]{3,2,1,0:T(2,128)(2,1)} %param.36) | copy-start | bytes 4612
  49.4 9.0 %copy-start.4 = (f32[4,256]{1,0:T(4,128)S(1)}, f32[4,256]{1,0:T(4,128)}, u32[]{:S(2)}) copy-start(f32[4,256]{1,0:T(4,128)} %param.27) | copy-start | bytes 12292
  49.4 39.7 %copy-start.3 = (f32[4,2,64]{2,1,0:T(2,128)S(1)}, f32[4,2,64]{2,1,0:T(2,128)}, u32[]{:S(2)}) copy-start(f32[4,2,64]{2,1,0:T(2,128)} %param.25) | copy-start | bytes 6148
  49.4 39.8 %copy-start.9 = (f32[2,64]{1,0:T(2,128)S(1)}, f32[2,64]{1,0:T(2,128)}, u32[]{:S(2)}) copy-start(f32[2,64]{1,0:T(2,128)} %param.26) | copy-start | bytes 1540
  49.5 39.9 %copy-start.11 = (f32[2]{0:T(128)S(1)}, f32[2]{0:T(128)}, u32[]{:S(2)}) copy-start(f32[2]{0:T(128)} %param.29) | copy-start | bytes 28
  49.5 40.0 %copy-start.12 = (f32[2]{0:T(128)S(1)}, f32[2]{0:T(128)}, u32[]{:S(2)}) copy-start(f32[2]{0:T(128)} %param.30) | copy-start | bytes 28
  49.5 40.2 %copy-start.13 = (f32[2]{0:T(128)S(1)}, f32[2]{0:T(128)}, u32[]{:S(2)}) copy-start(f32[2]{0:T(128)} %param.31) | copy-start | bytes 28
  49.5 40.3 %copy-start.10 = (f32[2,64]{1,0:T(2,128)S(1)}, f32[2,64]{1,0:T(2,128)}, u32[]{:S(2)}) copy-start(f32[2,64]{1,0:T(2,128)} %param.32) | copy-start | bytes 1540
  49.5 40.4 %copy-start.7 = (f32[256]{0:T(256)S(1)}, f32[256]{0:T(256)}, u32[]{:S(2)}) copy-start(f32[256]{0:T(256)} %param.28) | copy-start | bytes 3076
  51.3 44.9 %copy-start = (bf16[2,2,64,4096]{3,2,1,0:T(8,128)(2,1)S(1)}, bf16[2,2,64,4096]{3,2,1,0:T(8,128)(2,1)}, u32[]{:S(2)}) copy-start(bf16[2,2,64,4096]{3,2,1,0:T(8,128)(2,1)} %param.23) | copy-start | bytes 6291460
  51.3 18.1 %all-to-all-start.1 = ((bf16[8,208,128]{2,1,0:T(8,128)(2,1)}), bf16[8,208,128]{2,1,0:T(8,128)(2,1)S(1)}, u32[]{:S(2)}, u32[]{:S(2)}) async-start(bf16[8,208,128]{2,1,0:T(8,128)(2,1)} %combine.1), calls=%async_computation.1 | async-start | bytes 851968 | tf_op jit(solution)/shard_map/all_to_all | solution.py:28
  70.8 25.4 %all-to-all-start.2 = ((bf16[64,8,128]{2,1,0:T(8,128)(2,1)}), bf16[64,8,128]{2,1,0:T(8,128)(2,1)S(1)}, u32[]{:S(2)}, u32[]{:S(2)}) async-start(bf16[64,8,128]{2,1,0:T(8,128)(2,1)} %columns.1), calls=%async_computation.2 | async-start | bytes 262144 | tf_op jit(solution)/shard_map/all_to_all | solution.py:28
  100.1 15.9 %all-to-all-start.3 = ((bf16[64,8,128]{2,1,0:T(8,128)(2,1)}), bf16[64,8,128]{2,1,0:T(8,128)(2,1)S(1)}, u32[]{:S(2)}, u32[]{:S(2)}) async-start(bf16[64,8,128]{2,1,0:T(8,128)(2,1)} %get-tuple-element.10), calls=%async_computation.3 | async-start | bytes 262144 | tf_op jit(solution)/shard_map/all_to_all | solution.py:28

commit v6 on v5

--- a/solution.py
+++ b/solution.py
@@ -13,7 +13,7 @@
 F32 = jnp.float32
 LANES = 128
 HALF = 64
-VMEM_LIMIT = 24 * 1024 * 1024
+VMEM_LIMIT = 12 * 1024 * 1024
 
 STATE_ROWS = 256
 RATE_ROWS = 16
@@ -130,6 +130,24 @@
     count = got_ref.shape[0]
     groups = out_ref.shape[0]
     own_rows = ONE_STATE + TAIL_ROWS
+    low = low_half((TOKEN_ROWS, LANES))
+    at = STATE_ROWS + RATE_ROWS
+    for pair in range(0, count // 2, 2):
+        early, late = [], []
+        for k in (pair, pair + 1):
+            one = got_ref[k, at : at + TOKEN_ROWS, :].astype(F32)
+            two = got_ref[count // 2 + k, at : at + TOKEN_ROWS, :].astype(F32)
+            early.append(jnp.where(low, one, pltpu.roll(two, HALF, 1)))
+            late.append(jnp.where(low, pltpu.roll(one, HALF, 1), two))
+        for g in range(groups):
+            source = early if g < groups // 2 else late
+            r = (g % (groups // 2)) * 8
+            both = jnp.concatenate([s[r : r + 8] for s in source], axis=0)
+            near_ref[g, pair * 8 : pair * 8 + 16, :] = both.astype(BF)
+    move_near = pltpu.make_async_copy(
+        near_ref, out_ref.at[:, own_rows : own_rows + NEAR_ROWS, :], sems.at[groups]
+    )
+    move_near.start()
     rates = []
     for k in range(count):
         parts = got_ref[k, STATE_ROWS : STATE_ROWS + RATE_ROWS, :].astype(F32)
@@ -156,27 +174,7 @@
     ]
     for move in moves:
         move.start()
-    low = low_half((TOKEN_ROWS, LANES))
-    at = STATE_ROWS + RATE_ROWS
-    for pair in range(0, count // 2, 2):
-        early, late = [], []
-        for k in (pair, pair + 1):
-            one = got_ref[k, at : at + TOKEN_ROWS, :].astype(F32)
-            two = got_ref[count // 2 + k, at : at + TOKEN_ROWS, :].astype(F32)
-            early.append(jnp.where(low, one, pltpu.roll(two, HALF, 1)))
-            late.append(jnp.where(low, pltpu.roll(one, HALF, 1), two))
-        for g in range(groups):
-            source = early if g < groups // 2 else late
-            r = (g % (groups // 2)) * 8
-            both = jnp.concatenate([s[r : r + 8] for s in source], axis=0)
-            near_ref[g, pair * 8 : pair * 8 + 16, :] = both.astype(BF)
-    moves.append(
-        pltpu.make_async_copy(
-            near_ref, out_ref.at[:, own_rows : own_rows + NEAR_ROWS, :], sems.at[groups]
-        )
-    )
-    moves[-1].start()
-    for move in moves:
+    for move in [*moves, move_near]:
         move.wait()
 
 
@@ -206,11 +204,9 @@
 
 
 def decode_kernel(
-    place_ref, everyone_ref, arrived_ref, gain_ref, small_ref, zx_ref, w_out_hbm, out_ref, extra_ref,
-    wo_ref, x_ref, b_ref, c_ref, tile_ref, load_sem, sems,
+    place_ref, everyone_ref, arrived_ref, gain_ref, small_ref, weights_ref, out_ref, extra_ref,
+    x_ref, b_ref, c_ref, tile_ref, sems,
 ):
-    load_out = pltpu.make_async_copy(w_out_hbm, wo_ref, load_sem)
-    load_out.start()
     peers = everyone_ref.shape[0]
     model = peers * HALF
     lane = lax.broadcasted_iota(jnp.int32, (8, LANES), 1)
@@ -285,7 +281,7 @@
     y = jnp.exp(log_total) * jnp.where(row % 2 == 0, from_start[0], from_start[1])
 
     projected = lax.dot_general(
-        normed, zx_ref[...], (((1,), (1,)), ((), ())), preferred_element_type=F32
+        normed, weights_ref[0 : 2 * LANES, :], (((1,), (1,)), ((), ())), preferred_element_type=F32
     )
     gate = projected[:, 0:LANES]
     x_ref[6:14, :] = projected[:, LANES : 2 * LANES]
@@ -314,11 +310,10 @@
     extra_ref[8:16, :] = b_conv
     extra_ref[16:24, :] = jnp.exp(last)
 
-    load_out.wait()
     moves = []
     for n in range(peers // 16):
         wide = jnp.dot(
-            weighted, wo_ref[:, n * 1024 : (n + 1) * 1024], preferred_element_type=F32
+            weighted, weights_ref[2 * LANES :, n * 1024 : (n + 1) * 1024], preferred_element_type=F32
         )
         for m in range(8):
             piece = wide[:, m * LANES : (m + 1) * LANES]
@@ -478,7 +473,11 @@
         compiler_params=PARAMS,
         name="columns",
     )(place, arrived, near_gain, w_near)
+    piece, w_zx, w_out = lax.optimization_barrier((piece, w_zx, w_out))
     everyone = exchange(piece, BOTH)
+    weights = jnp.concatenate(
+        [w_zx.reshape(2 * channels, model), w_out.reshape(channels, model)], axis=0
+    )
 
     head_at = (tp * n_ctx + ctx) * heads
     place = jnp.concatenate(
@@ -490,15 +489,13 @@
             jax.ShapeDtypeStruct((peers, rows, LANES), BF),
             jax.ShapeDtypeStruct((24, LANES), F32),
         ),
-        in_specs=[SM, VM, VM, VM, VM, VM, HB],
+        in_specs=[SM, VM, VM, VM, VM, VM],
         out_specs=(HB, VM),
         scratch_shapes=[
-            pltpu.VMEM((channels, model), BF),
             pltpu.VMEM((16, LANES), F32),
             pltpu.VMEM((16, LANES), F32),
             pltpu.VMEM((16, LANES), F32),
             pltpu.VMEM((peers, rows, LANES), BF),
-            pltpu.SemaphoreType.DMA(()),
             pltpu.SemaphoreType.DMA((peers // 16,)),
         ],
         compiler_params=PARAMS,
@@ -509,8 +506,7 @@
         arrived,
         norm_gain.reshape(model // LANES, LANES),
         small,
-        w_zx.reshape(2 * channels, model),
-        in_hbm(w_out.reshape(channels, model)),
+        weights,
     )
     incoming = exchange(outgoing, BOTH)
 

time: 117 us -> 118 us (level)
  waiting for transfers between devices: 25.1 us -> 21.1 us
  local copies, waits for them, and re-layouts: 2.76 us -> 6.35 us
  other arithmetic: 0.4 us -> 3.14 us
  Pallas kernels: 10.9 us -> 9.62 us
    all_to_all x4, waiting for transfers between devices: 25.1 us -> 21.1 us  [exchange(): return lax.all_to_all(pieces, axis, 0, 0, tiled=True)]
    unnamed x30 -> x40, local copies, waits for them, and re-layouts: 0.11 us -> 2.49 us
    concatenate x0 -> x1, other arithmetic: none -> 2.16 us  [per_device(): jnp.concatenate([w_zx.reshape(2 * channels, model), w_out.reshape(channel...]
    pallas_call x1, Pallas kernels: 3.92 us -> 2.68 us  [per_device(): pl.pallas_call(decode_kernel, out_shape=(jax.ShapeDtypeStruct((peers, row...]
  transfers between devices with their start and end apart: 4 -> 4, of which waited for: 3 -> 3; matrix products, arithmetic and copies ran while one was open for 4% -> 7% of each run, Pallas kernels for 0% -> 0%
where the time goes in v6:
time: 118 us; the launch traced here: 117 us
  starting transfers between devices  40.2 us (34%)
  blocking collectives  30.8 us (26%)
  waiting for transfers between devices  21.1 us (18%)
  Pallas kernels  9.62 us (8%)
  local copies, waits for them, and re-layouts  6.35 us (5%)
  between operations  4.95 us (4%)
  other arithmetic  3.14 us (3%)
    all_to_all x4, starting transfers between devices, exchange(): return lax.all_to_all(pieces, axis, 0, 0, tiled=True)  40.2 us
    all_gather x1, blocking collectives, per_device(): w_near = lax.all_gather(w_bcdt.T, 'tp')  30.8 us
    all_to_all x4, waiting for transfers between devices, exchange(): return lax.all_to_all(pieces, axis, 0, 0, tiled=True)  21.1 us
    pallas_call x1, Pallas kernels, per_device(): pl.pallas_call(send_kernel, out_shape=jax.ShapeDtypeStruct((n_ctx, STATE_...  3.03 us
    pallas_call x1, Pallas kernels, per_device(): pl.pallas_call(decode_kernel, out_shape=(jax.ShapeDtypeStruct((peers, row...  2.68 us
    unnamed x40, local copies, waits for them, and re-layouts  2.49 us
  transfers between devices with their start and end apart: 4, of which 3 were waited for; matrix products, arithmetic and copies ran while one was open for 7% of the time, Pallas kernels for 0%

profile of v6, /device:TPU:1, one launch (start us, length us, event | category | flops | bytes accessed | tf_op | source)
XLA Modules:
  0.0 117.2 jit_solution(16083974959849343405)
XLA Ops:
  0.7 3.0 %send.1 = bf16[16,304,128]{2,1,0:T(8,128)(2,1)} custom-call(s32[4,16]{1,0:T(4,128)} %tokens_hbm.1, s32[16]{0:T(128)} %prompt_hbm.1, f32[2,32]{1,0:T(2,128)} %bitcast.39, bf16[64,6285]{1,0:T(8,128)(2,1)} %bitcast.31, bf16[2,16,128,128]{3,2,1,0:T(8,128)(2,1)} %bitcast.29), custom_call_target="tpu_custom_call" | custom-call | tf_op jit(solution)/shard_map/send/pallas_call | solution.py:383
  3.7 13.4 %all-to-all-start = ((bf16[16,304,128]{2,1,0:T(8,128)(2,1)}), bf16[16,304,128]{2,1,0:T(8,128)(2,1)S(1)}, u32[]{:S(2)}, u32[]{:S(2)}) async-start(bf16[16,304,128]{2,1,0:T(8,128)(2,1)} %send.1), calls=%async_computation | async-start | bytes 2490368 | tf_op jit(solution)/shard_map/all_to_all | solution.py:28
  17.3 30.8 %all-gather.1 = bf16[4,6,4096]{2,1,0:T(8,128)(2,1)S(1)} all-gather(bf16[1,6,4096]{2,1,0:T(8,128)(2,1)S(1)} %bitcast.34), channel_id=2, replica_groups=mesh['ctx'=16,'dp'=8,'tp'=4] {'tp'}, dimensions={0}, use_global_device_ids=true | all-gather | bytes 245760 | tf_op jit(solution)/shard_map/all_gather | solution.py:411
  48.1 0.4 reshape.77
  48.5 0.2 constant_dynamic-slice_fusion.3
  49.6 1.7 %combine.1 = bf16[8,208,128]{2,1,0:T(8,128)(2,1)} custom-call(s32[8]{0:T(128)S(1)} %convert_element_type.12.chosen_ref, bf16[16,304,128]{2,1,0:T(8,128)(2,1)S(1)} %all-to-all-done.got_ref, bf16[2,16,128]{2,1,0:T(8,128)(2,1)S(1)} %fusion.6.tails_ref), custom_call_target="tpu_custom_call" | custom-call | tf_op jit(solution)/shard_map/combine/pallas_call | solution.py:447
  51.3 6.8 %all-to-all-start.1 = ((bf16[8,208,128]{2,1,0:T(8,128)(2,1)}), bf16[8,208,128]{2,1,0:T(8,128)(2,1)S(1)}, u32[]{:S(2)}, u32[]{:S(2)}) async-start(bf16[8,208,128]{2,1,0:T(8,128)(2,1)} %combine.1), calls=%async_computation.1 | async-start | bytes 851968 | tf_op jit(solution)/shard_map/all_to_all | solution.py:28
  58.2 0.6 fusion.11
  62.3 0.6 pad.14.small_ref
  64.2 0.7 pad_add_fusion.place_ref
  65.0 4.3 %all-to-all-done.1.arrived_ref = bf16[8,208,128]{2,1,0:T(8,128)(2,1)S(1)} async-done(((bf16[8,208,128]{2,1,0:T(8,128)(2,1)}), bf16[8,208,128]{2,1,0:T(8,128)(2,1)S(1)}, u32[]{:S(2)}, u32[]{:S(2)}) %all-to-all-start.1) | async-done | bytes 426016 | tf_op jit(solution)/shard_map/all_to_all | solution.py:28
  69.3 1.4 %columns.1 = bf16[64,8,128]{2,1,0:T(8,128)(2,1)} custom-call(s32[2]{0:T(128)S(1)} %pad_add_fusion.1.place_ref, bf16[8,208,128]{2,1,0:T(8,128)(2,1)S(1)} %all-to-all-done.1.arrived_ref, f32[8,128]{1,0:T(8,128)S(1)} %reshape.80.gain_ref, bf16[128,1024]{1,0:T(8,128)(2,1)S(1)} %fusion.3.weight_ref), custom_call_target="tpu_custom_call" | custom-call | tf_op jit(solution)/shard_map/columns/pallas_call | solution.py:463
  70.7 15.1 %all-to-all-start.2 = ((bf16[64,8,128]{2,1,0:T(8,128)(2,1)}), bf16[64,8,128]{2,1,0:T(8,128)(2,1)S(1)}, u32[]{:S(2)}, u32[]{:S(2)}) async-start(bf16[64,8,128]{2,1,0:T(8,128)(2,1)} %columns.1), calls=%async_computation.2 | async-start | bytes 262144 | tf_op jit(solution)/shard_map/all_to_all | solution.py:28
  85.8 2.2 %pad_maximum_fusion.weights_ref = bf16[384,4096]{1,0:T(8,128)(2,1)S(1)} fusion(bf16[128,4096]{1,0:T(8,128)(2,1)} %bitcast.30, bf16[256,4096]{1,0:T(8,128)(2,1)} %bitcast.28), kind=kLoop, calls=%fused_computation | loop fusion | flops 6291456 | bytes 6291456 | tf_op jit(solution)/shard_map/concatenate | solution.py:478
  87.9 0.6 constant_dynamic-slice_fusion.1
  88.6 7.5 %all-to-all-done.2.everyone_ref = bf16[64,8,128]{2,1,0:T(8,128)(2,1)S(1)} async-done(((bf16[64,8,128]{2,1,0:T(8,128)(2,1)}), bf16[64,8,128]{2,1,0:T(8,128)(2,1)S(1)}, u32[]{:S(2)}, u32[]{:S(2)}) %all-to-all-start.2) | async-done | bytes 131104 | tf_op jit(solution)/shard_map/all_to_all | solution.py:28
  96.1 1.0 copy-done.1
  97.1 0.7 copy-done.3
  97.8 0.7 copy-done.4
  98.5 2.7 %decode.1 = (bf16[64,8,128]{2,1,0:T(8,128)(2,1)}, f32[24,128]{1,0:T(8,128)S(1)}) custom-call(s32[3]{0:T(128)S(1)} %copy-done.4, bf16[64,8,128]{2,1,0:T(8,128)(2,1)S(1)} %all-to-all-done.2.everyone_ref, bf16[8,208,128]{2,1,0:T(8,128)(2,1)S(1)} %copy-done.1, f32[32,128]{1,0:T(8,128)S(1)} %bitcast.27, f32[24,128]{1,0:T(8,128)S(1)} %copy-done.3, ...), custom_call_target="tpu_custom_call" | custom-call | tf_op jit(solution)/shard_map/decode/pallas_call | solution.py:486
  101.2 4.9 %all-to-all-start.3 = ((bf16[64,8,128]{2,1,0:T(8,128)(2,1)}), bf16[64,8,128]{2,1,0:T(8,128)(2,1)S(1)}, u32[]{:S(2)}, u32[]{:S(2)}) async-start(bf16[64,8,128]{2,1,0:T(8,128)(2,1)} %get-tuple-element.16), calls=%async_computation.3 | async-start | bytes 262144 | tf_op jit(solution)/shard_map/all_to_all | solution.py:28
  106.1 1.1 convolution_add_fusion
  107.2 9.3 %all-to-all-done.3.incoming_ref = bf16[64,8,128]{2,1,0:T(8,128)(2,1)S(1)} async-done(((bf16[64,8,128]{2,1,0:T(8,128)(2,1)}), bf16[64,8,128]{2,1,0:T(8,128)(2,1)S(1)}, u32[]{:S(2)}, u32[]{:S(2)}) %all-to-all-start.3) | async-done | bytes 131104 | tf_op jit(solution)/shard_map/all_to_all | solution.py:28
  116.4 0.8 finish.1
  (69 shorter events, 1.8 us)
Async XLA Ops:
  0.6 16.6 %copy-start.7 = (bf16[4096,6]{0,1:T(8,128)(2,1)S(1)}, bf16[4096,6]{0,1:T(8,128)(2,1)}, u32[]{:S(2)}) copy-start(bf16[4096,6]{0,1:T(8,128)(2,1)} %param.24) | copy-start | bytes 147460
  0.6 48.3 %copy-start.2 = (f32[4096]{0:T(1024)S(1)}, f32[4096]{0:T(1024)}, u32[]{:S(2)}) copy-start(f32[4096]{0:T(1024)} %param.22) | copy-start | bytes 49156
  0.7 48.5 %copy-start.13 = (s32[16]{0:T(128)S(1)}, s32[16]{0:T(128)}, u32[]{:S(2)}) copy-start(s32[16]{0:T(128)} %prompt_hbm.1) | copy-start | bytes 196
  0.7 48.7 %copy-start.10 = (bf16[2,3,256]{2,0,1:T(2,128)(2,1)S(1)}, bf16[2,3,256]{2,0,1:T(2,128)(2,1)}, u32[]{:S(2)}) copy-start(bf16[2,3,256]{2,0,1:T(2,128)(2,1)} %param.37) | copy-start | bytes 9220
  0.7 48.8 %copy-start.11 = (bf16[2,3,2,64]{3,2,1,0:T(2,128)(2,1)S(1)}, bf16[2,3,2,64]{3,2,1,0:T(2,128)(2,1)}, u32[]{:S(2)}) copy-start(bf16[2,3,2,64]{3,2,1,0:T(2,128)(2,1)} %param.36) | copy-start | bytes 4612
  3.7 45.8 %all-to-all-start = ((bf16[16,304,128]{2,1,0:T(8,128)(2,1)}), bf16[16,304,128]{2,1,0:T(8,128)(2,1)S(1)}, u32[]{:S(2)}, u32[]{:S(2)}) async-start(bf16[16,304,128]{2,1,0:T(8,128)(2,1)} %send.1), calls=%async_computation | async-start | bytes 2490368 | tf_op jit(solution)/shard_map/all_to_all | solution.py:28
  17.2 44.3 %copy-start.8 = (f32[4,2,64]{2,1,0:T(2,128)S(1)}, f32[4,2,64]{2,1,0:T(2,128)}, u32[]{:S(2)}) copy-start(f32[4,2,64]{2,1,0:T(2,128)} %param.25) | copy-start | bytes 6148
  17.2 44.4 %copy-start.16 = (f32[2]{0:T(128)S(1)}, f32[2]{0:T(128)}, u32[]{:S(2)}) copy-start(f32[2]{0:T(128)} %param.29) | copy-start | bytes 28
  17.2 44.5 %copy-start.17 = (f32[2]{0:T(128)S(1)}, f32[2]{0:T(128)}, u32[]{:S(2)}) copy-start(f32[2]{0:T(128)} %param.30) | copy-start | bytes 28
  17.2 44.7 %copy-start.18 = (f32[2]{0:T(128)S(1)}, f32[2]{0:T(128)}, u32[]{:S(2)}) copy-start(f32[2]{0:T(128)} %param.31) | copy-start | bytes 28
  17.2 44.8 %copy-start.14 = (f32[2,64]{1,0:T(2,128)S(1)}, f32[2,64]{1,0:T(2,128)}, u32[]{:S(2)}) copy-start(f32[2,64]{1,0:T(2,128)} %param.26) | copy-start | bytes 1540
  17.2 44.9 %copy-start.15 = (f32[2,64]{1,0:T(2,128)S(1)}, f32[2,64]{1,0:T(2,128)}, u32[]{:S(2)}) copy-start(f32[2,64]{1,0:T(2,128)} %param.32) | copy-start | bytes 1540
  17.2 45.0 %copy-start.9 = (f32[4,256]{1,0:T(4,128)S(1)}, f32[4,256]{1,0:T(4,128)}, u32[]{:S(2)}) copy-start(f32[4,256]{1,0:T(4,128)} %param.27) | copy-start | bytes 12292
  17.3 45.0 %copy-start.12 = (f32[256]{0:T(256)S(1)}, f32[256]{0:T(256)}, u32[]{:S(2)}) copy-start(f32[256]{0:T(256)} %param.28) | copy-start | bytes 3076
  51.3 18.0 %all-to-all-start.1 = ((bf16[8,208,128]{2,1,0:T(8,128)(2,1)}), bf16[8,208,128]{2,1,0:T(8,128)(2,1)S(1)}, u32[]{:S(2)}, u32[]{:S(2)}) async-start(bf16[8,208,128]{2,1,0:T(8,128)(2,1)} %combine.1), calls=%async_computation.1 | async-start | bytes 851968 | tf_op jit(solution)/shard_map/all_to_all | solution.py:28
  69.2 16.5 %copy-start = (bf16[8,208,128]{2,1,0:T(8,128)(2,1)}, bf16[8,208,128]{2,1,0:T(8,128)(2,1)S(1)}, u32[]{:S(2)}) copy-start(bf16[8,208,128]{2,1,0:T(8,128)(2,1)S(1)} %all-to-all-done.1.arrived_ref) | copy-start | bytes 1277956
  70.7 25.4 %all-to-all-start.2 = ((bf16[64,8,128]{2,1,0:T(8,128)(2,1)}), bf16[64,8,128]{2,1,0:T(8,128)(2,1)S(1)}, u32[]{:S(2)}, u32[]{:S(2)}) async-start(bf16[64,8,128]{2,1,0:T(8,128)(2,1)} %columns.1), calls=%async_computation.2 | async-start | bytes 262144 | tf_op jit(solution)/shard_map/all_to_all | solution.py:28
  85.7 2.2 %slice-start = ((bf16[8,208,128]{2,1,0:T(8,128)(2,1)}), bf16[8,128,128]{2,1,0:T(8,128)(2,1)S(1)}, s32[]{:S(2)}) async-start(bf16[8,208,128]{2,1,0:T(8,128)(2,1)} %copy-done), calls=%async_computation.4 | async-start | bytes 524288 | tf_op jit(solution)/shard_map/slice | solution.py:515
  96.1 1.0 copy-start.1
  97.1 0.7 copy-start.3
  97.8 0.7 copy-start.4
  98.5 7.6 %copy-start.5 = (bf16[1,128,128]{2,1,0:T(8,128)(2,1)S(1)}, bf16[1,128,128]{2,1,0:T(8,128)(2,1)}, u32[]{:S(2)}) copy-start(bf16[1,128,128]{2,1,0:T(8,128)(2,1)} %get-tuple-element.18) | copy-start | bytes 98308
  98.5 7.6 %copy-start.6 = (bf16[1,128,128]{2,1,0:T(8,128)(2,1)S(1)}, bf16[1,128,128]{2,1,0:T(8,128)(2,1)}, u32[]{:S(2)}) copy-start(bf16[1,128,128]{2,1,0:T(8,128)(2,1)} %get-tuple-element.19) | copy-start | bytes 98308
  101.2 15.3 %all-to-all-start.3 = ((bf16[64,8,128]{2,1,0:T(8,128)(2,1)}), bf16[64,8,128]{2,1,0:T(8,128)(2,1)S(1)}, u32[]{:S(2)}, u32[]{:S(2)}) async-start(bf16[64,8,128]{2,1,0:T(8,128)(2,1)} %get-tuple-element.16), calls=%async_computation.3 | async-start | bytes 262144 | tf_op jit(solution)/shard_map/all_to_all | solution.py:28

commit v7 on v6

--- a/solution.py
+++ b/solution.py
@@ -178,7 +178,7 @@
         move.wait()
 
 
-def columns_kernel(place_ref, arrived_ref, gain_ref, weight_ref, out_ref, near_ref, tile_ref, sem):
+def columns_kernel(arrived_ref, gain_ref, weight_ref, out_ref, near_ref, tile_ref, sem):
     groups = arrived_ref.shape[0]
     at = ONE_STATE + TAIL_ROWS
     total = arrived_ref[0, at : at + NEAR_ROWS, :].astype(F32)
@@ -193,7 +193,9 @@
     partial = lax.dot_general(
         weighted, weight_ref[...], (((1,), (1,)), ((), ())), preferred_element_type=F32
     )
-    own = pltpu.roll(near_ref[place_ref[0]], place_ref[1], 1)
+    ctx = lax.axis_index("ctx")
+    half = lax.axis_size("ctx") // 2
+    own = pltpu.roll(near_ref[lax.rem(ctx, half)], ctx // half * HALF, 1)
     lane = lax.broadcasted_iota(jnp.int32, (8, LANES), 1)
     first = partial.astype(BF).astype(F32)
     tile = jnp.where(lane < HALF, own, jnp.where(lane < HALF + 24, first, partial - first))
@@ -204,9 +206,15 @@
 
 
 def decode_kernel(
-    place_ref, everyone_ref, arrived_ref, gain_ref, small_ref, weights_ref, out_ref, extra_ref,
-    x_ref, b_ref, c_ref, tile_ref, sems,
+    everyone_ref, weights_ref, arrived_hbm, prompt_hbm, gain_hbm, small_hbm, out_ref, extra_ref,
+    arrived_ref, prompt_ref, gain_ref, small_ref, x_ref, b_ref, c_ref, tile_ref, load_sems, sems,
 ):
+    pairs = [(prompt_hbm, prompt_ref), (gain_hbm, gain_ref), (small_hbm, small_ref)]
+    loads = [pltpu.make_async_copy(a, b, load_sems.at[n]) for n, (a, b) in enumerate(pairs)]
+    for load in loads:
+        load.start()
+    ctx, group, tp = (lax.axis_index(a) for a in ("ctx", "dp", "tp"))
+    head_at = (tp * lax.axis_size("ctx") + ctx) * 2
     peers = everyone_ref.shape[0]
     model = peers * HALF
     lane = lax.broadcasted_iota(jnp.int32, (8, LANES), 1)
@@ -220,9 +228,24 @@
     squares = rows[0] * rows[0]
     for r in rows[1:]:
         squares = squares + r * r
+    own_rows = arrived_ref.shape[1]
+    loads[0].wait()
+    for slot in range(2):
+        holder = prompt_ref[group * 2 + slot] // 2
+        loads.append(
+            pltpu.make_async_copy(
+                arrived_hbm.at[holder, 0:own_rows, :], arrived_ref.at[slot], load_sems.at[3 + slot]
+            )
+        )
+        loads[-1].start()
+    loads[1].wait()
     inverse = lax.rsqrt(jnp.sum(squares, axis=1, keepdims=True) * (1.0 / model) + EPS)
     normed = jnp.concatenate(
         [(r * inverse * gain_ref[n : n + 1, :]).astype(BF) for n, r in enumerate(rows)], axis=1
+    )
+
+    projected = lax.dot_general(
+        normed, weights_ref[0 : 2 * LANES, :], (((1,), (1,)), ((), ())), preferred_element_type=F32
     )
 
     columns = [jnp.zeros((8, LANES), F32) for _ in range(3)]
@@ -239,8 +262,11 @@
             columns[first + 1] = columns[first + 1] + jnp.where(lane < offset, part, 0.0)
     columns = [v * inverse for v in columns]
 
+    for load in loads[2:]:
+        load.wait()
+
     for slot in range(2):
-        tail = arrived_ref[place_ref[slot], ONE_STATE : ONE_STATE + TAIL_ROWS, :].astype(F32)
+        tail = arrived_ref[slot, ONE_STATE : ONE_STATE + TAIL_ROWS, :].astype(F32)
         for k in range(3):
             at = 2 * k + slot
             x_ref[at : at + 1, :] = tail[k : k + 1]
@@ -258,7 +284,7 @@
     b_conv = convolved(b_ref, 4, 13)
     c_conv = convolved(c_ref, 8, 14)
 
-    raw = pltpu.roll(columns[2], place_ref[2], 1)
+    raw = pltpu.roll(columns[2], lax.rem(LANES - head_at, LANES), 1)
     raw = jnp.where(low, raw[:, 0:1], raw[:, 1:2]) + small_ref[15:16, :]
     step = jnp.maximum(raw, 0.0) + jnp.log1p(jnp.exp(-jnp.abs(raw)))
     log_retain = -step * jnp.exp(small_ref[16:17, :])
@@ -273,16 +299,13 @@
     c_parts = jnp.concatenate([p.astype(F32) for p in in_three(c_conv)], axis=0).astype(BF)
     from_start = []
     for slot in range(2):
-        state = arrived_ref[place_ref[slot], 0:ONE_STATE, :]
+        state = arrived_ref[slot, 0:ONE_STATE, :]
         product = lax.dot_general(
             c_parts, state, (((1,), (1,)), ((), ())), preferred_element_type=F32
         )
         from_start.append(product[0:8] + product[8:16] + product[16:24])
     y = jnp.exp(log_total) * jnp.where(row % 2 == 0, from_start[0], from_start[1])
 
-    projected = lax.dot_general(
-        normed, weights_ref[0 : 2 * LANES, :], (((1,), (1,)), ((), ())), preferred_element_type=F32
-    )
     gate = projected[:, 0:LANES]
     x_ref[6:14, :] = projected[:, LANES : 2 * LANES]
     x_conv = convolved(x_ref, 0, 12)
@@ -459,11 +482,10 @@
     )(prompt_for, got, tails)
     arrived = exchange(routed, "dp")
 
-    place = jnp.stack([ctx % (n_ctx // 2), (ctx // (n_ctx // 2)) * HALF]).astype(jnp.int32)
     piece = pl.pallas_call(
         columns_kernel,
         out_shape=jax.ShapeDtypeStruct((peers, rows, LANES), BF),
-        in_specs=[SM, VM, VM, VM],
+        in_specs=[VM, VM, VM],
         out_specs=HB,
         scratch_shapes=[
             pltpu.VMEM((NEAR_ROWS // 8, 8, LANES), F32),
@@ -472,47 +494,48 @@
         ],
         compiler_params=PARAMS,
         name="columns",
-    )(place, arrived, near_gain, w_near)
+    )(arrived, near_gain, w_near)
     piece, w_zx, w_out = lax.optimization_barrier((piece, w_zx, w_out))
     everyone = exchange(piece, BOTH)
     weights = jnp.concatenate(
         [w_zx.reshape(2 * channels, model), w_out.reshape(channels, model)], axis=0
     )
 
-    head_at = (tp * n_ctx + ctx) * heads
-    place = jnp.concatenate(
-        [own_slots // slots, ((LANES - head_at) % LANES)[None]]
-    ).astype(jnp.int32)
     outgoing, extra = pl.pallas_call(
         decode_kernel,
         out_shape=(
             jax.ShapeDtypeStruct((peers, rows, LANES), BF),
             jax.ShapeDtypeStruct((24, LANES), F32),
         ),
-        in_specs=[SM, VM, VM, VM, VM, VM],
+        in_specs=[VM, VM, HB, HB, HB, HB],
         out_specs=(HB, VM),
         scratch_shapes=[
+            pltpu.VMEM((slots, ONE_STATE + TAIL_ROWS, width), BF),
+            pltpu.SMEM(decode_prompt.shape, jnp.int32),
+            pltpu.VMEM((model // LANES, LANES), F32),
+            pltpu.VMEM(small.shape, F32),
             pltpu.VMEM((16, LANES), F32),
             pltpu.VMEM((16, LANES), F32),
             pltpu.VMEM((16, LANES), F32),
             pltpu.VMEM((peers, rows, LANES), BF),
+            pltpu.SemaphoreType.DMA((3 + slots,)),
             pltpu.SemaphoreType.DMA((peers // 16,)),
         ],
         compiler_params=PARAMS,
         name="decode",
     )(
-        place,
         everyone,
-        arrived,
-        norm_gain.reshape(model // LANES, LANES),
-        small,
         weights,
+        in_hbm(arrived),
+        in_hbm(decode_prompt),
+        in_hbm(norm_gain.reshape(model // LANES, LANES)),
+        in_hbm(small),
     )
     incoming = exchange(outgoing, BOTH)
 
     start = jnp.stack(
         [
-            lax.dynamic_index_in_dim(arrived[:, :ONE_STATE], place[s], 0, keepdims=False)
+            lax.dynamic_index_in_dim(arrived[:, :ONE_STATE], own_slots[s] // slots, 0, keepdims=False)
             for s in range(slots)
         ]
     )

time: 118 us -> 115 us (0.975)
  local copies, waits for them, and re-layouts: 6.35 us -> 3.96 us
  between operations: 4.95 us -> 6.19 us
    unnamed x40 -> x34, local copies, waits for them, and re-layouts: 2.49 us -> 0.11 us
  transfers between devices with their start and end apart: 4 -> 4, of which waited for: 3 -> 3; matrix products, arithmetic and copies ran while one was open for 7% -> 6% of each run, Pallas kernels for 0% -> 0%
where the time goes in v7:
time: 115 us
  starting transfers between devices  40.2 us (35%)
  blocking collectives  30.8 us (27%)
  waiting for transfers between devices  20.7 us (18%)
  Pallas kernels  9.33 us (8%)
  between operations  6.19 us (5%)
  local copies, waits for them, and re-layouts  3.96 us (3%)
  other arithmetic  2.32 us (2%)
    all_to_all x4, starting transfers between devices, exchange(): return lax.all_to_all(pieces, axis, 0, 0, tiled=True)  40.2 us
    all_gather x1, blocking collectives, per_device(): w_near = lax.all_gather(w_bcdt.T, 'tp')  30.8 us
    all_to_all x4, waiting for transfers between devices, exchange(): return lax.all_to_all(pieces, axis, 0, 0, tiled=True)  20.7 us
    pallas_call x1, Pallas kernels, per_device(): pl.pallas_call(send_kernel, out_shape=jax.ShapeDtypeStruct((n_ctx, STATE_...  3.02 us
    pallas_call x1, Pallas kernels, per_device(): pl.pallas_call(decode_kernel, out_shape=(jax.ShapeDtypeStruct((peers, row...  2.93 us
  transfers between devices with their start and end apart: 4, of which 3 were waited for; matrix products, arithmetic and copies ran while one was open for 6% of the time, Pallas kernels for 0%

profile of v7, /device:TPU:1, one launch (start us, length us, event | category | flops | bytes accessed | tf_op | source)
XLA Modules:
  0.0 114.6 jit_solution(15311590798346069759)
XLA Ops:
  0.7 3.0 %send.1 = bf16[16,304,128]{2,1,0:T(8,128)(2,1)} custom-call(s32[4,16]{1,0:T(4,128)} %tokens_hbm.1, s32[16]{0:T(128)} %prompt_hbm.3, f32[2,32]{1,0:T(2,128)} %bitcast.36, bf16[64,6285]{1,0:T(8,128)(2,1)} %bitcast.27, bf16[2,16,128,128]{3,2,1,0:T(8,128)(2,1)} %bitcast.25), custom_call_target="tpu_custom_call" | custom-call | tf_op jit(solution)/shard_map/send/pallas_call | solution.py:406
  3.7 13.4 %all-to-all-start = ((bf16[16,304,128]{2,1,0:T(8,128)(2,1)}), bf16[16,304,128]{2,1,0:T(8,128)(2,1)S(1)}, u32[]{:S(2)}, u32[]{:S(2)}) async-start(bf16[16,304,128]{2,1,0:T(8,128)(2,1)} %send.1), calls=%async_computation | async-start | bytes 2490368 | tf_op jit(solution)/shard_map/all_to_all | solution.py:28
  17.3 30.8 %all-gather.1 = bf16[4,6,4096]{2,1,0:T(8,128)(2,1)S(1)} all-gather(bf16[1,6,4096]{2,1,0:T(8,128)(2,1)S(1)} %bitcast.31), channel_id=2, replica_groups=mesh['ctx'=16,'dp'=8,'tp'=4] {'tp'}, dimensions={0}, use_global_device_ids=true | all-gather | bytes 245760 | tf_op jit(solution)/shard_map/all_gather | solution.py:434
  48.1 0.4 reshape.77
  48.5 0.2 constant_dynamic-slice_fusion.3
  48.8 0.1 reshape.78
  49.1 0.1 eq.7
  49.2 0.1 reduce_or.9
  49.4 0.1 reshape.102
  49.5 1.7 %combine.1 = bf16[8,208,128]{2,1,0:T(8,128)(2,1)} custom-call(s32[8]{0:T(128)S(1)} %convert_element_type.12.chosen_ref, bf16[16,304,128]{2,1,0:T(8,128)(2,1)S(1)} %all-to-all-done.got_ref, bf16[2,16,128]{2,1,0:T(8,128)(2,1)S(1)} %fusion.6.tails_ref), custom_call_target="tpu_custom_call" | custom-call | tf_op jit(solution)/shard_map/combine/pallas_call | solution.py:470
  51.3 6.8 %all-to-all-start.1 = ((bf16[8,208,128]{2,1,0:T(8,128)(2,1)}), bf16[8,208,128]{2,1,0:T(8,128)(2,1)S(1)}, u32[]{:S(2)}, u32[]{:S(2)}) async-start(bf16[8,208,128]{2,1,0:T(8,128)(2,1)} %combine.1), calls=%async_computation.1 | async-start | bytes 851968 | tf_op jit(solution)/shard_map/all_to_all | solution.py:28
  58.2 0.6 fusion.11
  64.8 0.6 pad.14.small_hbm
  65.4 3.9 %all-to-all-done.1.arrived_ref.arrived_hbm = bf16[8,208,128]{2,1,0:T(8,128)(2,1)S(1)} async-done(((bf16[8,208,128]{2,1,0:T(8,128)(2,1)}), bf16[8,208,128]{2,1,0:T(8,128)(2,1)S(1)}, u32[]{:S(2)}, u32[]{:S(2)}) %all-to-all-start.1) | async-done | bytes 426016 | tf_op jit(solution)/shard_map/all_to_all | solution.py:28
  69.2 0.9 columns.1
  70.1 15.1 %all-to-all-start.2 = ((bf16[64,8,128]{2,1,0:T(8,128)(2,1)}), bf16[64,8,128]{2,1,0:T(8,128)(2,1)S(1)}, u32[]{:S(2)}, u32[]{:S(2)}) async-start(bf16[64,8,128]{2,1,0:T(8,128)(2,1)} %columns.1), calls=%async_computation.2 | async-start | bytes 262144 | tf_op jit(solution)/shard_map/all_to_all | solution.py:28
  85.2 2.2 %pad_maximum_fusion.weights_ref = bf16[384,4096]{1,0:T(8,128)(2,1)S(1)} fusion(bf16[128,4096]{1,0:T(8,128)(2,1)} %bitcast.26, bf16[256,4096]{1,0:T(8,128)(2,1)} %bitcast.24), kind=kLoop, calls=%fused_computation | loop fusion | flops 6291456 | bytes 6291456 | tf_op jit(solution)/shard_map/concatenate | solution.py:500
  87.4 0.6 constant_dynamic-slice_fusion.1
  88.0 7.5 %all-to-all-done.2.everyone_ref = bf16[64,8,128]{2,1,0:T(8,128)(2,1)S(1)} async-done(((bf16[64,8,128]{2,1,0:T(8,128)(2,1)}), bf16[64,8,128]{2,1,0:T(8,128)(2,1)S(1)}, u32[]{:S(2)}, u32[]{:S(2)}) %all-to-all-start.2) | async-done | bytes 131104 | tf_op jit(solution)/shard_map/all_to_all | solution.py:28
  95.6 2.9 %decode.1 = (bf16[64,8,128]{2,1,0:T(8,128)(2,1)}, f32[24,128]{1,0:T(8,128)S(1)}) custom-call(bf16[64,8,128]{2,1,0:T(8,128)(2,1)S(1)} %all-to-all-done.2.everyone_ref, bf16[384,4096]{1,0:T(8,128)(2,1)S(1)} %pad_maximum_fusion.weights_ref, bf16[8,208,128]{2,1,0:T(8,128)(2,1)} %copy-done, s32[16]{0:T(128)} %prompt_hbm.3, f32[32,128]{1,0:T(8,128)} %bitcast.30, ...), custom_call_target="tpu_custom_call" | custom-call | tf_op jit(solution)/shard_map/decode/pallas_call | solution.py:504
  98.5 4.9 %all-to-all-start.3 = ((bf16[64,8,128]{2,1,0:T(8,128)(2,1)}), bf16[64,8,128]{2,1,0:T(8,128)(2,1)S(1)}, u32[]{:S(2)}, u32[]{:S(2)}) async-start(bf16[64,8,128]{2,1,0:T(8,128)(2,1)} %get-tuple-element.16), calls=%async_computation.3 | async-start | bytes 262144 | tf_op jit(solution)/shard_map/all_to_all | solution.py:28
  103.4 1.1 convolution_add_fusion
  104.5 9.3 %all-to-all-done.3.incoming_ref = bf16[64,8,128]{2,1,0:T(8,128)(2,1)S(1)} async-done(((bf16[64,8,128]{2,1,0:T(8,128)(2,1)}), bf16[64,8,128]{2,1,0:T(8,128)(2,1)S(1)}, u32[]{:S(2)}, u32[]{:S(2)}) %all-to-all-start.3) | async-done | bytes 131104 | tf_op jit(solution)/shard_map/all_to_all | solution.py:28
  113.8 0.8 finish.1
  (61 shorter events, 1.3 us)
Async XLA Ops:
  0.6 16.6 %copy-start.4 = (bf16[4096,6]{0,1:T(8,128)(2,1)S(1)}, bf16[4096,6]{0,1:T(8,128)(2,1)}, u32[]{:S(2)}) copy-start(bf16[4096,6]{0,1:T(8,128)(2,1)} %param.24) | copy-start | bytes 147460
  0.6 48.3 %copy-start.3 = (f32[4096]{0:T(1024)S(1)}, f32[4096]{0:T(1024)}, u32[]{:S(2)}) copy-start(f32[4096]{0:T(1024)} %param.22) | copy-start | bytes 49156
  0.7 48.5 %copy-start.9 = (s32[16]{0:T(128)S(1)}, s32[16]{0:T(128)}, u32[]{:S(2)}) copy-start(s32[16]{0:T(128)} %prompt_hbm.3) | copy-start | bytes 196
  0.7 48.7 %copy-start.7 = (bf16[2,3,256]{2,0,1:T(2,128)(2,1)S(1)}, bf16[2,3,256]{2,0,1:T(2,128)(2,1)}, u32[]{:S(2)}) copy-start(bf16[2,3,256]{2,0,1:T(2,128)(2,1)} %param.37) | copy-start | bytes 9220
  0.7 48.7 %copy-start.8 = (bf16[2,3,2,64]{3,2,1,0:T(2,128)(2,1)S(1)}, bf16[2,3,2,64]{3,2,1,0:T(2,128)(2,1)}, u32[]{:S(2)}) copy-start(bf16[2,3,2,64]{3,2,1,0:T(2,128)(2,1)} %param.36) | copy-start | bytes 4612
  3.7 45.8 %all-to-all-start = ((bf16[16,304,128]{2,1,0:T(8,128)(2,1)}), bf16[16,304,128]{2,1,0:T(8,128)(2,1)S(1)}, u32[]{:S(2)}, u32[]{:S(2)}) async-start(bf16[16,304,128]{2,1,0:T(8,128)(2,1)} %send.1), calls=%async_computation | async-start | bytes 2490368 | tf_op jit(solution)/shard_map/all_to_all | solution.py:28
  17.2 46.8 %copy-start.5 = (f32[4,2,64]{2,1,0:T(2,128)S(1)}, f32[4,2,64]{2,1,0:T(2,128)}, u32[]{:S(2)}) copy-start(f32[4,2,64]{2,1,0:T(2,128)} %param.25) | copy-start | bytes 6148
  17.2 46.9 %copy-start.13 = (f32[2]{0:T(128)S(1)}, f32[2]{0:T(128)}, u32[]{:S(2)}) copy-start(f32[2]{0:T(128)} %param.29) | copy-start | bytes 28
  17.2 47.1 %copy-start.14 = (f32[2]{0:T(128)S(1)}, f32[2]{0:T(128)}, u32[]{:S(2)}) copy-start(f32[2]{0:T(128)} %param.30) | copy-start | bytes 28
  17.2 47.2 %copy-start.15 = (f32[2]{0:T(128)S(1)}, f32[2]{0:T(128)}, u32[]{:S(2)}) copy-start(f32[2]{0:T(128)} %param.31) | copy-start | bytes 28
  17.2 47.3 %copy-start.11 = (f32[2,64]{1,0:T(2,128)S(1)}, f32[2,64]{1,0:T(2,128)}, u32[]{:S(2)}) copy-start(f32[2,64]{1,0:T(2,128)} %param.26) | copy-start | bytes 1540
  17.2 47.4 %copy-start.12 = (f32[2,64]{1,0:T(2,128)S(1)}, f32[2,64]{1,0:T(2,128)}, u32[]{:S(2)}) copy-start(f32[2,64]{1,0:T(2,128)} %param.32) | copy-start | bytes 1540
  17.2 47.5 %copy-start.6 = (f32[4,256]{1,0:T(4,128)S(1)}, f32[4,256]{1,0:T(4,128)}, u32[]{:S(2)}) copy-start(f32[4,256]{1,0:T(4,128)} %param.27) | copy-start | bytes 12292
  17.2 47.5 %copy-start.10 = (f32[256]{0:T(256)S(1)}, f32[256]{0:T(256)}, u32[]{:S(2)}) copy-start(f32[256]{0:T(256)} %param.28) | copy-start | bytes 3076
  51.3 18.0 %all-to-all-start.1 = ((bf16[8,208,128]{2,1,0:T(8,128)(2,1)}), bf16[8,208,128]{2,1,0:T(8,128)(2,1)S(1)}, u32[]{:S(2)}, u32[]{:S(2)}) async-start(bf16[8,208,128]{2,1,0:T(8,128)(2,1)} %combine.1), calls=%async_computation.1 | async-start | bytes 851968 | tf_op jit(solution)/shard_map/all_to_all | solution.py:28
  69.2 16.0 %copy-start = (bf16[8,208,128]{2,1,0:T(8,128)(2,1)}, bf16[8,208,128]{2,1,0:T(8,128)(2,1)S(1)}, u32[]{:S(2)}) copy-start(bf16[8,208,128]{2,1,0:T(8,128)(2,1)S(1)} %all-to-all-done.1.arrived_ref.arrived_hbm) | copy-start | bytes 1277956
  70.1 25.4 %all-to-all-start.2 = ((bf16[64,8,128]{2,1,0:T(8,128)(2,1)}), bf16[64,8,128]{2,1,0:T(8,128)(2,1)S(1)}, u32[]{:S(2)}, u32[]{:S(2)}) async-start(bf16[64,8,128]{2,1,0:T(8,128)(2,1)} %columns.1), calls=%async_computation.2 | async-start | bytes 262144 | tf_op jit(solution)/shard_map/all_to_all | solution.py:28
  85.2 2.2 %slice-start = ((bf16[8,208,128]{2,1,0:T(8,128)(2,1)}), bf16[8,128,128]{2,1,0:T(8,128)(2,1)S(1)}, s32[]{:S(2)}) async-start(bf16[8,208,128]{2,1,0:T(8,128)(2,1)} %copy-done), calls=%async_computation.4 | async-start | bytes 524288 | tf_op jit(solution)/shard_map/slice | solution.py:538
  88.0 15.4 %copy-start.1 = (bf16[1,128,128]{2,1,0:T(8,128)(2,1)S(1)}, bf16[1,128,128]{2,1,0:T(8,128)(2,1)}, u32[]{:S(2)}) copy-start(bf16[1,128,128]{2,1,0:T(8,128)(2,1)} %get-tuple-element.18) | copy-start | bytes 98308
  88.0 15.4 %copy-start.2 = (bf16[1,128,128]{2,1,0:T(8,128)(2,1)S(1)}, bf16[1,128,128]{2,1,0:T(8,128)(2,1)}, u32[]{:S(2)}) copy-start(bf16[1,128,128]{2,1,0:T(8,128)(2,1)} %get-tuple-element.19) | copy-start | bytes 98308
  98.5 15.3 %all-to-all-start.3 = ((bf16[64,8,128]{2,1,0:T(8,128)(2,1)}), bf16[64,8,128]{2,1,0:T(8,128)(2,1)S(1)}, u32[]{:S(2)}, u32[]{:S(2)}) async-start(bf16[64,8,128]{2,1,0:T(8,128)(2,1)} %get-tuple-element.16), calls=%async_computation.3 | async-start | bytes 262144 | tf_op jit(solution)/shard_map/all_to_all | solution.py:28

commit v8 on v7

--- a/solution.py
+++ b/solution.py
@@ -431,13 +431,6 @@
     )
     got = exchange(sent, "ctx")
 
-    w_near = lax.all_gather(w_bcdt.T, "tp")
-    own_columns = n_tp * w_bcdt.shape[1]
-    w_near = w_near.reshape(own_columns, 2, n_ctx // 2, n_tp, features)
-    w_near = lax.dynamic_index_in_dim(w_near, tp, 3, keepdims=False)
-    w_near = jnp.swapaxes(w_near, 1, 2).reshape(own_columns, -1)
-    w_near = jnp.concatenate([w_near, w_near], axis=0)
-    w_near = jnp.pad(w_near, ((HALF, LANES - HALF - 2 * own_columns), (0, 0)))
     near_gain = norm_gain.reshape(2, n_ctx // 2, n_tp, features)
     near_gain = lax.dynamic_index_in_dim(near_gain, tp, 2, keepdims=False)
     near_gain = jnp.swapaxes(near_gain, 0, 1).reshape(n_ctx // 2, -1)
@@ -466,7 +459,7 @@
     )
     small = jnp.pad(small, ((0, -small.shape[0] % 8), (0, 0)))
 
-    got, w_near, near_gain = lax.optimization_barrier((got, w_near, near_gain))
+    got, near_gain, small = lax.optimization_barrier((got, near_gain, small))
     routed = pl.pallas_call(
         combine_kernel,
         out_shape=jax.ShapeDtypeStruct((n_dp, ONE_STATE + TAIL_ROWS + NEAR_ROWS, width), BF),
@@ -480,7 +473,16 @@
         compiler_params=PARAMS,
         name="combine",
     )(prompt_for, got, tails)
+    routed, w_bcdt = lax.optimization_barrier((routed, w_bcdt))
     arrived = exchange(routed, "dp")
+
+    w_near = lax.all_gather(w_bcdt.T, "tp")
+    own_columns = n_tp * w_bcdt.shape[1]
+    w_near = w_near.reshape(own_columns, 2, n_ctx // 2, n_tp, features)
+    w_near = lax.dynamic_index_in_dim(w_near, tp, 3, keepdims=False)
+    w_near = jnp.swapaxes(w_near, 1, 2).reshape(own_columns, -1)
+    w_near = jnp.concatenate([w_near, w_near], axis=0)
+    w_near = jnp.pad(w_near, ((HALF, LANES - HALF - 2 * own_columns), (0, 0)))
 
     piece = pl.pallas_call(
         columns_kernel,

time: 115 us -> 112 us (0.974)
  waiting for transfers between devices: 20.7 us -> 41 us
  blocking collectives: 30.8 us -> 14.6 us
  starting transfers between devices: 40.2 us -> 32.8 us
    all_to_all x4, waiting for transfers between devices: 20.7 us -> 41 us  [exchange(): return lax.all_to_all(pieces, axis, 0, 0, tiled=True)]
    all_gather x1, blocking collectives: 30.8 us -> 14.6 us  [per_device(): w_near = lax.all_gather(w_bcdt.T, 'tp')]
    all_to_all x4, starting transfers between devices: 40.2 us -> 32.8 us  [exchange(): return lax.all_to_all(pieces, axis, 0, 0, tiled=True)]
  transfers between devices with their start and end apart: 4 -> 4, of which waited for: 3 -> 3; matrix products, arithmetic and copies ran while one was open for 6% -> 7% of each run, Pallas kernels for 0% -> 0%
where the time goes in v8:
time: 112 us; the launch traced here: 111 us
  waiting for transfers between devices  41 us (37%)
  starting transfers between devices  32.8 us (29%)
  blocking collectives  14.6 us (13%)
  Pallas kernels  9.36 us (8%)
  between operations  6.21 us (6%)
  local copies, waits for them, and re-layouts  3.94 us (4%)
  other arithmetic  2.32 us (2%)
    all_to_all x4, waiting for transfers between devices, exchange(): return lax.all_to_all(pieces, axis, 0, 0, tiled=True)  41 us
    all_to_all x4, starting transfers between devices, exchange(): return lax.all_to_all(pieces, axis, 0, 0, tiled=True)  32.8 us
    all_gather x1, blocking collectives, per_device(): w_near = lax.all_gather(w_bcdt.T, 'tp')  14.6 us
    pallas_call x1, Pallas kernels, per_device(): pl.pallas_call(send_kernel, out_shape=jax.ShapeDtypeStruct((n_ctx, STATE_...  3.05 us
    pallas_call x1, Pallas kernels, per_device(): pl.pallas_call(decode_kernel, out_shape=(jax.ShapeDtypeStruct((peers, row...  2.93 us
  transfers between devices with their start and end apart: 4, of which 3 were waited for; matrix products, arithmetic and copies ran while one was open for 7% of the time, Pallas kernels for 0%

profile of v8, /device:TPU:1, one launch (start us, length us, event | category | flops | bytes accessed | tf_op | source)
XLA Modules:
  0.0 111.3 jit_solution(8756834542532759553)
XLA Ops:
  0.8 3.0 %send.1 = bf16[16,304,128]{2,1,0:T(8,128)(2,1)} custom-call(s32[4,16]{1,0:T(4,128)} %tokens_hbm.1, s32[16]{0:T(128)} %prompt_hbm.3, f32[2,32]{1,0:T(2,128)} %bitcast.36, bf16[64,6285]{1,0:T(8,128)(2,1)} %bitcast.27, bf16[2,16,128,128]{3,2,1,0:T(8,128)(2,1)} %bitcast.25), custom_call_target="tpu_custom_call" | custom-call | tf_op jit(solution)/shard_map/send/pallas_call | solution.py:406
  3.8 13.6 %all-to-all-start = ((bf16[16,304,128]{2,1,0:T(8,128)(2,1)}), bf16[16,304,128]{2,1,0:T(8,128)(2,1)S(1)}, u32[]{:S(2)}, u32[]{:S(2)}) async-start(bf16[16,304,128]{2,1,0:T(8,128)(2,1)} %send.1), calls=%async_computation | async-start | bytes 2490368 | tf_op jit(solution)/shard_map/all_to_all | solution.py:28
  18.3 0.1 eq.7
  18.4 0.1 reduce_or.9
  18.6 0.1 reshape.102
  18.8 0.6 pad.12.small_hbm
  19.4 24.2 %all-to-all-done.got_ref = bf16[16,304,128]{2,1,0:T(8,128)(2,1)S(1)} async-done(((bf16[16,304,128]{2,1,0:T(8,128)(2,1)}), bf16[16,304,128]{2,1,0:T(8,128)(2,1)S(1)}, u32[]{:S(2)}, u32[]{:S(2)}) %all-to-all-start) | async-done | bytes 1245216 | tf_op jit(solution)/shard_map/all_to_all | solution.py:28
  43.6 1.7 %combine.1 = bf16[8,208,128]{2,1,0:T(8,128)(2,1)} custom-call(s32[8]{0:T(128)S(1)} %convert_element_type.12.chosen_ref, bf16[16,304,128]{2,1,0:T(8,128)(2,1)S(1)} %all-to-all-done.got_ref, bf16[2,16,128]{2,1,0:T(8,128)(2,1)S(1)} %fusion.6.tails_ref), custom_call_target="tpu_custom_call" | custom-call | tf_op jit(solution)/shard_map/combine/pallas_call | solution.py:463
  45.4 6.9 %all-to-all-start.1 = ((bf16[8,208,128]{2,1,0:T(8,128)(2,1)}), bf16[8,208,128]{2,1,0:T(8,128)(2,1)S(1)}, u32[]{:S(2)}, u32[]{:S(2)}) async-start(bf16[8,208,128]{2,1,0:T(8,128)(2,1)} %combine.1), calls=%async_computation.1 | async-start | bytes 851968 | tf_op jit(solution)/shard_map/all_to_all | solution.py:28
  52.3 0.6 fusion.11
  58.1 14.6 %all-gather.1 = bf16[4,6,4096]{2,1,0:T(8,128)(2,1)S(1)} all-gather(bf16[1,6,4096]{2,1,0:T(8,128)(2,1)S(1)} %bitcast.31), channel_id=2, replica_groups=mesh['ctx'=16,'dp'=8,'tp'=4] {'tp'}, dimensions={0}, use_global_device_ids=true | all-gather | bytes 245760 | tf_op jit(solution)/shard_map/all_gather | solution.py:479
  72.7 0.4 reshape.88
  73.1 0.2 constant_dynamic-slice_fusion.2
  73.4 0.1 reshape.89
  73.6 0.9 columns.1
  74.5 7.5 %all-to-all-start.2 = ((bf16[64,8,128]{2,1,0:T(8,128)(2,1)}), bf16[64,8,128]{2,1,0:T(8,128)(2,1)S(1)}, u32[]{:S(2)}, u32[]{:S(2)}) async-start(bf16[64,8,128]{2,1,0:T(8,128)(2,1)} %columns.1), calls=%async_computation.2 | async-start | bytes 262144 | tf_op jit(solution)/shard_map/all_to_all | solution.py:28
  82.0 2.2 %pad_maximum_fusion.weights_ref = bf16[384,4096]{1,0:T(8,128)(2,1)S(1)} fusion(bf16[128,4096]{1,0:T(8,128)(2,1)} %bitcast.26, bf16[256,4096]{1,0:T(8,128)(2,1)} %bitcast.24), kind=kLoop, calls=%fused_computation | loop fusion | flops 6291456 | bytes 6291456 | tf_op jit(solution)/shard_map/concatenate | solution.py:502
  84.1 0.6 constant_dynamic-slice_fusion.1
  84.8 7.5 %all-to-all-done.2.everyone_ref = bf16[64,8,128]{2,1,0:T(8,128)(2,1)S(1)} async-done(((bf16[64,8,128]{2,1,0:T(8,128)(2,1)}), bf16[64,8,128]{2,1,0:T(8,128)(2,1)S(1)}, u32[]{:S(2)}, u32[]{:S(2)}) %all-to-all-start.2) | async-done | bytes 131104 | tf_op jit(solution)/shard_map/all_to_all | solution.py:28
  92.3 2.9 %decode.1 = (bf16[64,8,128]{2,1,0:T(8,128)(2,1)}, f32[24,128]{1,0:T(8,128)S(1)}) custom-call(bf16[64,8,128]{2,1,0:T(8,128)(2,1)S(1)} %all-to-all-done.2.everyone_ref, bf16[384,4096]{1,0:T(8,128)(2,1)S(1)} %pad_maximum_fusion.weights_ref, bf16[8,208,128]{2,1,0:T(8,128)(2,1)} %copy-done, s32[16]{0:T(128)} %prompt_hbm.3, f32[32,128]{1,0:T(8,128)} %bitcast.30, ...), custom_call_target="tpu_custom_call" | custom-call | tf_op jit(solution)/shard_map/decode/pallas_call | solution.py:506
  95.2 4.9 %all-to-all-start.3 = ((bf16[64,8,128]{2,1,0:T(8,128)(2,1)}), bf16[64,8,128]{2,1,0:T(8,128)(2,1)S(1)}, u32[]{:S(2)}, u32[]{:S(2)}) async-start(bf16[64,8,128]{2,1,0:T(8,128)(2,1)} %get-tuple-element.20), calls=%async_computation.3 | async-start | bytes 262144 | tf_op jit(solution)/shard_map/all_to_all | solution.py:28
  100.2 1.1 convolution_add_fusion
  101.2 9.3 %all-to-all-done.3.incoming_ref = bf16[64,8,128]{2,1,0:T(8,128)(2,1)S(1)} async-done(((bf16[64,8,128]{2,1,0:T(8,128)(2,1)}), bf16[64,8,128]{2,1,0:T(8,128)(2,1)S(1)}, u32[]{:S(2)}, u32[]{:S(2)}) %all-to-all-start.3) | async-done | bytes 131104 | tf_op jit(solution)/shard_map/all_to_all | solution.py:28
  110.5 0.8 finish.1
  (61 shorter events, 1.3 us)
Async XLA Ops:
  0.6 17.7 %copy-start.9 = (s32[16]{0:T(128)S(1)}, s32[16]{0:T(128)}, u32[]{:S(2)}) copy-start(s32[16]{0:T(128)} %prompt_hbm.3) | copy-start | bytes 196
  0.6 16.8 %copy-start.3 = (f32[4096]{0:T(1024)S(1)}, f32[4096]{0:T(1024)}, u32[]{:S(2)}) copy-start(f32[4096]{0:T(1024)} %param.22) | copy-start | bytes 49156
  0.7 16.9 %copy-start.5 = (f32[4,2,64]{2,1,0:T(2,128)S(1)}, f32[4,2,64]{2,1,0:T(2,128)}, u32[]{:S(2)}) copy-start(f32[4,2,64]{2,1,0:T(2,128)} %param.25) | copy-start | bytes 6148
  0.7 17.0 %copy-start.13 = (f32[2]{0:T(128)S(1)}, f32[2]{0:T(128)}, u32[]{:S(2)}) copy-start(f32[2]{0:T(128)} %param.29) | copy-start | bytes 28
  0.7 17.2 %copy-start.14 = (f32[2]{0:T(128)S(1)}, f32[2]{0:T(128)}, u32[]{:S(2)}) copy-start(f32[2]{0:T(128)} %param.30) | copy-start | bytes 28
  0.7 17.3 %copy-start.15 = (f32[2]{0:T(128)S(1)}, f32[2]{0:T(128)}, u32[]{:S(2)}) copy-start(f32[2]{0:T(128)} %param.31) | copy-start | bytes 28
  0.7 17.5 %copy-start.11 = (f32[2,64]{1,0:T(2,128)S(1)}, f32[2,64]{1,0:T(2,128)}, u32[]{:S(2)}) copy-start(f32[2,64]{1,0:T(2,128)} %param.26) | copy-start | bytes 1540
  0.7 17.5 %copy-start.12 = (f32[2,64]{1,0:T(2,128)S(1)}, f32[2,64]{1,0:T(2,128)}, u32[]{:S(2)}) copy-start(f32[2,64]{1,0:T(2,128)} %param.32) | copy-start | bytes 1540
  0.7 17.8 %copy-start.7 = (bf16[2,3,256]{2,0,1:T(2,128)(2,1)S(1)}, bf16[2,3,256]{2,0,1:T(2,128)(2,1)}, u32[]{:S(2)}) copy-start(bf16[2,3,256]{2,0,1:T(2,128)(2,1)} %param.37) | copy-start | bytes 9220
  0.7 17.9 %copy-start.8 = (bf16[2,3,2,64]{3,2,1,0:T(2,128)(2,1)S(1)}, bf16[2,3,2,64]{3,2,1,0:T(2,128)(2,1)}, u32[]{:S(2)}) copy-start(bf16[2,3,2,64]{3,2,1,0:T(2,128)(2,1)} %param.36) | copy-start | bytes 4612
  0.7 18.0 %copy-start.6 = (f32[4,256]{1,0:T(4,128)S(1)}, f32[4,256]{1,0:T(4,128)}, u32[]{:S(2)}) copy-start(f32[4,256]{1,0:T(4,128)} %param.27) | copy-start | bytes 12292
  0.7 18.0 %copy-start.10 = (f32[256]{0:T(256)S(1)}, f32[256]{0:T(256)}, u32[]{:S(2)}) copy-start(f32[256]{0:T(256)} %param.28) | copy-start | bytes 3076
  3.8 54.3 %copy-start.4 = (bf16[4096,6]{0,1:T(8,128)(2,1)S(1)}, bf16[4096,6]{0,1:T(8,128)(2,1)}, u32[]{:S(2)}) copy-start(bf16[4096,6]{0,1:T(8,128)(2,1)} %param.24) | copy-start | bytes 147460
  3.8 39.8 %all-to-all-start = ((bf16[16,304,128]{2,1,0:T(8,128)(2,1)}), bf16[16,304,128]{2,1,0:T(8,128)(2,1)S(1)}, u32[]{:S(2)}, u32[]{:S(2)}) async-start(bf16[16,304,128]{2,1,0:T(8,128)(2,1)} %send.1), calls=%async_computation | async-start | bytes 2490368 | tf_op jit(solution)/shard_map/all_to_all | solution.py:28
  45.4 28.2 %all-to-all-start.1 = ((bf16[8,208,128]{2,1,0:T(8,128)(2,1)}), bf16[8,208,128]{2,1,0:T(8,128)(2,1)S(1)}, u32[]{:S(2)}, u32[]{:S(2)}) async-start(bf16[8,208,128]{2,1,0:T(8,128)(2,1)} %combine.1), calls=%async_computation.1 | async-start | bytes 851968 | tf_op jit(solution)/shard_map/all_to_all | solution.py:28
  73.6 8.4 %copy-start = (bf16[8,208,128]{2,1,0:T(8,128)(2,1)}, bf16[8,208,128]{2,1,0:T(8,128)(2,1)S(1)}, u32[]{:S(2)}) copy-start(bf16[8,208,128]{2,1,0:T(8,128)(2,1)S(1)} %all-to-all-done.1.arrived_ref.arrived_hbm) | copy-start | bytes 1277956
  74.5 17.8 %all-to-all-start.2 = ((bf16[64,8,128]{2,1,0:T(8,128)(2,1)}), bf16[64,8,128]{2,1,0:T(8,128)(2,1)S(1)}, u32[]{:S(2)}, u32[]{:S(2)}) async-start(bf16[64,8,128]{2,1,0:T(8,128)(2,1)} %columns.1), calls=%async_computation.2 | async-start | bytes 262144 | tf_op jit(solution)/shard_map/all_to_all | solution.py:28
  82.0 2.2 %slice-start = ((bf16[8,208,128]{2,1,0:T(8,128)(2,1)}), bf16[8,128,128]{2,1,0:T(8,128)(2,1)S(1)}, s32[]{:S(2)}) async-start(bf16[8,208,128]{2,1,0:T(8,128)(2,1)} %copy-done), calls=%async_computation.4 | async-start | bytes 524288 | tf_op jit(solution)/shard_map/slice | solution.py:540
  84.8 15.4 %copy-start.1 = (bf16[1,128,128]{2,1,0:T(8,128)(2,1)S(1)}, bf16[1,128,128]{2,1,0:T(8,128)(2,1)}, u32[]{:S(2)}) copy-start(bf16[1,128,128]{2,1,0:T(8,128)(2,1)} %get-tuple-element.22) | copy-start | bytes 98308
  84.8 15.4 %copy-start.2 = (bf16[1,128,128]{2,1,0:T(8,128)(2,1)S(1)}, bf16[1,128,128]{2,1,0:T(8,128)(2,1)}, u32[]{:S(2)}) copy-start(bf16[1,128,128]{2,1,0:T(8,128)(2,1)} %get-tuple-element.23) | copy-start | bytes 98308
  95.2 15.3 %all-to-all-start.3 = ((bf16[64,8,128]{2,1,0:T(8,128)(2,1)}), bf16[64,8,128]{2,1,0:T(8,128)(2,1)S(1)}, u32[]{:S(2)}, u32[]{:S(2)}) async-start(bf16[64,8,128]{2,1,0:T(8,128)(2,1)} %get-tuple-element.20), calls=%async_computation.3 | async-start | bytes 262144 | tf_op jit(solution)/shard_map/all_to_all | solution.py:28

commit v9 on v7

--- a/solution.py
+++ b/solution.py
@@ -21,7 +21,7 @@
 SIDE_ROWS = RATE_ROWS + TOKEN_ROWS
 ONE_STATE = 128
 TAIL_ROWS = 16
-NEAR_ROWS = 64
+NEAR_ROWS = 16
 
 
 def exchange(pieces, axis):
@@ -126,28 +126,42 @@
         store.wait()
 
 
-def combine_kernel(chosen_ref, got_ref, tails_ref, out_ref, bundle_ref, near_ref, sems):
+def combine_kernel(
+    chosen_ref, got_ref, tails_ref, gain_ref, weight_ref, out_ref, bundle_ref, near_ref, sems
+):
     count = got_ref.shape[0]
     groups = out_ref.shape[0]
     own_rows = ONE_STATE + TAIL_ROWS
+
     low = low_half((TOKEN_ROWS, LANES))
     at = STATE_ROWS + RATE_ROWS
-    for pair in range(0, count // 2, 2):
-        early, late = [], []
-        for k in (pair, pair + 1):
-            one = got_ref[k, at : at + TOKEN_ROWS, :].astype(F32)
-            two = got_ref[count // 2 + k, at : at + TOKEN_ROWS, :].astype(F32)
-            early.append(jnp.where(low, one, pltpu.roll(two, HALF, 1)))
-            late.append(jnp.where(low, pltpu.roll(one, HALF, 1), two))
-        for g in range(groups):
-            source = early if g < groups // 2 else late
-            r = (g % (groups // 2)) * 8
-            both = jnp.concatenate([s[r : r + 8] for s in source], axis=0)
-            near_ref[g, pair * 8 : pair * 8 + 16, :] = both.astype(BF)
+    pieces = []
+    for k in range(count // 2):
+        one = got_ref[k, at : at + TOKEN_ROWS, :].astype(F32)
+        two = got_ref[count // 2 + k, at : at + TOKEN_ROWS, :].astype(F32)
+        early = jnp.where(low, one, pltpu.roll(two, HALF, 1))
+        late = jnp.where(low, pltpu.roll(one, HALF, 1), two)
+        rows = jnp.concatenate([early, late], axis=0)
+        pieces.append((rows * gain_ref[k : k + 1, :]).astype(BF))
+    partial = lax.dot_general(
+        jnp.concatenate(pieces, axis=1),
+        weight_ref[...],
+        (((1,), (1,)), ((), ())),
+        preferred_element_type=F32,
+    )
+    one = got_ref[lax.axis_index("ctx"), at : at + TOKEN_ROWS, :].astype(F32)
+    own = jnp.concatenate([one, pltpu.roll(one, HALF, 1)], axis=0)
+    lane = lax.broadcasted_iota(jnp.int32, own.shape, 1)
+    first = partial.astype(BF).astype(F32)
+    tiles = jnp.where(lane < HALF, own, jnp.where(lane < HALF + 24, first, partial - first))
+    for g in range(groups):
+        tile = jnp.concatenate([tiles[8 * g : 8 * g + 8], jnp.zeros((8, LANES), F32)], axis=0)
+        near_ref[g] = tile.astype(BF)
     move_near = pltpu.make_async_copy(
         near_ref, out_ref.at[:, own_rows : own_rows + NEAR_ROWS, :], sems.at[groups]
     )
     move_near.start()
+
     rates = []
     for k in range(count):
         parts = got_ref[k, STATE_ROWS : STATE_ROWS + RATE_ROWS, :].astype(F32)
@@ -178,35 +192,19 @@
         move.wait()
 
 
-def columns_kernel(arrived_ref, gain_ref, weight_ref, out_ref, near_ref, tile_ref, sem):
-    groups = arrived_ref.shape[0]
+def spread_kernel(arrived_ref, out_ref, tile_ref, sem):
     at = ONE_STATE + TAIL_ROWS
     total = arrived_ref[0, at : at + NEAR_ROWS, :].astype(F32)
-    for g in range(1, groups):
+    for g in range(1, arrived_ref.shape[0]):
         total = total + arrived_ref[g, at : at + NEAR_ROWS, :].astype(F32)
-    pieces = []
-    for k in range(NEAR_ROWS // 8):
-        rows = total[k * 8 : (k + 1) * 8]
-        near_ref[k] = rows
-        pieces.append((rows * gain_ref[k : k + 1, :]).astype(BF))
-    weighted = jnp.concatenate(pieces, axis=1)
-    partial = lax.dot_general(
-        weighted, weight_ref[...], (((1,), (1,)), ((), ())), preferred_element_type=F32
-    )
-    ctx = lax.axis_index("ctx")
-    half = lax.axis_size("ctx") // 2
-    own = pltpu.roll(near_ref[lax.rem(ctx, half)], ctx // half * HALF, 1)
-    lane = lax.broadcasted_iota(jnp.int32, (8, LANES), 1)
-    first = partial.astype(BF).astype(F32)
-    tile = jnp.where(lane < HALF, own, jnp.where(lane < HALF + 24, first, partial - first))
-    tile_ref[...] = jnp.broadcast_to(tile.astype(BF)[None], tile_ref.shape)
+    tile_ref[...] = jnp.broadcast_to(total[0:8].astype(BF)[None], tile_ref.shape)
     move = pltpu.make_async_copy(tile_ref, out_ref, sem)
     move.start()
     move.wait()
 
 
 def decode_kernel(
-    everyone_ref, weights_ref, arrived_hbm, prompt_hbm, gain_hbm, small_hbm, out_ref, extra_ref,
+    everyone_ref, weights_ref, arrived_hbm, prompt_hbm, gain_hbm, small_hbm, out_ref, start_ref, extra_ref,
     arrived_ref, prompt_ref, gain_ref, small_ref, x_ref, b_ref, c_ref, tile_ref, load_sems, sems,
 ):
     pairs = [(prompt_hbm, prompt_ref), (gain_hbm, gain_ref), (small_hbm, small_ref)]
@@ -300,6 +298,7 @@
     from_start = []
     for slot in range(2):
         state = arrived_ref[slot, 0:ONE_STATE, :]
+        start_ref[slot] = state
         product = lax.dot_general(
             c_parts, state, (((1,), (1,)), ((), ())), preferred_element_type=F32
         )
@@ -445,7 +444,6 @@
     tails = jnp.pad(tails, ((0, 0), (0, TAIL_ROWS - tails.shape[1]), (0, 0)))
     wanted = decode_prompt.reshape(n_dp, slots) - group * slots
     prompt_for = jnp.any(wanted == 1, axis=1).astype(jnp.int32)
-    own_slots = lax.dynamic_slice_in_dim(decode_prompt, group * slots, slots)
 
     def spread(values):
         return jnp.broadcast_to(values[:, None], (heads, HEAD_DIM)).reshape(1, channels)
@@ -466,11 +464,10 @@
     )
     small = jnp.pad(small, ((0, -small.shape[0] % 8), (0, 0)))
 
-    got, w_near, near_gain = lax.optimization_barrier((got, w_near, near_gain))
     routed = pl.pallas_call(
         combine_kernel,
         out_shape=jax.ShapeDtypeStruct((n_dp, ONE_STATE + TAIL_ROWS + NEAR_ROWS, width), BF),
-        in_specs=[SM, VM, VM],
+        in_specs=[SM, VM, VM, VM, VM],
         out_specs=HB,
         scratch_shapes=[
             pltpu.VMEM((slots, ONE_STATE + TAIL_ROWS, width), BF),
@@ -479,36 +476,36 @@
         ],
         compiler_params=PARAMS,
         name="combine",
-    )(prompt_for, got, tails)
+    )(prompt_for, got, tails, near_gain, w_near)
     arrived = exchange(routed, "dp")
 
     piece = pl.pallas_call(
-        columns_kernel,
+        spread_kernel,
         out_shape=jax.ShapeDtypeStruct((peers, rows, LANES), BF),
-        in_specs=[VM, VM, VM],
+        in_specs=[VM],
         out_specs=HB,
         scratch_shapes=[
-            pltpu.VMEM((NEAR_ROWS // 8, 8, LANES), F32),
             pltpu.VMEM((peers, rows, LANES), BF),
             pltpu.SemaphoreType.DMA(()),
         ],
         compiler_params=PARAMS,
-        name="columns",
-    )(arrived, near_gain, w_near)
+        name="spread",
+    )(arrived)
     piece, w_zx, w_out = lax.optimization_barrier((piece, w_zx, w_out))
     everyone = exchange(piece, BOTH)
     weights = jnp.concatenate(
         [w_zx.reshape(2 * channels, model), w_out.reshape(channels, model)], axis=0
     )
 
-    outgoing, extra = pl.pallas_call(
+    outgoing, start, extra = pl.pallas_call(
         decode_kernel,
         out_shape=(
             jax.ShapeDtypeStruct((peers, rows, LANES), BF),
+            jax.ShapeDtypeStruct((slots, ONE_STATE, width), BF),
             jax.ShapeDtypeStruct((24, LANES), F32),
         ),
         in_specs=[VM, VM, HB, HB, HB, HB],
-        out_specs=(HB, VM),
+        out_specs=(HB, VM, VM),
         scratch_shapes=[
             pltpu.VMEM((slots, ONE_STATE + TAIL_ROWS, width), BF),
             pltpu.SMEM(decode_prompt.shape, jnp.int32),
@@ -533,12 +530,6 @@
     )
     incoming = exchange(outgoing, BOTH)
 
-    start = jnp.stack(
-        [
-            lax.dynamic_index_in_dim(arrived[:, :ONE_STATE], own_slots[s] // slots, 0, keepdims=False)
-            for s in range(slots)
-        ]
-    )
     push = extra[0:8].reshape(steps, slots, channels)
     b_conv = extra[8:16].reshape(steps, slots, width)
     kept = extra[16:18]

time: 115 us -> 114 us (level)
  waiting for transfers between devices: 20.7 us -> 26.2 us
  between operations: 6.19 us -> 0.94 us
  local copies, waits for them, and re-layouts: 3.96 us -> 2.65 us
    all_to_all x4, waiting for transfers between devices: 20.7 us -> 26.2 us  [exchange(): return lax.all_to_all(pieces, axis, 0, 0, tiled=True)]
  transfers between devices with their start and end apart: 4 -> 4, of which waited for: 3 -> 3; matrix products, arithmetic and copies ran while one was open for 6% -> 5% of each run, Pallas kernels for 0% -> 0%
where the time goes in v9:
time: 114 us; the launch traced here: 113 us
  starting transfers between devices  39.4 us (35%)
  blocking collectives  30.3 us (27%)
  waiting for transfers between devices  26.2 us (23%)
  Pallas kernels  10.2 us (9%)
  local copies, waits for them, and re-layouts  2.65 us (2%)
  other arithmetic  2.29 us (2%)
    all_to_all x4, starting transfers between devices, exchange(): return lax.all_to_all(pieces, axis, 0, 0, tiled=True)  39.4 us
    all_gather x1, blocking collectives, per_device(): w_near = lax.all_gather(w_bcdt.T, 'tp')  30.3 us
    all_to_all x4, waiting for transfers between devices, exchange(): return lax.all_to_all(pieces, axis, 0, 0, tiled=True)  26.2 us
    pallas_call x1, Pallas kernels, per_device(): pl.pallas_call(decode_kernel, out_shape=(jax.ShapeDtypeStruct((peers, row...  3.85 us
    pallas_call x1, Pallas kernels, per_device(): pl.pallas_call(send_kernel, out_shape=jax.ShapeDtypeStruct((n_ctx, STATE_...  3.05 us
  transfers between devices with their start and end apart: 4, of which 3 were waited for; matrix products, arithmetic and copies ran while one was open for 5% of the time, Pallas kernels for 0%

profile of v9, /device:TPU:1, one launch (start us, length us, event | category | flops | bytes accessed | tf_op | source)
XLA Modules:
  0.0 113.1 jit_solution(5917745547412183730)
XLA Ops:
  0.7 3.1 %send.1 = bf16[16,304,128]{2,1,0:T(8,128)(2,1)} custom-call(s32[4,16]{1,0:T(4,128)} %tokens_hbm.1, s32[16]{0:T(128)} %prompt_hbm.3, f32[2,32]{1,0:T(2,128)} %bitcast.34, bf16[64,6285]{1,0:T(8,128)(2,1)} %bitcast.25, bf16[2,16,128,128]{3,2,1,0:T(8,128)(2,1)} %bitcast.23), custom_call_target="tpu_custom_call" | custom-call | tf_op jit(solution)/shard_map/send/pallas_call | solution.py:405
  3.8 13.6 %all-to-all-start = ((bf16[16,304,128]{2,1,0:T(8,128)(2,1)}), bf16[16,304,128]{2,1,0:T(8,128)(2,1)S(1)}, u32[]{:S(2)}, u32[]{:S(2)}) async-start(bf16[16,304,128]{2,1,0:T(8,128)(2,1)} %send.1), calls=%async_computation | async-start | bytes 2490368 | tf_op jit(solution)/shard_map/all_to_all | solution.py:28
  17.4 0.1 eq.7
  17.5 0.1 reduce_or.9
  17.7 0.1 reshape.102
  18.0 30.3 %all-gather.1 = bf16[4,6,4096]{2,1,0:T(8,128)(2,1)S(1)} all-gather(bf16[1,6,4096]{2,1,0:T(8,128)(2,1)S(1)} %bitcast.29), channel_id=2, replica_groups=mesh['ctx'=16,'dp'=8,'tp'=4] {'tp'}, dimensions={0}, use_global_device_ids=true | all-gather | bytes 245760 | tf_op jit(solution)/shard_map/all_gather | solution.py:433
  48.3 0.4 reshape.81
  48.7 0.2 constant_dynamic-slice_fusion
  49.1 0.1 reshape.82
  49.2 1.8 %combine.1 = bf16[8,160,128]{2,1,0:T(8,128)(2,1)} custom-call(s32[8]{0:T(128)S(1)} %convert_element_type.12.chosen_ref, bf16[16,304,128]{2,1,0:T(8,128)(2,1)S(1)} %all-to-all-done.got_ref, bf16[2,16,128]{2,1,0:T(8,128)(2,1)S(1)} %fusion.6.tails_ref, f32[8,128]{1,0:T(8,128)S(1)} %reshape.80.gain_ref, bf16[128,1024]{1,0:T(8,128)(2,1)S(1)} %fusion.3.weight_ref), custom_call_target="tpu_custom_call" | custom-call | tf_op jit(solution)/shard_map/combine/pallas_call | solution.py:467
  51.1 6.8 %all-to-all-start.1 = ((bf16[8,160,128]{2,1,0:T(8,128)(2,1)}), bf16[8,160,128]{2,1,0:T(8,128)(2,1)S(1)}, u32[]{:S(2)}, u32[]{:S(2)}) async-start(bf16[8,160,128]{2,1,0:T(8,128)(2,1)} %combine.1), calls=%async_computation.1 | async-start | bytes 655360 | tf_op jit(solution)/shard_map/all_to_all | solution.py:28
  58.2 0.1 reshape.89
  58.3 0.1 reshape.90
  58.7 0.6 pad.14.small_hbm
  59.3 8.7 %all-to-all-done.1.arrived_ref.arrived_hbm = bf16[8,160,128]{2,1,0:T(8,128)(2,1)S(1)} async-done(((bf16[8,160,128]{2,1,0:T(8,128)(2,1)}), bf16[8,160,128]{2,1,0:T(8,128)(2,1)S(1)}, u32[]{:S(2)}, u32[]{:S(2)}) %all-to-all-start.1) | async-done | bytes 327712 | tf_op jit(solution)/shard_map/all_to_all | solution.py:28
  68.0 0.7 spread.1
  68.8 14.2 %all-to-all-start.2 = ((bf16[64,8,128]{2,1,0:T(8,128)(2,1)}), bf16[64,8,128]{2,1,0:T(8,128)(2,1)}, u32[]{:S(2)}, u32[]{:S(2)}) async-start(bf16[64,8,128]{2,1,0:T(8,128)(2,1)} %spread.1), calls=%async_computation.2 | async-start | bytes 262144 | tf_op jit(solution)/shard_map/all_to_all | solution.py:28
  82.9 2.1 %pad_maximum_fusion.weights_ref = bf16[384,4096]{1,0:T(8,128)(2,1)S(1)} fusion(bf16[128,4096]{1,0:T(8,128)(2,1)} %bitcast.24, bf16[256,4096]{1,0:T(8,128)(2,1)} %bitcast.22), kind=kLoop, calls=%fused_computation | loop fusion | flops 6291456 | bytes 6291456 | tf_op jit(solution)/shard_map/concatenate | solution.py:496
  85.1 8.1 %all-to-all-done.2.everyone_ref = bf16[64,8,128]{2,1,0:T(8,128)(2,1)} async-done(((bf16[64,8,128]{2,1,0:T(8,128)(2,1)}), bf16[64,8,128]{2,1,0:T(8,128)(2,1)}, u32[]{:S(2)}, u32[]{:S(2)}) %all-to-all-start.2) | async-done | bytes 131104 | tf_op jit(solution)/shard_map/all_to_all | solution.py:28
  93.2 3.8 %decode.1 = (bf16[64,8,128]{2,1,0:T(8,128)(2,1)}, bf16[2,128,128]{2,1,0:T(8,128)(2,1)S(1)}, f32[24,128]{1,0:T(8,128)S(1)}) custom-call(bf16[64,8,128]{2,1,0:T(8,128)(2,1)} %all-to-all-done.2.everyone_ref, bf16[384,4096]{1,0:T(8,128)(2,1)S(1)} %pad_maximum_fusion.weights_ref, bf16[8,160,128]{2,1,0:T(8,128)(2,1)} %copy-done, s32[16]{0:T(128)} %prompt_hbm.3, ...), custom_call_target="tpu_custom_call" | custom-call | tf_op jit(solution)/shard_map/decode/pallas_call | solution.py:500
  97.1 4.9 %all-to-all-start.3 = ((bf16[64,8,128]{2,1,0:T(8,128)(2,1)}), bf16[64,8,128]{2,1,0:T(8,128)(2,1)S(1)}, u32[]{:S(2)}, u32[]{:S(2)}) async-start(bf16[64,8,128]{2,1,0:T(8,128)(2,1)} %get-tuple-element.11), calls=%async_computation.3 | async-start | bytes 262144 | tf_op jit(solution)/shard_map/all_to_all | solution.py:28
  102.0 1.1 convolution_add_fusion
  103.0 9.3 %all-to-all-done.3.incoming_ref = bf16[64,8,128]{2,1,0:T(8,128)(2,1)S(1)} async-done(((bf16[64,8,128]{2,1,0:T(8,128)(2,1)}), bf16[64,8,128]{2,1,0:T(8,128)(2,1)S(1)}, u32[]{:S(2)}, u32[]{:S(2)}) %all-to-all-start.3) | async-done | bytes 131104 | tf_op jit(solution)/shard_map/all_to_all | solution.py:28
  112.3 0.8 finish.1
  (52 shorter events, 1.0 us)
Async XLA Ops:
  0.6 16.8 %copy-start.7 = (s32[16]{0:T(128)S(1)}, s32[16]{0:T(128)}, u32[]{:S(2)}) copy-start(s32[16]{0:T(128)} %prompt_hbm.3) | copy-start | bytes 196
  0.6 17.0 %copy-start.6 = (bf16[2,3,2,64]{3,2,1,0:T(2,128)(2,1)S(1)}, bf16[2,3,2,64]{3,2,1,0:T(2,128)(2,1)}, u32[]{:S(2)}) copy-start(bf16[2,3,2,64]{3,2,1,0:T(2,128)(2,1)} %param.36) | copy-start | bytes 4612
  0.7 17.1 %copy-start.5 = (bf16[2,3,256]{2,0,1:T(2,128)(2,1)S(1)}, bf16[2,3,256]{2,0,1:T(2,128)(2,1)}, u32[]{:S(2)}) copy-start(bf16[2,3,256]{2,0,1:T(2,128)(2,1)} %param.37) | copy-start | bytes 9220
  0.7 17.1 %copy-start.1 = (f32[4096]{0:T(1024)S(1)}, f32[4096]{0:T(1024)}, u32[]{:S(2)}) copy-start(f32[4096]{0:T(1024)} %param.22) | copy-start | bytes 49156
  0.7 17.3 %copy-start.2 = (bf16[4096,6]{0,1:T(8,128)(2,1)S(1)}, bf16[4096,6]{0,1:T(8,128)(2,1)}, u32[]{:S(2)}) copy-start(bf16[4096,6]{0,1:T(8,128)(2,1)} %param.24) | copy-start | bytes 147460
  3.7 54.2 %copy-start.9 = (f32[2,64]{1,0:T(2,128)S(1)}, f32[2,64]{1,0:T(2,128)}, u32[]{:S(2)}) copy-start(f32[2,64]{1,0:T(2,128)} %param.26) | copy-start | bytes 1540
  3.8 54.2 %copy-start.10 = (f32[2,64]{1,0:T(2,128)S(1)}, f32[2,64]{1,0:T(2,128)}, u32[]{:S(2)}) copy-start(f32[2,64]{1,0:T(2,128)} %param.32) | copy-start | bytes 1540
  3.8 54.3 %copy-start.11 = (f32[2]{0:T(128)S(1)}, f32[2]{0:T(128)}, u32[]{:S(2)}) copy-start(f32[2]{0:T(128)} %param.29) | copy-start | bytes 28
  3.8 54.5 %copy-start.12 = (f32[2]{0:T(128)S(1)}, f32[2]{0:T(128)}, u32[]{:S(2)}) copy-start(f32[2]{0:T(128)} %param.30) | copy-start | bytes 28
  3.8 54.6 %copy-start.13 = (f32[2]{0:T(128)S(1)}, f32[2]{0:T(128)}, u32[]{:S(2)}) copy-start(f32[2]{0:T(128)} %param.31) | copy-start | bytes 28
  3.8 54.7 %copy-start.3 = (f32[4,2,64]{2,1,0:T(2,128)S(1)}, f32[4,2,64]{2,1,0:T(2,128)}, u32[]{:S(2)}) copy-start(f32[4,2,64]{2,1,0:T(2,128)} %param.25) | copy-start | bytes 6148
  3.8 54.8 %copy-start.4 = (f32[4,256]{1,0:T(4,128)S(1)}, f32[4,256]{1,0:T(4,128)}, u32[]{:S(2)}) copy-start(f32[4,256]{1,0:T(4,128)} %param.27) | copy-start | bytes 12292
  3.8 54.8 %copy-start.8 = (f32[256]{0:T(256)S(1)}, f32[256]{0:T(256)}, u32[]{:S(2)}) copy-start(f32[256]{0:T(256)} %param.28) | copy-start | bytes 3076
  3.8 45.4 %all-to-all-start = ((bf16[16,304,128]{2,1,0:T(8,128)(2,1)}), bf16[16,304,128]{2,1,0:T(8,128)(2,1)S(1)}, u32[]{:S(2)}, u32[]{:S(2)}) async-start(bf16[16,304,128]{2,1,0:T(8,128)(2,1)} %send.1), calls=%async_computation | async-start | bytes 2490368 | tf_op jit(solution)/shard_map/all_to_all | solution.py:28
  51.1 17.0 %all-to-all-start.1 = ((bf16[8,160,128]{2,1,0:T(8,128)(2,1)}), bf16[8,160,128]{2,1,0:T(8,128)(2,1)S(1)}, u32[]{:S(2)}, u32[]{:S(2)}) async-start(bf16[8,160,128]{2,1,0:T(8,128)(2,1)} %combine.1), calls=%async_computation.1 | async-start | bytes 655360 | tf_op jit(solution)/shard_map/all_to_all | solution.py:28
  68.0 17.0 %copy-start = (bf16[8,160,128]{2,1,0:T(8,128)(2,1)}, bf16[8,160,128]{2,1,0:T(8,128)(2,1)S(1)}, u32[]{:S(2)}) copy-start(bf16[8,160,128]{2,1,0:T(8,128)(2,1)S(1)} %all-to-all-done.1.arrived_ref.arrived_hbm) | copy-start | bytes 983044
  68.8 24.4 %all-to-all-start.2 = ((bf16[64,8,128]{2,1,0:T(8,128)(2,1)}), bf16[64,8,128]{2,1,0:T(8,128)(2,1)}, u32[]{:S(2)}, u32[]{:S(2)}) async-start(bf16[64,8,128]{2,1,0:T(8,128)(2,1)} %spread.1), calls=%async_computation.2 | async-start | bytes 262144 | tf_op jit(solution)/shard_map/all_to_all | solution.py:28
  97.1 15.3 %all-to-all-start.3 = ((bf16[64,8,128]{2,1,0:T(8,128)(2,1)}), bf16[64,8,128]{2,1,0:T(8,128)(2,1)S(1)}, u32[]{:S(2)}, u32[]{:S(2)}) async-start(bf16[64,8,128]{2,1,0:T(8,128)(2,1)} %get-tuple-element.11), calls=%async_computation.3 | async-start | bytes 262144 | tf_op jit(solution)/shard_map/all_to_all | solution.py:28

commit v10 on v8

--- a/solution.py
+++ b/solution.py
@@ -206,7 +206,7 @@
 
 
 def decode_kernel(
-    everyone_ref, weights_ref, arrived_hbm, prompt_hbm, gain_hbm, small_hbm, out_ref, extra_ref,
+    everyone_ref, weights_ref, arrived_hbm, prompt_hbm, gain_hbm, small_hbm, out_ref, start_ref, extra_ref,
     arrived_ref, prompt_ref, gain_ref, small_ref, x_ref, b_ref, c_ref, tile_ref, load_sems, sems,
 ):
     pairs = [(prompt_hbm, prompt_ref), (gain_hbm, gain_ref), (small_hbm, small_ref)]
@@ -300,6 +300,7 @@
     from_start = []
     for slot in range(2):
         state = arrived_ref[slot, 0:ONE_STATE, :]
+        start_ref[slot] = state
         product = lax.dot_general(
             c_parts, state, (((1,), (1,)), ((), ())), preferred_element_type=F32
         )
@@ -438,7 +439,6 @@
     tails = jnp.pad(tails, ((0, 0), (0, TAIL_ROWS - tails.shape[1]), (0, 0)))
     wanted = decode_prompt.reshape(n_dp, slots) - group * slots
     prompt_for = jnp.any(wanted == 1, axis=1).astype(jnp.int32)
-    own_slots = lax.dynamic_slice_in_dim(decode_prompt, group * slots, slots)
 
     def spread(values):
         return jnp.broadcast_to(values[:, None], (heads, HEAD_DIM)).reshape(1, channels)
@@ -503,14 +503,15 @@
         [w_zx.reshape(2 * channels, model), w_out.reshape(channels, model)], axis=0
     )
 
-    outgoing, extra = pl.pallas_call(
+    outgoing, start, extra = pl.pallas_call(
         decode_kernel,
         out_shape=(
             jax.ShapeDtypeStruct((peers, rows, LANES), BF),
+            jax.ShapeDtypeStruct((slots, ONE_STATE, width), BF),
             jax.ShapeDtypeStruct((24, LANES), F32),
         ),
         in_specs=[VM, VM, HB, HB, HB, HB],
-        out_specs=(HB, VM),
+        out_specs=(HB, VM, VM),
         scratch_shapes=[
             pltpu.VMEM((slots, ONE_STATE + TAIL_ROWS, width), BF),
             pltpu.SMEM(decode_prompt.shape, jnp.int32),
@@ -535,12 +536,6 @@
     )
     incoming = exchange(outgoing, BOTH)
 
-    start = jnp.stack(
-        [
-            lax.dynamic_index_in_dim(arrived[:, :ONE_STATE], own_slots[s] // slots, 0, keepdims=False)
-            for s in range(slots)
-        ]
-    )
     push = extra[0:8].reshape(steps, slots, channels)
     b_conv = extra[8:16].reshape(steps, slots, width)
     kept = extra[16:18]

time: 112 us -> 112 us (level)
  starting transfers between devices: 32.8 us -> 38.5 us
  between operations: 6.21 us -> 0.94 us
  local copies, waits for them, and re-layouts: 3.94 us -> 2.64 us
    all_to_all x4, starting transfers between devices: 32.8 us -> 38.5 us  [exchange(): return lax.all_to_all(pieces, axis, 0, 0, tiled=True)]
  transfers between devices with their start and end apart: 4 -> 4, of which waited for: 3 -> 3; matrix products, arithmetic and copies ran while one was open for 7% -> 5% of each run, Pallas kernels for 0% -> 0%
where the time goes in v10:
time: 112 us; the launch traced here: 111 us
  waiting for transfers between devices  41.9 us (37%)
  starting transfers between devices  38.5 us (34%)
  blocking collectives  14.6 us (13%)
  Pallas kernels  9.42 us (8%)
  local copies, waits for them, and re-layouts  2.64 us (2%)
  other arithmetic  2.29 us (2%)
    all_to_all x4, waiting for transfers between devices, exchange(): return lax.all_to_all(pieces, axis, 0, 0, tiled=True)  41.9 us
    all_to_all x4, starting transfers between devices, exchange(): return lax.all_to_all(pieces, axis, 0, 0, tiled=True)  38.5 us
    all_gather x1, blocking collectives, per_device(): w_near = lax.all_gather(w_bcdt.T, 'tp')  14.6 us
    pallas_call x1, Pallas kernels, per_device(): pl.pallas_call(send_kernel, out_shape=jax.ShapeDtypeStruct((n_ctx, STATE_...  3.11 us
    pallas_call x1, Pallas kernels, per_device(): pl.pallas_call(decode_kernel, out_shape=(jax.ShapeDtypeStruct((peers, row...  2.94 us
  transfers between devices with their start and end apart: 4, of which 3 were waited for; matrix products, arithmetic and copies ran while one was open for 5% of the time, Pallas kernels for 0%

profile of v10, /device:TPU:1, one launch (start us, length us, event | category | flops | bytes accessed | tf_op | source)
XLA Modules:
  0.0 111.4 jit_solution(17806219341733860542)
XLA Ops:
  0.8 3.1 %send.1 = bf16[16,304,128]{2,1,0:T(8,128)(2,1)} custom-call(s32[4,16]{1,0:T(4,128)} %tokens_hbm.1, s32[16]{0:T(128)} %prompt_hbm.3, f32[2,32]{1,0:T(2,128)} %bitcast.34, bf16[64,6285]{1,0:T(8,128)(2,1)} %bitcast.25, bf16[2,16,128,128]{3,2,1,0:T(8,128)(2,1)} %bitcast.23), custom_call_target="tpu_custom_call" | custom-call | tf_op jit(solution)/shard_map/send/pallas_call | solution.py:407
  3.9 13.6 %all-to-all-start = ((bf16[16,304,128]{2,1,0:T(8,128)(2,1)}), bf16[16,304,128]{2,1,0:T(8,128)(2,1)S(1)}, u32[]{:S(2)}, u32[]{:S(2)}) async-start(bf16[16,304,128]{2,1,0:T(8,128)(2,1)} %send.1), calls=%async_computation | async-start | bytes 2490368 | tf_op jit(solution)/shard_map/all_to_all | solution.py:28
  17.7 0.1 eq.7
  17.7 0.1 reduce_or.9
  18.0 0.1 reshape.82
  18.1 0.1 reshape.83
  18.4 0.1 reshape.102
  18.8 0.6 pad.12.small_hbm
  19.4 24.4 %all-to-all-done.got_ref = bf16[16,304,128]{2,1,0:T(8,128)(2,1)S(1)} async-done(((bf16[16,304,128]{2,1,0:T(8,128)(2,1)}), bf16[16,304,128]{2,1,0:T(8,128)(2,1)S(1)}, u32[]{:S(2)}, u32[]{:S(2)}) %all-to-all-start) | async-done | bytes 1245216 | tf_op jit(solution)/shard_map/all_to_all | solution.py:28
  43.8 1.7 %combine.1 = bf16[8,208,128]{2,1,0:T(8,128)(2,1)} custom-call(s32[8]{0:T(128)S(1)} %convert_element_type.12.chosen_ref, bf16[16,304,128]{2,1,0:T(8,128)(2,1)S(1)} %all-to-all-done.got_ref, bf16[2,16,128]{2,1,0:T(8,128)(2,1)S(1)} %fusion.6.tails_ref), custom_call_target="tpu_custom_call" | custom-call | tf_op jit(solution)/shard_map/combine/pallas_call | solution.py:463
  45.6 6.7 %all-to-all-start.1 = ((bf16[8,208,128]{2,1,0:T(8,128)(2,1)}), bf16[8,208,128]{2,1,0:T(8,128)(2,1)S(1)}, u32[]{:S(2)}, u32[]{:S(2)}) async-start(bf16[8,208,128]{2,1,0:T(8,128)(2,1)} %combine.1), calls=%async_computation.1 | async-start | bytes 851968 | tf_op jit(solution)/shard_map/all_to_all | solution.py:28
  52.3 14.6 %all-gather.1 = bf16[4,6,4096]{2,1,0:T(8,128)(2,1)S(1)} all-gather(bf16[1,6,4096]{2,1,0:T(8,128)(2,1)S(1)} %bitcast.29), channel_id=2, replica_groups=mesh['ctx'=16,'dp'=8,'tp'=4] {'tp'}, dimensions={0}, use_global_device_ids=true | all-gather | bytes 245760 | tf_op jit(solution)/shard_map/all_gather | solution.py:479
  66.9 0.4 reshape.88
  67.3 0.2 constant_dynamic-slice_fusion
  67.6 0.1 reshape.89
  67.8 0.9 columns.1
  68.6 13.3 %all-to-all-start.2 = ((bf16[64,8,128]{2,1,0:T(8,128)(2,1)}), bf16[64,8,128]{2,1,0:T(8,128)(2,1)S(1)}, u32[]{:S(2)}, u32[]{:S(2)}) async-start(bf16[64,8,128]{2,1,0:T(8,128)(2,1)} %columns.1), calls=%async_computation.2 | async-start | bytes 262144 | tf_op jit(solution)/shard_map/all_to_all | solution.py:28
  82.0 2.1 %pad_maximum_fusion.weights_ref = bf16[384,4096]{1,0:T(8,128)(2,1)S(1)} fusion(bf16[128,4096]{1,0:T(8,128)(2,1)} %bitcast.24, bf16[256,4096]{1,0:T(8,128)(2,1)} %bitcast.22), kind=kLoop, calls=%fused_computation | loop fusion | flops 6291456 | bytes 6291456 | tf_op jit(solution)/shard_map/concatenate | solution.py:502
  84.1 8.2 %all-to-all-done.2.everyone_ref = bf16[64,8,128]{2,1,0:T(8,128)(2,1)S(1)} async-done(((bf16[64,8,128]{2,1,0:T(8,128)(2,1)}), bf16[64,8,128]{2,1,0:T(8,128)(2,1)S(1)}, u32[]{:S(2)}, u32[]{:S(2)}) %all-to-all-start.2) | async-done | bytes 131104 | tf_op jit(solution)/shard_map/all_to_all | solution.py:28
  92.4 2.9 %decode.1 = (bf16[64,8,128]{2,1,0:T(8,128)(2,1)}, bf16[2,128,128]{2,1,0:T(8,128)(2,1)S(1)}, f32[24,128]{1,0:T(8,128)S(1)}) custom-call(bf16[64,8,128]{2,1,0:T(8,128)(2,1)S(1)} %all-to-all-done.2.everyone_ref, bf16[384,4096]{1,0:T(8,128)(2,1)S(1)} %pad_maximum_fusion.weights_ref, bf16[8,208,128]{2,1,0:T(8,128)(2,1)} %copy-done, s32[16]{0:T(128)} %prompt_hbm.3, ...), custom_call_target="tpu_custom_call" | custom-call | tf_op jit(solution)/shard_map/decode/pallas_call | solution.py:506
  95.3 4.9 %all-to-all-start.3 = ((bf16[64,8,128]{2,1,0:T(8,128)(2,1)}), bf16[64,8,128]{2,1,0:T(8,128)(2,1)S(1)}, u32[]{:S(2)}, u32[]{:S(2)}) async-start(bf16[64,8,128]{2,1,0:T(8,128)(2,1)} %get-tuple-element.21), calls=%async_computation.3 | async-start | bytes 262144 | tf_op jit(solution)/shard_map/all_to_all | solution.py:28
  100.2 1.1 convolution_add_fusion
  101.3 9.3 %all-to-all-done.3.incoming_ref = bf16[64,8,128]{2,1,0:T(8,128)(2,1)S(1)} async-done(((bf16[64,8,128]{2,1,0:T(8,128)(2,1)}), bf16[64,8,128]{2,1,0:T(8,128)(2,1)S(1)}, u32[]{:S(2)}, u32[]{:S(2)}) %all-to-all-start.3) | async-done | bytes 131104 | tf_op jit(solution)/shard_map/all_to_all | solution.py:28
  110.6 0.8 finish.1
  (52 shorter events, 1.0 us)
Async XLA Ops:
  0.6 17.0 %copy-start.7 = (s32[16]{0:T(128)S(1)}, s32[16]{0:T(128)}, u32[]{:S(2)}) copy-start(s32[16]{0:T(128)} %prompt_hbm.3) | copy-start | bytes 196
  0.6 16.8 %copy-start.9 = (f32[2,64]{1,0:T(2,128)S(1)}, f32[2,64]{1,0:T(2,128)}, u32[]{:S(2)}) copy-start(f32[2,64]{1,0:T(2,128)} %param.26) | copy-start | bytes 1540
  0.7 16.9 %copy-start.10 = (f32[2,64]{1,0:T(2,128)S(1)}, f32[2,64]{1,0:T(2,128)}, u32[]{:S(2)}) copy-start(f32[2,64]{1,0:T(2,128)} %param.32) | copy-start | bytes 1540
  0.7 17.2 %copy-start.11 = (f32[2]{0:T(128)S(1)}, f32[2]{0:T(128)}, u32[]{:S(2)}) copy-start(f32[2]{0:T(128)} %param.29) | copy-start | bytes 28
  0.7 17.4 %copy-start.12 = (f32[2]{0:T(128)S(1)}, f32[2]{0:T(128)}, u32[]{:S(2)}) copy-start(f32[2]{0:T(128)} %param.30) | copy-start | bytes 28
  0.7 17.5 %copy-start.13 = (f32[2]{0:T(128)S(1)}, f32[2]{0:T(128)}, u32[]{:S(2)}) copy-start(f32[2]{0:T(128)} %param.31) | copy-start | bytes 28
  0.7 17.7 %copy-start.3 = (f32[4,2,64]{2,1,0:T(2,128)S(1)}, f32[4,2,64]{2,1,0:T(2,128)}, u32[]{:S(2)}) copy-start(f32[4,2,64]{2,1,0:T(2,128)} %param.25) | copy-start | bytes 6148
  0.7 17.7 %copy-start.6 = (bf16[2,3,2,64]{3,2,1,0:T(2,128)(2,1)S(1)}, bf16[2,3,2,64]{3,2,1,0:T(2,128)(2,1)}, u32[]{:S(2)}) copy-start(bf16[2,3,2,64]{3,2,1,0:T(2,128)(2,1)} %param.36) | copy-start | bytes 4612
  0.7 17.8 %copy-start.5 = (bf16[2,3,256]{2,0,1:T(2,128)(2,1)S(1)}, bf16[2,3,256]{2,0,1:T(2,128)(2,1)}, u32[]{:S(2)}) copy-start(bf16[2,3,256]{2,0,1:T(2,128)(2,1)} %param.37) | copy-start | bytes 9220
  0.7 17.8 %copy-start.1 = (f32[4096]{0:T(1024)S(1)}, f32[4096]{0:T(1024)}, u32[]{:S(2)}) copy-start(f32[4096]{0:T(1024)} %param.22) | copy-start | bytes 49156
  0.7 18.0 %copy-start.4 = (f32[4,256]{1,0:T(4,128)S(1)}, f32[4,256]{1,0:T(4,128)}, u32[]{:S(2)}) copy-start(f32[4,256]{1,0:T(4,128)} %param.27) | copy-start | bytes 12292
  0.7 18.0 %copy-start.8 = (f32[256]{0:T(256)S(1)}, f32[256]{0:T(256)}, u32[]{:S(2)}) copy-start(f32[256]{0:T(256)} %param.28) | copy-start | bytes 3076
  3.9 48.4 %copy-start.2 = (bf16[4096,6]{0,1:T(8,128)(2,1)S(1)}, bf16[4096,6]{0,1:T(8,128)(2,1)}, u32[]{:S(2)}) copy-start(bf16[4096,6]{0,1:T(8,128)(2,1)} %param.24) | copy-start | bytes 147460
  3.9 40.0 %all-to-all-start = ((bf16[16,304,128]{2,1,0:T(8,128)(2,1)}), bf16[16,304,128]{2,1,0:T(8,128)(2,1)S(1)}, u32[]{:S(2)}, u32[]{:S(2)}) async-start(bf16[16,304,128]{2,1,0:T(8,128)(2,1)} %send.1), calls=%async_computation | async-start | bytes 2490368 | tf_op jit(solution)/shard_map/all_to_all | solution.py:28
  45.6 22.2 %all-to-all-start.1 = ((bf16[8,208,128]{2,1,0:T(8,128)(2,1)}), bf16[8,208,128]{2,1,0:T(8,128)(2,1)S(1)}, u32[]{:S(2)}, u32[]{:S(2)}) async-start(bf16[8,208,128]{2,1,0:T(8,128)(2,1)} %combine.1), calls=%async_computation.1 | async-start | bytes 851968 | tf_op jit(solution)/shard_map/all_to_all | solution.py:28
  67.8 14.2 %copy-start = (bf16[8,208,128]{2,1,0:T(8,128)(2,1)}, bf16[8,208,128]{2,1,0:T(8,128)(2,1)S(1)}, u32[]{:S(2)}) copy-start(bf16[8,208,128]{2,1,0:T(8,128)(2,1)S(1)} %all-to-all-done.1.arrived_ref.arrived_hbm) | copy-start | bytes 1277956
  68.6 23.7 %all-to-all-start.2 = ((bf16[64,8,128]{2,1,0:T(8,128)(2,1)}), bf16[64,8,128]{2,1,0:T(8,128)(2,1)S(1)}, u32[]{:S(2)}, u32[]{:S(2)}) async-start(bf16[64,8,128]{2,1,0:T(8,128)(2,1)} %columns.1), calls=%async_computation.2 | async-start | bytes 262144 | tf_op jit(solution)/shard_map/all_to_all | solution.py:28
  95.3 15.3 %all-to-all-start.3 = ((bf16[64,8,128]{2,1,0:T(8,128)(2,1)}), bf16[64,8,128]{2,1,0:T(8,128)(2,1)S(1)}, u32[]{:S(2)}, u32[]{:S(2)}) async-start(bf16[64,8,128]{2,1,0:T(8,128)(2,1)} %get-tuple-element.21), calls=%async_computation.3 | async-start | bytes 262144 | tf_op jit(solution)/shard_map/all_to_all | solution.py:28

commit v11 on v9

--- a/solution.py
+++ b/solution.py
@@ -430,11 +430,16 @@
     )
     got = exchange(sent, "ctx")
 
-    w_near = lax.all_gather(w_bcdt.T, "tp")
     own_columns = n_tp * w_bcdt.shape[1]
-    w_near = w_near.reshape(own_columns, 2, n_ctx // 2, n_tp, features)
-    w_near = lax.dynamic_index_in_dim(w_near, tp, 3, keepdims=False)
-    w_near = jnp.swapaxes(w_near, 1, 2).reshape(own_columns, -1)
+    quarters = w_bcdt.T.reshape(-1, 2, n_ctx // 2, n_tp, features)
+    quarters = jnp.transpose(quarters, (3, 0, 2, 1, 4)).reshape(n_tp, w_bcdt.shape[1], -1)
+    w_near = jnp.zeros_like(quarters)
+    for step in range(n_tp):
+        piece = lax.dynamic_index_in_dim(quarters, (tp + step) % n_tp, 0, keepdims=True)
+        if step:
+            piece = lax.ppermute(piece, "tp", [(t, (t + step) % n_tp) for t in range(n_tp)])
+        w_near = lax.dynamic_update_slice_in_dim(w_near, piece, (tp - step) % n_tp, 0)
+    w_near = w_near.reshape(own_columns, -1)
     w_near = jnp.concatenate([w_near, w_near], axis=0)
     w_near = jnp.pad(w_near, ((HALF, LANES - HALF - 2 * own_columns), (0, 0)))
     near_gain = norm_gain.reshape(2, n_ctx // 2, n_tp, features)

time: 114 us -> 111 us (0.974)
  blocking collectives: 30.3 us -> 0 us
  waiting for transfers between devices: 26.2 us -> 45.1 us
  starting transfers between devices: 39.4 us -> 48.3 us
    all_gather x1 -> x0, blocking collectives: 30.3 us -> none  [per_device(): w_near = lax.all_gather(w_bcdt.T, 'tp')]
    ppermute x0 -> x3, waiting for transfers between devices: none -> 19 us  [per_device(): lax.ppermute(piece, 'tp', [(t, (t + step) % n_tp) for t in range(n_tp)])]
    ppermute x0 -> x3, starting transfers between devices: none -> 8.94 us  [per_device(): lax.ppermute(piece, 'tp', [(t, (t + step) % n_tp) for t in range(n_tp)])]
  transfers between devices with their start and end apart: 4 -> 7, of which waited for: 3 -> 6; matrix products, arithmetic and copies ran while one was open for 5% -> 5% of each run, Pallas kernels for 0% -> 0%
where the time goes in v11:
time: 111 us; the launch traced here: 110 us
  starting transfers between devices  48.3 us (44%)
  waiting for transfers between devices  45.1 us (41%)
  Pallas kernels  10.2 us (9%)
  local copies, waits for them, and re-layouts  2.32 us (2%)
  other arithmetic  2.29 us (2%)
  between operations  1.13 us (1%)
    all_to_all x4, starting transfers between devices, exchange(): return lax.all_to_all(pieces, axis, 0, 0, tiled=True)  39.4 us
    all_to_all x4, waiting for transfers between devices, exchange(): return lax.all_to_all(pieces, axis, 0, 0, tiled=True)  26.1 us
    ppermute x3, waiting for transfers between devices, per_device(): lax.ppermute(piece, 'tp', [(t, (t + step) % n_tp) for t in range(n_tp)])  19 us
    ppermute x3, starting transfers between devices, per_device(): lax.ppermute(piece, 'tp', [(t, (t + step) % n_tp) for t in range(n_tp)])  8.94 us
    pallas_call x1, Pallas kernels, per_device(): pl.pallas_call(decode_kernel, out_shape=(jax.ShapeDtypeStruct((peers, row...  3.85 us
    pallas_call x1, Pallas kernels, per_device(): pl.pallas_call(send_kernel, out_shape=jax.ShapeDtypeStruct((n_ctx, STATE_...  3.01 us
  transfers between devices with their start and end apart: 7, of which 6 were waited for; matrix products, arithmetic and copies ran while one was open for 5% of the time, Pallas kernels for 0%

profile of v11, /device:TPU:1, one launch (start us, length us, event | category | flops | bytes accessed | tf_op | source)
XLA Modules:
  0.0 110.4 jit_solution(11118259244698383705)
XLA Ops:
  0.7 3.0 %send.1 = bf16[16,304,128]{2,1,0:T(8,128)(2,1)} custom-call(s32[4,16]{1,0:T(4,128)} %tokens_hbm.1, s32[16]{0:T(128)} %prompt_hbm.3, f32[2,32]{1,0:T(2,128)} %bitcast.32, bf16[64,6285]{1,0:T(8,128)(2,1)} %bitcast.23, bf16[2,16,128,128]{3,2,1,0:T(8,128)(2,1)} %bitcast.21), custom_call_target="tpu_custom_call" | custom-call | tf_op jit(solution)/shard_map/send/pallas_call | solution.py:405
  3.8 13.6 %all-to-all-start = ((bf16[16,304,128]{2,1,0:T(8,128)(2,1)}), bf16[16,304,128]{2,1,0:T(8,128)(2,1)S(1)}, u32[]{:S(2)}, u32[]{:S(2)}) async-start(bf16[16,304,128]{2,1,0:T(8,128)(2,1)} %send.1), calls=%async_computation | async-start | bytes 2490368 | tf_op jit(solution)/shard_map/all_to_all | solution.py:28
  17.6 0.1 reshape.85
  17.8 0.1 constant_dynamic-slice_fusion
  17.9 2.9 %collective-permute-start.2 = (bf16[1,6,1024]{2,0,1:T(2,128)(2,1)S(1)}, bf16[1,6,1024]{2,0,1:T(2,128)(2,1)S(1)}, u32[]{:S(2)}, u32[]{:S(2)}) collective-permute-start(bf16[1,6,1024]{2,0,1:T(2,128)(2,1)S(1)} %get-tuple-element.14), channel_id=1, source_target_pairs={{0,3},{1,0},{2,1},{3,2},{4,7},{5,4},{6,5},{7,6},{8,11},{9,8},{10,9... | collective-permute-start | bytes 36872 | tf_op jit(solution)/shard_map/ppermute | solution.py:440
  20.8 3.1 %collective-permute-start.1 = (bf16[1,6,1024]{2,0,1:T(2,128)(2,1)S(1)}, bf16[1,6,1024]{2,0,1:T(2,128)(2,1)S(1)}, u32[]{:S(2)}, u32[]{:S(2)}) collective-permute-start(bf16[1,6,1024]{2,0,1:T(2,128)(2,1)S(1)} %get-tuple-element.15), channel_id=1, source_target_pairs={{0,2},{1,3},{2,0},{3,1},{4,6},{5,7},{6,4},{7,5},{8,10},{9,11},{10,... | collective-permute-start | bytes 36872 | tf_op jit(solution)/shard_map/ppermute | solution.py:440
  23.9 3.0 %collective-permute-start = (bf16[1,6,1024]{2,0,1:T(2,128)(2,1)S(1)}, bf16[1,6,1024]{2,0,1:T(2,128)(2,1)S(1)}, u32[]{:S(2)}, u32[]{:S(2)}) collective-permute-start(bf16[1,6,1024]{2,0,1:T(2,128)(2,1)S(1)} %get-tuple-element.16), channel_id=1, source_target_pairs={{0,1},{1,2},{2,3},{3,0},{4,5},{5,6},{6,7},{7,4},{8,9},{9,10},{10,1... | collective-permute-start | bytes 36872 | tf_op jit(solution)/shard_map/ppermute | solution.py:440
  27.3 0.1 reduce_or.9
  27.5 9.3 %collective-permute-done = bf16[1,6,1024]{2,0,1:T(2,128)(2,1)S(1)} collective-permute-done((bf16[1,6,1024]{2,0,1:T(2,128)(2,1)S(1)}, bf16[1,6,1024]{2,0,1:T(2,128)(2,1)S(1)}, u32[]{:S(2)}, u32[]{:S(2)}) %collective-permute-start) | collective-permute-done | bytes 12320 | tf_op jit(solution)/shard_map/ppermute | solution.py:440
  36.8 8.1 %collective-permute-done.1 = bf16[1,6,1024]{2,0,1:T(2,128)(2,1)S(1)} collective-permute-done((bf16[1,6,1024]{2,0,1:T(2,128)(2,1)S(1)}, bf16[1,6,1024]{2,0,1:T(2,128)(2,1)S(1)}, u32[]{:S(2)}, u32[]{:S(2)}) %collective-permute-start.1) | collective-permute-done | bytes 12320 | tf_op jit(solution)/shard_map/ppermute | solution.py:440
  44.9 1.7 %collective-permute-done.2 = bf16[1,6,1024]{2,0,1:T(2,128)(2,1)S(1)} collective-permute-done((bf16[1,6,1024]{2,0,1:T(2,128)(2,1)S(1)}, bf16[1,6,1024]{2,0,1:T(2,128)(2,1)S(1)}, u32[]{:S(2)}, u32[]{:S(2)}) %collective-permute-start.2) | collective-permute-done | bytes 12320 | tf_op jit(solution)/shard_map/ppermute | solution.py:440
  46.7 1.8 %combine.1 = bf16[8,160,128]{2,1,0:T(8,128)(2,1)} custom-call(s32[8]{0:T(128)S(1)} %convert_element_type.12.chosen_ref, bf16[16,304,128]{2,1,0:T(8,128)(2,1)S(1)} %all-to-all-done.got_ref, bf16[2,16,128]{2,1,0:T(8,128)(2,1)S(1)} %fusion.6.tails_ref, f32[8,128]{1,0:T(8,128)S(1)} %reshape.83.gain_ref, bf16[128,1024]{1,0:T(8,128)(2,1)S(1)} %fusion.3.weight_ref), custom_call_target="tpu_custom_call" | custom-call | tf_op jit(solution)/shard_map/combine/pallas_call | solution.py:472
  48.5 6.8 %all-to-all-start.1 = ((bf16[8,160,128]{2,1,0:T(8,128)(2,1)}), bf16[8,160,128]{2,1,0:T(8,128)(2,1)S(1)}, u32[]{:S(2)}, u32[]{:S(2)}) async-start(bf16[8,160,128]{2,1,0:T(8,128)(2,1)} %combine.1), calls=%async_computation.1 | async-start | bytes 655360 | tf_op jit(solution)/shard_map/all_to_all | solution.py:28
  56.1 0.6 pad.14.small_hbm
  56.8 8.6 %all-to-all-done.1.arrived_ref.arrived_hbm = bf16[8,160,128]{2,1,0:T(8,128)(2,1)S(1)} async-done(((bf16[8,160,128]{2,1,0:T(8,128)(2,1)}), bf16[8,160,128]{2,1,0:T(8,128)(2,1)S(1)}, u32[]{:S(2)}, u32[]{:S(2)}) %all-to-all-start.1) | async-done | bytes 327712 | tf_op jit(solution)/shard_map/all_to_all | solution.py:28
  65.4 0.8 spread.1
  66.2 14.1 %all-to-all-start.2 = ((bf16[64,8,128]{2,1,0:T(8,128)(2,1)}), bf16[64,8,128]{2,1,0:T(8,128)(2,1)}, u32[]{:S(2)}, u32[]{:S(2)}) async-start(bf16[64,8,128]{2,1,0:T(8,128)(2,1)} %spread.1), calls=%async_computation.2 | async-start | bytes 262144 | tf_op jit(solution)/shard_map/all_to_all | solution.py:28
  80.2 2.1 %pad_maximum_fusion.weights_ref = bf16[384,4096]{1,0:T(8,128)(2,1)S(1)} fusion(bf16[128,4096]{1,0:T(8,128)(2,1)} %bitcast.22, bf16[256,4096]{1,0:T(8,128)(2,1)} %bitcast.20), kind=kLoop, calls=%fused_computation | loop fusion | flops 6291456 | bytes 6291456 | tf_op jit(solution)/shard_map/concatenate | solution.py:501
  82.4 8.1 %all-to-all-done.2.everyone_ref = bf16[64,8,128]{2,1,0:T(8,128)(2,1)} async-done(((bf16[64,8,128]{2,1,0:T(8,128)(2,1)}), bf16[64,8,128]{2,1,0:T(8,128)(2,1)}, u32[]{:S(2)}, u32[]{:S(2)}) %all-to-all-start.2) | async-done | bytes 131104 | tf_op jit(solution)/shard_map/all_to_all | solution.py:28
  90.5 3.8 %decode.1 = (bf16[64,8,128]{2,1,0:T(8,128)(2,1)}, bf16[2,128,128]{2,1,0:T(8,128)(2,1)S(1)}, f32[24,128]{1,0:T(8,128)S(1)}) custom-call(bf16[64,8,128]{2,1,0:T(8,128)(2,1)} %all-to-all-done.2.everyone_ref, bf16[384,4096]{1,0:T(8,128)(2,1)S(1)} %pad_maximum_fusion.weights_ref, bf16[8,160,128]{2,1,0:T(8,128)(2,1)} %copy-done, s32[16]{0:T(128)} %prompt_hbm.3, ...), custom_call_target="tpu_custom_call" | custom-call | tf_op jit(solution)/shard_map/decode/pallas_call | solution.py:505
  94.4 4.9 %all-to-all-start.3 = ((bf16[64,8,128]{2,1,0:T(8,128)(2,1)}), bf16[64,8,128]{2,1,0:T(8,128)(2,1)S(1)}, u32[]{:S(2)}, u32[]{:S(2)}) async-start(bf16[64,8,128]{2,1,0:T(8,128)(2,1)} %get-tuple-element.11), calls=%async_computation.3 | async-start | bytes 262144 | tf_op jit(solution)/shard_map/all_to_all | solution.py:28
  99.3 1.1 convolution_add_fusion
  100.3 9.3 %all-to-all-done.3.incoming_ref = bf16[64,8,128]{2,1,0:T(8,128)(2,1)S(1)} async-done(((bf16[64,8,128]{2,1,0:T(8,128)(2,1)}), bf16[64,8,128]{2,1,0:T(8,128)(2,1)S(1)}, u32[]{:S(2)}, u32[]{:S(2)}) %all-to-all-start.3) | async-done | bytes 131104 | tf_op jit(solution)/shard_map/all_to_all | solution.py:28
  109.6 0.8 finish.1
  (62 shorter events, 1.5 us)
Async XLA Ops:
  0.6 16.8 %copy-start.2 = (bf16[4096,6]{0,1:T(8,128)(2,1)S(1)}, bf16[4096,6]{0,1:T(8,128)(2,1)}, u32[]{:S(2)}) copy-start(bf16[4096,6]{0,1:T(8,128)(2,1)} %param.24) | copy-start | bytes 147460
  0.6 26.2 %copy-start.6 = (bf16[2,3,2,64]{3,2,1,0:T(2,128)(2,1)S(1)}, bf16[2,3,2,64]{3,2,1,0:T(2,128)(2,1)}, u32[]{:S(2)}) copy-start(bf16[2,3,2,64]{3,2,1,0:T(2,128)(2,1)} %param.36) | copy-start | bytes 4612
  0.7 26.3 %copy-start.5 = (bf16[2,3,256]{2,0,1:T(2,128)(2,1)S(1)}, bf16[2,3,256]{2,0,1:T(2,128)(2,1)}, u32[]{:S(2)}) copy-start(bf16[2,3,256]{2,0,1:T(2,128)(2,1)} %param.37) | copy-start | bytes 9220
  0.7 26.3 %copy-start.1 = (f32[4096]{0:T(1024)S(1)}, f32[4096]{0:T(1024)}, u32[]{:S(2)}) copy-start(f32[4096]{0:T(1024)} %param.22) | copy-start | bytes 49156
  0.7 26.4 %copy-start.7 = (s32[16]{0:T(128)S(1)}, s32[16]{0:T(128)}, u32[]{:S(2)}) copy-start(s32[16]{0:T(128)} %prompt_hbm.3) | copy-start | bytes 196
  3.7 51.7 %copy-start.9 = (f32[2,64]{1,0:T(2,128)S(1)}, f32[2,64]{1,0:T(2,128)}, u32[]{:S(2)}) copy-start(f32[2,64]{1,0:T(2,128)} %param.26) | copy-start | bytes 1540
  3.7 51.7 %copy-start.10 = (f32[2,64]{1,0:T(2,128)S(1)}, f32[2,64]{1,0:T(2,128)}, u32[]{:S(2)}) copy-start(f32[2,64]{1,0:T(2,128)} %param.32) | copy-start | bytes 1540
  3.7 51.8 %copy-start.11 = (f32[2]{0:T(128)S(1)}, f32[2]{0:T(128)}, u32[]{:S(2)}) copy-start(f32[2]{0:T(128)} %param.29) | copy-start | bytes 28
  3.7 51.9 %copy-start.12 = (f32[2]{0:T(128)S(1)}, f32[2]{0:T(128)}, u32[]{:S(2)}) copy-start(f32[2]{0:T(128)} %param.30) | copy-start | bytes 28
  3.8 52.1 %copy-start.13 = (f32[2]{0:T(128)S(1)}, f32[2]{0:T(128)}, u32[]{:S(2)}) copy-start(f32[2]{0:T(128)} %param.31) | copy-start | bytes 28
  3.8 52.2 %copy-start.3 = (f32[4,2,64]{2,1,0:T(2,128)S(1)}, f32[4,2,64]{2,1,0:T(2,128)}, u32[]{:S(2)}) copy-start(f32[4,2,64]{2,1,0:T(2,128)} %param.25) | copy-start | bytes 6148
  3.8 52.3 %copy-start.4 = (f32[4,256]{1,0:T(4,128)S(1)}, f32[4,256]{1,0:T(4,128)}, u32[]{:S(2)}) copy-start(f32[4,256]{1,0:T(4,128)} %param.27) | copy-start | bytes 12292
  3.8 52.3 %copy-start.8 = (f32[256]{0:T(256)S(1)}, f32[256]{0:T(256)}, u32[]{:S(2)}) copy-start(f32[256]{0:T(256)} %param.28) | copy-start | bytes 3076
  3.8 42.9 %all-to-all-start = ((bf16[16,304,128]{2,1,0:T(8,128)(2,1)}), bf16[16,304,128]{2,1,0:T(8,128)(2,1)S(1)}, u32[]{:S(2)}, u32[]{:S(2)}) async-start(bf16[16,304,128]{2,1,0:T(8,128)(2,1)} %send.1), calls=%async_computation | async-start | bytes 2490368 | tf_op jit(solution)/shard_map/all_to_all | solution.py:28
  17.9 28.7 %collective-permute-start.2 = (bf16[1,6,1024]{2,0,1:T(2,128)(2,1)S(1)}, bf16[1,6,1024]{2,0,1:T(2,128)(2,1)S(1)}, u32[]{:S(2)}, u32[]{:S(2)}) collective-permute-start(bf16[1,6,1024]{2,0,1:T(2,128)(2,1)S(1)} %get-tuple-element.14), channel_id=1, source_target_pairs={{0,3},{1,0},{2,1},{3,2},{4,7},{5,4},{6,5},{7,6},{8,11},{9,8},{10,9... | collective-permute-start | bytes 36872 | tf_op jit(solution)/shard_map/ppermute | solution.py:440
  20.8 24.2 %collective-permute-start.1 = (bf16[1,6,1024]{2,0,1:T(2,128)(2,1)S(1)}, bf16[1,6,1024]{2,0,1:T(2,128)(2,1)S(1)}, u32[]{:S(2)}, u32[]{:S(2)}) collective-permute-start(bf16[1,6,1024]{2,0,1:T(2,128)(2,1)S(1)} %get-tuple-element.15), channel_id=1, source_target_pairs={{0,2},{1,3},{2,0},{3,1},{4,6},{5,7},{6,4},{7,5},{8,10},{9,11},{10,... | collective-permute-start | bytes 36872 | tf_op jit(solution)/shard_map/ppermute | solution.py:440
  23.9 12.9 %collective-permute-start = (bf16[1,6,1024]{2,0,1:T(2,128)(2,1)S(1)}, bf16[1,6,1024]{2,0,1:T(2,128)(2,1)S(1)}, u32[]{:S(2)}, u32[]{:S(2)}) collective-permute-start(bf16[1,6,1024]{2,0,1:T(2,128)(2,1)S(1)} %get-tuple-element.16), channel_id=1, source_target_pairs={{0,1},{1,2},{2,3},{3,0},{4,5},{5,6},{6,7},{7,4},{8,9},{9,10},{10,1... | collective-permute-start | bytes 36872 | tf_op jit(solution)/shard_map/ppermute | solution.py:440
  48.5 16.9 %all-to-all-start.1 = ((bf16[8,160,128]{2,1,0:T(8,128)(2,1)}), bf16[8,160,128]{2,1,0:T(8,128)(2,1)S(1)}, u32[]{:S(2)}, u32[]{:S(2)}) async-start(bf16[8,160,128]{2,1,0:T(8,128)(2,1)} %combine.1), calls=%async_computation.1 | async-start | bytes 655360 | tf_op jit(solution)/shard_map/all_to_all | solution.py:28
  65.4 17.0 %copy-start = (bf16[8,160,128]{2,1,0:T(8,128)(2,1)}, bf16[8,160,128]{2,1,0:T(8,128)(2,1)S(1)}, u32[]{:S(2)}) copy-start(bf16[8,160,128]{2,1,0:T(8,128)(2,1)S(1)} %all-to-all-done.1.arrived_ref.arrived_hbm) | copy-start | bytes 983044
  66.2 24.4 %all-to-all-start.2 = ((bf16[64,8,128]{2,1,0:T(8,128)(2,1)}), bf16[64,8,128]{2,1,0:T(8,128)(2,1)}, u32[]{:S(2)}, u32[]{:S(2)}) async-start(bf16[64,8,128]{2,1,0:T(8,128)(2,1)} %spread.1), calls=%async_computation.2 | async-start | bytes 262144 | tf_op jit(solution)/shard_map/all_to_all | solution.py:28
  94.4 15.3 %all-to-all-start.3 = ((bf16[64,8,128]{2,1,0:T(8,128)(2,1)}), bf16[64,8,128]{2,1,0:T(8,128)(2,1)S(1)}, u32[]{:S(2)}, u32[]{:S(2)}) async-start(bf16[64,8,128]{2,1,0:T(8,128)(2,1)} %get-tuple-element.11), calls=%async_computation.3 | async-start | bytes 262144 | tf_op jit(solution)/shard_map/all_to_all | solution.py:28
